TPU v7x, 32 devices: a whole 2x2x4 slice. The times are simulated.
32 devices in a mesh: walker: 4 (over x, core), prow: 2 (over y), pcol: 4 (over z).
Axes of the slice: x: 2, y: 2, z: 4, core: 2. Of those that a mesh axis runs over, the one named last changes fastest.
Arguments:
- o_rows: bfloat16 [8192, 2048], P('walker', ('prow', 'pcol')), may hold values from -21 to 21
- o_cols: bfloat16 [8192, 4096], P('walker', ('pcol', 'prow')), may hold values from -48 to 48
- grad_energy: bfloat16 [8192, 4096], P('walker', ('pcol', 'prow')), may hold values from -8 to 8
- energy: float32 [8192], P('walker'), may hold values from -5 to 1
Outputs:
- hamil: float32 [2048, 4096], P(('prow', 'walker'), 'pcol')
- correlation: float32 [2048, 4096], P(('prow', 'walker'), 'pcol')
All inputs are finite; a program needn't handle non-finite values.
Results may differ from a plain program's by a relative error of at most 0.008.
Values may be sent and summed in bfloat16 or wider, within the bound.
No kernel may reach another device: no remote copies, remote signals or barrier semaphores. Data moves between devices by JAX's collectives and lax.ppermute only.
A program may use at most 128 MiB of HBM per device.

v0:
```python
import jax
import jax.numpy as jnp
from jax import lax
from jax.sharding import PartitionSpec as P


def column_sums(values):
    return jnp.sum(values.astype(jnp.float32), axis=0)


def tile_product(row_tile, right_tile):
    return lax.dot_general(
        row_tile, right_tile, (((0,), (0,)), ((), ())), preferred_element_type=jnp.float32
    )


def per_device(o_rows, o_cols, grad_energy, energy):
    count = energy.shape[0] * lax.axis_size("walker")
    row_total, col_total = lax.psum((column_sums(o_rows), column_sums(o_cols)), "walker")
    row_shard = (o_rows - row_total / count).astype(jnp.bfloat16)
    col_shard = (o_cols - col_total / count).astype(jnp.bfloat16)
    row_tile = lax.all_gather(row_shard, "pcol", axis=1, tiled=True)
    col_tile, grad_tile = (
        lax.all_gather(col_shard, "prow", axis=1, tiled=True),
        lax.all_gather(grad_energy, "prow", axis=1, tiled=True),
    )
    weighted = (energy[:, None] * col_tile + grad_tile).astype(jnp.bfloat16)
    paired = jnp.concatenate((col_tile, weighted), axis=1)
    summed = lax.psum_scatter(
        tile_product(row_tile, paired), "walker", scatter_dimension=0, tiled=True
    )
    width = col_tile.shape[1]
    correlation = summed[:, :width]
    hamil = summed[:, width:]
    return (hamil / count, correlation / count)


def solution(mesh):
    in_specs = (
        P("walker", ("prow", "pcol")),
        P("walker", ("pcol", "prow")),
        P("walker", ("pcol", "prow")),
        P("walker"),
    )
    out_specs = (P(("prow", "walker"), "pcol"), P(("prow", "walker"), "pcol"))
    return jax.shard_map(
        per_device, mesh=mesh, in_specs=in_specs, out_specs=out_specs, check_vma=False
    )
```

profile of v0, /device:TPU:0, one launch (start us, length us, event | category | flops | bytes accessed | tf_op | source)
XLA Modules:
  0.0 305.0 jit_solution(11272045929542060751)
XLA Ops:
  7.2 0.0 copy-start
  7.2 0.0 all-gather.8.cloned.1.call-start
  7.2 0.7 all-gather.8.cloned.1.call-update
  7.9 0.0 all-gather.6.cloned.1.call-start
  8.0 1.5 convert_reduce_fusion.1
  9.5 0.0 copy-done
  9.5 0.0 copy-start.1
  9.5 0.3 convert_reduce_fusion
  9.8 8.3 %all-reduce = (f32[256]{0:T(256)S(1)}, f32[512]{0:T(512)S(1)}) all-reduce(f32[256]{0:T(256)S(1)} %convert_reduce_fusion.1, f32[512]{0:T(512)S(1)} %convert_reduce_fusion), channel_id=1, replica_groups=mesh['walker'=4,'prow'=2,'pcol'=4] {'walker'}, use_global_device_ids=true, to_apply=%region_1.0 | all-reduce | flops 768 | bytes 6144 | tf_op jit(solution)/shard_map/psum | solution.py:19
  18.2 0.0 copy-start.2
  18.2 1.8 fusion.4
  19.9 0.0 all-gather.6.cloned.1.call-update
  20.0 0.0 all-gather.4.cloned.1.call-start
  20.0 0.0 copy-done.1
  20.0 1.2 fusion.5
  21.2 0.0 all-gather.4.cloned.1.call-update
  21.3 0.0 reduce-scatter.2.cloned.1.call-start
  21.3 47.7 %all-gather.8.cloned.1.call-done = bf16[2048,1024]{1,0:T(8,128)(2,1)} async-done(((bf16[2048,512]{1,0:T(8,128)(2,1)}), bf16[2048,1024]{1,0:T(8,128)(2,1)}) %all-gather.8.cloned.1.call-update) | async-done | bytes 4194320 | tf_op jit(solution)/shard_map/all_gather | solution.py:25
  69.0 58.3 %all-gather.6.cloned.1.call-done = bf16[2048,1024]{1,0:T(8,128)(2,1)} async-done(((bf16[2048,512]{1,0:T(8,128)(2,1)}), bf16[2048,1024]{1,0:T(8,128)(2,1)}) %all-gather.6.cloned.1.call-update) | async-done | bytes 4194320 | tf_op jit(solution)/shard_map/all_gather | solution.py:24
  127.4 0.0 copy-done.2
  127.4 5.4 %add_convert_fusion = bf16[2048,1024]{1,0:T(8,128)(2,1)} fusion(bf16[2048,1024]{1,0:T(8,128)(2,1)} %all-gather.8.cloned.1.call-done, bf16[2048,1024]{1,0:T(8,128)(2,1)} %all-gather.6.cloned.1.call-done, f32[2048]{0:T(1024)S(1)} %copy-done.2), kind=kLoop, calls=%fused_computation.4 | loop fusion | flops 10485760 | bytes 12591104 | tf_op jit(solution)/shard_map/convert_element_type | solution.py:27
  132.8 77.3 %all-gather.4.cloned.1.call-done = bf16[2048,1024]{1,0:T(8,128)(2,1)} async-done(((bf16[2048,256]{1,0:T(8,128)(2,1)}), bf16[2048,1024]{1,0:T(8,128)(2,1)}) %all-gather.4.cloned.1.call-update) | async-done | bytes 4194320 | tf_op jit(solution)/shard_map/all_gather | solution.py:22
  210.1 15.2 %fusion = f32[1024,2048]{1,0:T(8,128)} fusion(bf16[2048,1024]{1,0:T(8,128)(2,1)} %all-gather.4.cloned.1.call-done, bf16[2048,1024]{1,0:T(8,128)(2,1)} %add_convert_fusion, bf16[2048,1024]{1,0:T(8,128)(2,1)} %all-gather.6.cloned.1.call-done), kind=kOutput, calls=%fused_computation | convolution fusion | flops 8606711808 | bytes 20971520 | tf_op jit(solution)/shard_map/dot_general | solution.py:12
  225.3 0.0 reduce-scatter.2.cloned.1.call-update
  225.3 70.1 %reduce-scatter.2.cloned.1.call-done = f32[256,2048]{1,0:T(8,128)} async-done(((f32[1024,2048]{1,0:T(8,128)}), f32[256,2048]{1,0:T(8,128)}) %reduce-scatter.2.cloned.1.call-update) | async-done | bytes 2097168 | tf_op jit(solution)/shard_map/reduce_scatter | solution.py:29
  295.3 3.2 %slice_multiply_fusion = (f32[256,1024]{1,0:T(8,128)}, f32[256,1024]{1,0:T(8,128)}) fusion(f32[256,2048]{1,0:T(8,128)} %reduce-scatter.2.cloned.1.call-done), kind=kLoop, calls=%fused_computation.11 | loop fusion | flops 524288 | bytes 4194304 | tf_op jit(solution)/shard_map/div | solution.py:35
  (2 shorter events, 0.0 us)
Async XLA Ops:
  7.2 2.3 copy-start
  7.2 61.9 %all-gather.8.cloned.1.call-start = ((), (), s32[]{:S(2)}) async-start(), calls=%async_computation.3 | async-start | bytes 6291456 | tf_op jit(solution)/shard_map/all_gather | solution.py:25
  7.9 119.5 %all-gather.6.cloned.1.call-start = ((), (), s32[]{:S(2)}) async-start(), calls=%async_computation.2 | async-start | bytes 6291456 | tf_op jit(solution)/shard_map/all_gather | solution.py:24
  9.5 10.6 %copy-start.1 = (bf16[2048,256]{1,0:T(8,128)(2,1)S(1)}, bf16[2048,256]{1,0:T(8,128)(2,1)}, u32[]{:S(2)}) copy-start(bf16[2048,256]{1,0:T(8,128)(2,1)} %param.4) | copy-start | bytes 3145732
  18.2 109.2 %copy-start.2 = (f32[2048]{0:T(1024)S(1)}, f32[2048]{0:T(1024)}, u32[]{:S(2)}) copy-start(f32[2048]{0:T(1024)} %param.7) | copy-start | bytes 24580
  20.0 190.1 %all-gather.4.cloned.1.call-start = ((), (), s32[]{:S(2)}) async-start(), calls=%async_computation.1 | async-start | bytes 5242880 | tf_op jit(solution)/shard_map/all_gather | solution.py:22
  21.3 274.1 %reduce-scatter.2.cloned.1.call-start = ((), (), s32[]{:S(2)}) async-start(), calls=%async_computation.4 | async-start | bytes 10485760 | tf_op jit(solution)/shard_map/reduce_scatter | solution.py:29
Sparse Core Ops, SparseCore 0:
  9.6 59.4 all-gather.7
  70.6 56.7 all-gather.5
  129.5 80.5 all-gather.3
  225.4 69.8 reduce-scatter.1
where the time goes:
time: 305 us
  waiting for transfers between devices  254 us (83%)
  matrix products  15.2 us (5%)
  between operations  13.8 us (5%)
  other arithmetic  13.4 us (4%)
  blocking collectives  8.33 us (3%)
    all_gather x1, waiting for transfers between devices, per_device(): row_tile = lax.all_gather(row_shard, 'pcol', axis=1, tiled=True)  77.3 us
    reduce_scatter x1, waiting for transfers between devices, per_device(): lax.psum_scatter(tile_product(row_tile, paired), 'walker', scatter_dimens...  70.1 us
    all_gather x1, waiting for transfers between devices, per_device(): lax.all_gather(col_shard, 'prow', axis=1, tiled=True)  58.3 us
    all_gather x1, waiting for transfers between devices, per_device(): lax.all_gather(grad_energy, 'prow', axis=1, tiled=True)  47.7 us
    dot_general x1, matrix products, tile_product(): lax.dot_general(row_tile, right_tile, (((0,), (0,)), ((), ())), preferred...  15.2 us
    psum x1, blocking collectives, per_device(): lax.psum((column_sums(o_rows), column_sums(o_cols)), 'walker')  8.33 us
  transfers between devices with their start and end apart: 4, of which 4 were waited for; matrix products, arithmetic and copies ran while one was open for 3% of the time, Pallas kernels for 0%

commit v1 on v0

v1 whole, which is shorter than its diff:
```python
import functools

import jax
import jax.numpy as jnp
from jax import lax
from jax.experimental import pallas as pl
from jax.experimental.pallas import tpu as pltpu
from jax.sharding import PartitionSpec as P

BF = jnp.bfloat16
F32 = jnp.float32
VMEM = pl.BlockSpec(memory_space=pltpu.VMEM)
SMEM = pl.BlockSpec(memory_space=pltpu.SMEM)
MID, LOW, CORE, STRAIGHT, TABLE = 0, 1, 2, 3, 4


def call(kernel, outs, *args, scratch=(), limit=40):
    return pl.pallas_call(
        kernel,
        out_shape=[jax.ShapeDtypeStruct(s, d) for s, d in outs],
        in_specs=[SMEM if a.dtype == jnp.int32 else VMEM for a in args],
        out_specs=[VMEM] * len(outs),
        scratch_shapes=list(scratch),
        compiler_params=pltpu.CompilerParams(vmem_limit_bytes=limit * 2**20),
        cost_estimate=pl.CostEstimate(flops=0, bytes_accessed=0, transcendentals=0),
    )(*args)


def after(value, *others):
    return lax.optimization_barrier((value,) + others)[0]


def centred(values, mean):
    return (values.astype(F32) - mean).astype(BF)


def weigh(energy, cols, grads):
    return (energy * cols.astype(F32) + grads.astype(F32)).astype(BF)


def dot(rows, right):
    return lax.dot_general(rows, right, (((0,), (0,)), ((), ())), preferred_element_type=F32)


def sums_kernel(rows, cols, out):
    width = rows.shape[1]
    out[:, :width] = jnp.sum(rows[...].astype(F32), axis=0, keepdims=True)
    out[:, width:] = jnp.sum(cols[...].astype(F32), axis=0, keepdims=True)


def own_kernel(count, cuts, cols, grads, energy, sums, out, *pieces):
    width = cols.shape[1]
    d = centred(cols[...], sums[:, -width:] / count)
    out[:, :width] = d
    out[:, width:] = weigh(energy[...], d, grads[...])
    for a, b, piece in zip(cuts[:-1], cuts[1:], pieces):
        piece[...] = grads[:, a:b]


def store_pieces(result, blocks, piece, core, send, keep, at, cols):
    for i in range(blocks[1]):
        walker = blocks[0] * blocks[1] + i
        value = result[i * piece : (i + 1) * piece].astype(BF)
        slot = at[walker]

        @pl.when(core == walker % 2)
        def _():
            keep[slot, :, cols] = value

        @pl.when(core != walker % 2)
        def _():
            send[slot, :, cols] = value


def group_products(info, tile, rights, blocks, per, slots, send, keep):
    piece = tile.shape[2] // per
    for j, b in enumerate(blocks):
        start = 0
        for right in rights:
            n = right.shape[1]
            store_pieces(
                dot(tile[j], right[...]),
                (b, per),
                piece,
                info[CORE],
                send,
                keep,
                slots,
                slice(start, start + n),
            )
            start += n


def early_kernel(
    count, per, slots,
    info, own_rows, near, mid1, mid2, m0, m1, m2, m3, ow, far_raw, far_sums,
    send, keep, tile, far,
):
    rw, cw = own_rows.shape[1], far_raw.shape[1]
    mid, low = info[MID] == 1, info[LOW] == 1
    far[...] = centred(far_raw[...], far_sums[:, rw:] / count)
    there = info[LOW]

    @pl.when(mid)
    def _():
        tile[there] = centred(mid1[...], m3[:, :rw] / count)
        tile[1 - there] = centred(own_rows[...], m0[:, :rw] / count)

    @pl.when(jnp.logical_not(mid))
    def _():
        tile[there] = centred(mid2[...], m2[:, :rw] / count)
        tile[1 - there] = centred(near[...], m1[:, :rw] / count)

    half = ow.shape[1] // 2
    group_products(
        info, tile, (ow.at[:, :half], ow.at[:, half:], far), (1, 2), per, slots, send, keep
    )


def late_kernel(
    count, per, slots,
    info, own_rows, near, last1, last2, m0, m1, m2, m3, ow, far,
    send, keep, tile,
):
    rw = own_rows.shape[1]
    mid = info[MID] == 1
    there = info[LOW]

    @pl.when(mid)
    def _():
        tile[there] = centred(last1[...], m2[:, :rw] / count)
        tile[1 - there] = centred(near[...], m1[:, :rw] / count)

    @pl.when(jnp.logical_not(mid))
    def _():
        tile[there] = centred(last2[...], m3[:, :rw] / count)
        tile[1 - there] = centred(own_rows[...], m0[:, :rw] / count)

    half = ow.shape[1] // 2
    group_products(
        info, tile, (ow.at[:, :half], ow.at[:, half:], far), (0, 3), per, slots, send, keep
    )


def chunk_kernel(start, per, slots, info, early, late, far, energy, grads, send, keep, right):
    n = grads.shape[1]
    right[...] = weigh(energy[...], far[:, start : start + n], grads[...])
    group_products(info, early, (right,), (1, 2), per, slots, send, keep)
    group_products(info, late, (right,), (0, 3), per, slots, send, keep)


def pair_kernel(first, pieces, info, keep, got, *outs):
    for k, out in enumerate(outs, 1):
        i = jnp.clip(info[TABLE + k] - first, 0, pieces - 1)
        out[...] = (keep[i].astype(F32) + got[i].astype(F32)).astype(BF)


def final_kernel(count, shapes, info, *refs):
    ham, corr = refs[-2:]
    cw = ham.shape[1] // 2
    straight = info[STRAIGHT] == 1
    pos = info[TABLE]

    def put(out, near, start, value):
        value = value / count

        @pl.when(straight == near)
        def _():
            out[:, start : start + value.shape[1]] = value

        @pl.when(straight != near)
        def _():
            out[:, cw + start : cw + start + value.shape[1]] = value

    at = 0
    for shifts, first, pieces, parts in shapes:
        keep, got = refs[at], refs[at + 1]
        others = refs[at + 2 : at + 2 + shifts]
        at += 2 + shifts

        @pl.when((pos >= first) & (pos < first + pieces))
        def _():
            i = pos - first
            for name, near, a, b, start in parts:
                value = keep[i, :, a:b].astype(F32) + got[i, :, a:b].astype(F32)
                for other in others:
                    value = value + other[:, a:b].astype(F32)
                put(ham if name == "ham" else corr, near, start, value)


def per_device(o_rows, o_cols, grad_energy, energy):
    samples, rw = o_rows.shape
    cw = o_cols.shape[1]
    walkers = lax.axis_size("walker")
    chips = walkers // 2
    per = walkers // 4
    piece = rw // per
    w, y, z = (lax.axis_index(a) for a in ("walker", "prow", "pcol"))
    count = samples * walkers
    flip = [(0, 1), (1, 0)]
    outer = [(0, 1), (1, 0), (2, 3), (3, 2)]
    inner = [(1, 2), (2, 1)]
    ends = [(1, 0), (2, 3)]
    other_core = [(v, v ^ 1) for v in range(walkers)]

    order = [b * per + i for b in (1, 2, 0, 3) for i in range(per)]
    place = {v: [u for u in order if u % 2 == v % 2].index(v) for v in order}
    late_slots = {v: place[v] - per for v in order}
    table = [[place[(v + 2 * k) % walkers] for k in range(chips)] for v in range(walkers)]
    info = jnp.concatenate(
        (
            jnp.stack(((z == 1) | (z == 2), z < 2, w % 2, y == 0)).astype(jnp.int32),
            jnp.asarray(table, jnp.int32)[w],
        )
    )

    def shift(k, first, pieces):
        return [
            (v, (v + 2 * k) % walkers)
            for v in range(walkers)
            if first <= table[v][k] < first + pieces
        ]

    far_raw = lax.ppermute(o_cols, "prow", flip)
    near = lax.ppermute(o_rows, "pcol", outer)
    mid1 = lax.ppermute(o_rows, "pcol", inner)

    (sums,) = call(sums_kernel, [((1, rw + cw), F32)], o_rows, o_cols)
    m0 = lax.psum(sums, "walker")
    m1 = lax.ppermute(m0, "pcol", outer)
    m2 = lax.ppermute(m0, "pcol", [(0, 2), (1, 3), (2, 0), (3, 1)])

    column = energy[:, None]
    cuts = [0, cw // 2, 3 * cw // 4, cw]
    widths = [b - a for a, b in zip(cuts[:-1], cuts[1:])]
    ow, *grads = call(
        functools.partial(own_kernel, count, cuts),
        [((samples, 2 * cw), BF)] + [((samples, n), BF) for n in widths],
        o_cols, grad_energy, column, m0,
    )

    near, mid1, m1, m2, ow, m0 = lax.optimization_barrier((near, mid1, m1, m2, ow, m0))
    m3 = lax.ppermute(m0, "pcol", [(0, 3), (1, 2), (2, 1), (3, 0)])
    far_sums = lax.ppermute(m0, "prow", flip)
    mid2 = lax.ppermute(mid1, "pcol", ends)
    last1 = lax.ppermute(near, "pcol", inner)
    far_grads = [lax.ppermute(after(grads[0], m3), "prow", flip)]

    mid2, last1, far_raw, far_sums, m3, grads[1] = lax.optimization_barrier(
        (mid2, last1, far_raw, far_sums, m3, grads[1])
    )
    last2 = lax.ppermute(last1, "pcol", ends)
    far_grads.append(lax.ppermute(grads[1], "prow", flip))

    n1 = 3 * cw
    group = [((per, piece, n1), BF), ((per, piece, n1), BF)]
    tile_shape = ((2, samples, rw), BF)
    e_send, e_keep, early, far = call(
        functools.partial(early_kernel, count, per, place),
        group + [tile_shape, ((samples, cw), BF)],
        info, o_rows, near, mid1, mid2, m0, m1, m2, m3, ow, far_raw, far_sums,
    )

    messages = []

    def reduce(send, keep, first, pieces, parts):
        got = lax.ppermute(send, "walker", other_core)
        sent = call(
            functools.partial(pair_kernel, first, pieces),
            [(keep.shape[1:], BF)] * (chips - 1),
            info, keep, got,
        )
        others = [
            lax.ppermute(s, "walker", shift(k, first, pieces)) for k, s in enumerate(sent, 1)
        ]
        messages.append((keep, got, others, first, pieces, parts))

    parts = [
        ("corr", True, 0, cw, 0),
        ("ham", True, cw, 2 * cw, 0),
        ("corr", False, 2 * cw, 3 * cw, 0),
    ]
    reduce(e_send, e_keep, 0, per, parts)

    last2, far_grads[0], grads[2] = lax.optimization_barrier((last2, far_grads[0], grads[2]))
    far_grads.append(lax.ppermute(grads[2], "prow", flip))
    l_send, l_keep, late = call(
        functools.partial(late_kernel, count, per, late_slots),
        group + [tile_shape],
        info, o_rows, near, last1, last2, m0, m1, m2, m3, ow, far,
    )
    reduce(l_send, l_keep, per, per, parts)

    for a, n, g in zip(cuts, widths, far_grads):
        send, keep = call(
            functools.partial(chunk_kernel, a, per, place),
            [((2 * per, piece, n), BF)] * 2,
            info, early, late, far, column, g,
            scratch=[pltpu.VMEM((samples, n), BF)],
        )
        reduce(send, keep, 0, 2 * per, [("ham", False, 0, n, a)])

    flat, shapes = [], []
    for keep, got, others, first, pieces, parts in messages:
        flat += [keep, got, *others]
        shapes.append((len(others), first, pieces, parts))
    return call(
        functools.partial(final_kernel, count, shapes),
        [((piece, 2 * cw), F32)] * 2,
        info, *flat,
    )


def solution(mesh):
    in_specs = (
        P("walker", ("prow", "pcol")),
        P("walker", ("pcol", "prow")),
        P("walker", ("pcol", "prow")),
        P("walker"),
    )
    out_specs = (P(("prow", "walker"), "pcol"), P(("prow", "walker"), "pcol"))

    def per(*args):
        return tuple(per_device(*args))

    return jax.shard_map(
        per, mesh=mesh, in_specs=in_specs, out_specs=out_specs, check_vma=False
    )
```

time: 305 us -> 142 us (0.47)
  waiting for transfers between devices: 254 us -> 55.5 us
  Pallas kernels: 0 us -> 33.5 us
  starting transfers between devices: 0.16 us -> 30.3 us
  matrix products: 15.2 us -> 0 us
  local copies, waits for them, and re-layouts: 0.01 us -> 15.1 us
  other arithmetic: 13.4 us -> 0 us
  between operations: 13.8 us -> 0.88 us
    all_gather x3 -> x0, waiting for transfers between devices: 183 us -> none  [the longest x1 77.3 us: per_device(): row_tile = lax.all_gather(row_shard, 'pcol', axis=1, tiled=True)]
    reduce_scatter x1 -> x0, waiting for transfers between devices: 70.1 us -> none  [per_device(): lax.psum_scatter(tile_product(row_tile, paired), 'walker', scatter_dimens...]
    ppermute x0 -> x23, waiting for transfers between devices: none -> 55.5 us  [the longest x1 15.7 us: per_device(): far_sums = lax.ppermute(m0, 'prow', flip)]
    pallas_call x0 -> x13, Pallas kernels: none -> 33.5 us  [call(): pl.pallas_call(kernel, out_shape=[jax.ShapeDtypeStruct(s, d) for s, d in...]
    ppermute x0 -> x23, starting transfers between devices: none -> 30.3 us  [the longest x5 7.17 us: reduce(): lax.ppermute(s, 'walker', shift(k, first, pieces))]
    dot_general x1 -> x0, matrix products: 15.2 us -> none  [tile_product(): lax.dot_general(row_tile, right_tile, (((0,), (0,)), ((), ())), preferred...]
    unnamed x6 -> x28, local copies, waits for them, and re-layouts: 0.01 us -> 14 us
    convert_element_type x3 -> x0, other arithmetic: 8.4 us -> none  [the longest x1 5.44 us: per_device(): weighted = (energy[:, None] * col_tile + grad_tile).astype(jnp.bfloat16)]
  transfers between devices with their start and end apart: 4 -> 23, of which waited for: 4 -> 11; matrix products, arithmetic and copies ran while one was open for 3% -> 1% of each run, Pallas kernels for 0% -> 22%
where the time goes in v1:
time: 142 us; the launch traced here: 141 us
  waiting for transfers between devices  55.5 us (39%)
  Pallas kernels  33.5 us (24%)
  starting transfers between devices  30.3 us (21%)
  local copies, waits for them, and re-layouts  15.1 us (11%)
  blocking collectives  6.14 us (4%)
    pallas_call x13, Pallas kernels, call(): pl.pallas_call(kernel, out_shape=[jax.ShapeDtypeStruct(s, d) for s, d in...  33.5 us
    ppermute x1, waiting for transfers between devices, per_device(): far_sums = lax.ppermute(m0, 'prow', flip)  15.7 us
    unnamed x28, local copies, waits for them, and re-layouts  14 us
    ppermute x1, waiting for transfers between devices, per_device(): last2 = lax.ppermute(last1, 'pcol', ends)  8.48 us
    ppermute x1, waiting for transfers between devices, per_device(): far_grads.append(lax.ppermute(grads[2], 'prow', flip))  7.89 us
    ppermute x1, waiting for transfers between devices, per_device(): far_grads.append(lax.ppermute(grads[1], 'prow', flip))  7.66 us
    ppermute x1, waiting for transfers between devices, per_device(): far_grads = [lax.ppermute(after(grads[0], m3), 'prow', flip)]  7.32 us
    ppermute x5, starting transfers between devices, reduce(): lax.ppermute(s, 'walker', shift(k, first, pieces))  7.17 us
  transfers between devices with their start and end apart: 23, of which 11 were waited for; matrix products, arithmetic and copies ran while one was open for 1% of the time, Pallas kernels for 22%

profile of v1, /device:TPU:0, one launch (start us, length us, event | category | flops | bytes accessed | tf_op | source)
XLA Modules:
  0.0 141.4 jit_solution(11863292022971879841)
XLA Ops:
  0.6 1.7 %collective-permute-start.1 = (bf16[2048,256]{1,0:T(8,128)(2,1)}, bf16[2048,256]{1,0:T(8,128)(2,1)}, u32[]{:S(2)}, u32[]{:S(2)}) collective-permute-start(bf16[2048,256]{1,0:T(8,128)(2,1)} %own_rows.3), channel_id=1, source_target_pairs={{1,2},{2,1},{5,6},{6,5},{9,10},{10,9},{13,14},{14,13},{17,18},{18,... | collective-permute-start | bytes 3145736 | tf_op jit(solution)/shard_map/ppermute | solution.py:226
  2.4 4.8 %collective-permute-start = (bf16[2048,256]{1,0:T(8,128)(2,1)}, bf16[2048,256]{1,0:T(8,128)(2,1)S(1)}, u32[]{:S(2)}, u32[]{:S(2)}) collective-permute-start(bf16[2048,256]{1,0:T(8,128)(2,1)} %own_rows.3), channel_id=1, source_target_pairs={{0,1},{1,0},{2,3},{3,2},{4,5},{5,4},{6,7},{7,6},{8,9},{9,8},{10,11... | collective-permute-start | bytes 3145736 | tf_op jit(solution)/shard_map/ppermute | solution.py:225
  7.2 1.5 %collective-permute-start.6 = (bf16[2048,512]{1,0:T(8,128)(2,1)}, bf16[2048,512]{1,0:T(8,128)(2,1)}, u32[]{:S(2)}, u32[]{:S(2)}) collective-permute-start(bf16[2048,512]{1,0:T(8,128)(2,1)} %cols.3), channel_id=1, source_target_pairs={{0,4},{4,0},{1,5},{5,1},{2,6},{6,2},{3,7},{7,3},{8,12},{12,8},{9,1... | collective-permute-start | bytes 6291464 | tf_op jit(solution)/shard_map/ppermute | solution.py:224
  8.7 1.2 copy-done.2
  10.0 1.6 %copy-done.4 = bf16[2048,512]{1,0:T(8,128)(2,1)S(1)} copy-done((bf16[2048,512]{1,0:T(8,128)(2,1)S(1)}, bf16[2048,512]{1,0:T(8,128)(2,1)}, u32[]{:S(2)}) %copy-start.4) | copy-done | bytes 2097176
  11.6 0.5 shard_map.68
  12.1 6.1 %psum.7.sums.m0 = f32[1,768]{1,0:T(1,128)S(1)} all-reduce(f32[1,768]{1,0:T(1,128)S(1)} %shard_map.68), channel_id=1, replica_groups=mesh['walker'=4,'prow'=2,'pcol'=4] {'walker'}, use_global_device_ids=true, to_apply=%region_0.1 | all-reduce | flops 768 | bytes 6144 | tf_op jit(solution)/shard_map/psum | solution.py:229
  18.2 1.1 collective-permute-start.3
  19.3 0.9 collective-permute-start.2
  20.2 0.4 copy.7.energy
  20.6 0.0 copy-start.5
  20.6 1.6 %copy-done.5 = bf16[2048,512]{1,0:T(8,128)(2,1)S(1)} copy-done((bf16[2048,512]{1,0:T(8,128)(2,1)S(1)}, bf16[2048,512]{1,0:T(8,128)(2,1)}, u32[]{:S(2)}) %copy-start.5) | copy-done | bytes 2097176
  22.2 1.6 %copy-done.6 = bf16[2048,512]{1,0:T(8,128)(2,1)S(1)} copy-done((bf16[2048,512]{1,0:T(8,128)(2,1)S(1)}, bf16[2048,512]{1,0:T(8,128)(2,1)}, u32[]{:S(2)}) %copy-start.6) | copy-done | bytes 2097176
  23.8 2.2 %shard_map.69 = (bf16[2048,1024]{1,0:T(8,128)(2,1)S(1)}, bf16[2048,256]{1,0:T(8,128)(2,1)}, bf16[2048,128]{1,0:T(8,128)(2,1)S(1)}, bf16[2048,128]{1,0:T(8,128)(2,1)S(1)}) custom-call(bf16[2048,512]{1,0:T(8,128)(2,1)S(1)} %copy-done.5, bf16[2048,512]{1,0:T(8,128)(2,1)S(1)} %copy-done.6, f32[2048,1]{1,0:T(8,128)S(1)} %copy.7.energy, f32[1,768]{1,0:T(1,128)S(1)} %psum.7.sums.m0), custom_call_target="tpu_custom_call" | custom-call | tf_op jit(solution)/shard_map/pallas_call | solution.py:18
  26.0 2.0 %copy-done = bf16[2048,1024]{1,0:T(8,128)(2,1)} copy-done((bf16[2048,1024]{1,0:T(8,128)(2,1)}, bf16[2048,1024]{1,0:T(8,128)(2,1)S(1)}, u32[]{:S(2)}) %copy-start) | copy-done | bytes 4194328
  27.9 0.8 copy-done.9
  28.7 0.8 copy-done.11
  29.5 0.8 collective-permute-done.3.m2
  30.3 0.1 collective-permute-done.2.m1
  30.4 1.3 collective-permute-start.4
  31.7 1.7 %collective-permute-start.5 = (bf16[2048,256]{1,0:T(8,128)(2,1)S(1)}, bf16[2048,256]{1,0:T(8,128)(2,1)}, u32[]{:S(2)}, u32[]{:S(2)}) collective-permute-start(bf16[2048,256]{1,0:T(8,128)(2,1)S(1)} %collective-permute-done.near), channel_id=1, source_target_pairs={{1,2},{2,1},{5,6},{6,5},{9,10},{10,9},{13,14},{14,13},{17,18},{18,... | collective-permute-start | bytes 3145736 | tf_op jit(solution)/shard_map/ppermute | solution.py:246
  33.4 2.2 %collective-permute-start.8 = (f32[1,768]{1,0:T(1,128)S(1)}, f32[1,768]{1,0:T(1,128)S(1)}, u32[]{:S(2)}, u32[]{:S(2)}) collective-permute-start(f32[1,768]{1,0:T(1,128)S(1)} %psum.7.sums.m0), channel_id=1, source_target_pairs={{0,3},{1,2},{2,1},{3,0},{4,7},{5,6},{6,5},{7,4},{8,11},{9,10},{10,... | collective-permute-start | bytes 9224 | tf_op jit(solution)/shard_map/ppermute | solution.py:243
  35.6 1.5 %collective-permute-start.7 = (f32[1,768]{1,0:T(1,128)S(1)}, f32[1,768]{1,0:T(1,128)S(1)}, u32[]{:S(2)}, u32[]{:S(2)}) collective-permute-start(f32[1,768]{1,0:T(1,128)S(1)} %psum.7.sums.m0), channel_id=1, source_target_pairs={{0,4},{4,0},{1,5},{5,1},{2,6},{6,2},{3,7},{7,3},{8,12},{12,8},{9,1... | collective-permute-start | bytes 9224 | tf_op jit(solution)/shard_map/ppermute | solution.py:244
  37.2 1.7 %collective-permute-done.8.m3 = f32[1,768]{1,0:T(1,128)S(1)} collective-permute-done((f32[1,768]{1,0:T(1,128)S(1)}, f32[1,768]{1,0:T(1,128)S(1)}, u32[]{:S(2)}, u32[]{:S(2)}) %collective-permute-start.8) | collective-permute-done | bytes 3104 | tf_op jit(solution)/shard_map/ppermute | solution.py:243
  38.9 1.5 %collective-permute-start.12 = (bf16[2048,256]{1,0:T(8,128)(2,1)}, bf16[2048,256]{1,0:T(8,128)(2,1)}, u32[]{:S(2)}, u32[]{:S(2)}) collective-permute-start(bf16[2048,256]{1,0:T(8,128)(2,1)} %get-tuple-element.51), channel_id=1, source_target_pairs={{0,4},{4,0},{1,5},{5,1},{2,6},{6,2},{3,7},{7,3},{8,12},{12,8},{9,1... | collective-permute-start | bytes 3145736 | tf_op jit(solution)/shard_map/ppermute | solution.py:247
  40.4 15.7 %collective-permute-done.7.far_sums = f32[1,768]{1,0:T(1,128)S(1)} collective-permute-done((f32[1,768]{1,0:T(1,128)S(1)}, f32[1,768]{1,0:T(1,128)S(1)}, u32[]{:S(2)}, u32[]{:S(2)}) %collective-permute-start.7) | collective-permute-done | bytes 3104 | tf_op jit(solution)/shard_map/ppermute | solution.py:244
  56.1 0.0 collective-permute-done.6.far_raw
  56.1 0.6 collective-permute-done.4.mid2
  56.7 1.0 copy-done.7
  57.7 0.0 collective-permute-done.5.last1
  57.7 1.3 collective-permute-start.11
  59.0 0.7 dynamic-slice_bitcast_fusion
  59.7 0.1 concatenate.3.info
  59.8 1.2 copy-done.8
  61.0 8.5 %shard_map.70 = (bf16[1,256,1536]{2,1,0:T(8,128)(2,1)S(1)}, bf16[1,256,1536]{2,1,0:T(8,128)(2,1)S(1)}, bf16[2,2048,256]{2,1,0:T(8,128)(2,1)S(1)}, bf16[2048,512]{1,0:T(8,128)(2,1)S(1)}) custom-call(s32[6]{0:T(128)S(1)} %concatenate.3.info, bf16[2048,256]{1,0:T(8,128)(2,1)S(1)} %copy-done.3, bf16[2048,256]{1,0:T(8,128)(2,1)S(1)} %collective-permute-done.near, ...), custom_call_target="tpu_custom_call" | custom-call | tf_op jit(solution)/shard_map/pallas_call | solution.py:18
  69.5 0.1 collective-permute-start.9
  69.6 7.3 %collective-permute-done.12.grads = bf16[2048,256]{1,0:T(8,128)(2,1)} collective-permute-done((bf16[2048,256]{1,0:T(8,128)(2,1)}, bf16[2048,256]{1,0:T(8,128)(2,1)}, u32[]{:S(2)}, u32[]{:S(2)}) %collective-permute-start.12) | collective-permute-done | bytes 1048608 | tf_op jit(solution)/shard_map/ppermute | solution.py:247
  76.9 8.5 %collective-permute-done.11.last2 = bf16[2048,256]{1,0:T(8,128)(2,1)} collective-permute-done((bf16[2048,256]{1,0:T(8,128)(2,1)}, bf16[2048,256]{1,0:T(8,128)(2,1)}, u32[]{:S(2)}, u32[]{:S(2)}) %collective-permute-start.11) | collective-permute-done | bytes 1048608 | tf_op jit(solution)/shard_map/ppermute | solution.py:252
  85.4 2.2 %copy-done.1 = bf16[2048,1024]{1,0:T(8,128)(2,1)S(1)} copy-done((bf16[2048,1024]{1,0:T(8,128)(2,1)S(1)}, bf16[2048,1024]{1,0:T(8,128)(2,1)}, u32[]{:S(2)}) %copy-start.1) | copy-done | bytes 4194328
  87.5 6.5 %shard_map.72 = (bf16[1,256,1536]{2,1,0:T(8,128)(2,1)S(1)}, bf16[1,256,1536]{2,1,0:T(8,128)(2,1)S(1)}, bf16[2,2048,256]{2,1,0:T(8,128)(2,1)S(1)}) custom-call(s32[6]{0:T(128)S(1)} %concatenate.3.info, bf16[2048,256]{1,0:T(8,128)(2,1)S(1)} %copy-done.3, bf16[2048,256]{1,0:T(8,128)(2,1)S(1)} %collective-permute-done.near, ...), custom_call_target="tpu_custom_call" | custom-call | tf_op jit(solution)/shard_map/pallas_call | solution.py:18
  94.0 0.1 collective-permute-start.13
  94.1 0.7 shard_map.71
  94.9 3.6 %collective-permute-start.10 = (bf16[256,1536]{1,0:T(8,128)(2,1)S(1)}, bf16[256,1536]{1,0:T(8,128)(2,1)S(1)}, u32[]{:S(2)}, u32[]{:S(2)}) collective-permute-start(bf16[256,1536]{1,0:T(8,128)(2,1)S(1)} %shard_map.71), channel_id=1, source_target_pairs={{0,16},{24,8},{1,17},{25,9},{2,18},{26,10},{3,19},{27,11},{4,20},{... | collective-permute-start | bytes 2359304 | tf_op jit(solution)/shard_map/ppermute | solution.py:274
  98.5 0.7 shard_map.73
  99.2 1.3 collective-permute-start.14
  100.5 0.6 collective-permute-start.17
  101.1 1.5 %collective-permute-start.20 = (bf16[2048,128]{1,0:T(8,128)(2,1)S(1)}, bf16[2048,128]{1,0:T(8,128)(2,1)S(1)}, u32[]{:S(2)}, u32[]{:S(2)}) collective-permute-start(bf16[2048,128]{1,0:T(8,128)(2,1)S(1)} %copy-done.10), channel_id=1, source_target_pairs={{0,4},{4,0},{1,5},{5,1},{2,6},{6,2},{3,7},{7,3},{8,12},{12,8},{9,1... | collective-permute-start | bytes 1572872 | tf_op jit(solution)/shard_map/ppermute | solution.py:286
  102.6 4.3 %shard_map.74 = (bf16[2,256,256]{2,1,0:T(8,128)(2,1)S(1)}, bf16[2,256,256]{2,1,0:T(8,128)(2,1)S(1)}) custom-call(s32[6]{0:T(128)S(1)} %concatenate.3.info, bf16[2,2048,256]{2,1,0:T(8,128)(2,1)S(1)} %get-tuple-element.57.early, bf16[2,2048,256]{2,1,0:T(8,128)(2,1)S(1)} %get-tuple-element.58.late, bf16[2048,512]{1,0:T(8,128)(2,1)S(1)} %get-tuple-element.54.far, ...), custom_call_target="tpu_custom_call" | custom-call | tf_op jit(solution)/shard_map/pallas_call | solution.py:18
  107.0 0.6 collective-permute-start.15
  107.6 7.7 %collective-permute-done.17.grads = bf16[2048,128]{1,0:T(8,128)(2,1)S(1)} collective-permute-done((bf16[2048,128]{1,0:T(8,128)(2,1)S(1)}, bf16[2048,128]{1,0:T(8,128)(2,1)S(1)}, u32[]{:S(2)}, u32[]{:S(2)}) %collective-permute-start.17) | collective-permute-done | bytes 524320 | tf_op jit(solution)/shard_map/ppermute | solution.py:253
  115.3 2.8 %shard_map.76 = (bf16[2,256,128]{2,1,0:T(8,128)(2,1)S(1)}, bf16[2,256,128]{2,1,0:T(8,128)(2,1)S(1)}) custom-call(s32[6]{0:T(128)S(1)} %concatenate.3.info, bf16[2,2048,256]{2,1,0:T(8,128)(2,1)S(1)} %get-tuple-element.57.early, bf16[2,2048,256]{2,1,0:T(8,128)(2,1)S(1)} %get-tuple-element.58.late, bf16[2048,512]{1,0:T(8,128)(2,1)S(1)} %get-tuple-element.54.far, ...), custom_call_target="tpu_custom_call" | custom-call | tf_op jit(solution)/shard_map/pallas_call | solution.py:18
  118.1 0.5 collective-permute-start.18
  118.6 7.9 %collective-permute-done.20.grads = bf16[2048,128]{1,0:T(8,128)(2,1)S(1)} collective-permute-done((bf16[2048,128]{1,0:T(8,128)(2,1)S(1)}, bf16[2048,128]{1,0:T(8,128)(2,1)S(1)}, u32[]{:S(2)}, u32[]{:S(2)}) %collective-permute-start.20) | collective-permute-done | bytes 524320 | tf_op jit(solution)/shard_map/ppermute | solution.py:286
  126.5 2.8 %shard_map.78 = (bf16[2,256,128]{2,1,0:T(8,128)(2,1)S(1)}, bf16[2,256,128]{2,1,0:T(8,128)(2,1)S(1)}) custom-call(s32[6]{0:T(128)S(1)} %concatenate.3.info, bf16[2,2048,256]{2,1,0:T(8,128)(2,1)S(1)} %get-tuple-element.57.early, bf16[2,2048,256]{2,1,0:T(8,128)(2,1)S(1)} %get-tuple-element.58.late, bf16[2048,512]{1,0:T(8,128)(2,1)S(1)} %get-tuple-element.54.far, ...), custom_call_target="tpu_custom_call" | custom-call | tf_op jit(solution)/shard_map/pallas_call | solution.py:18
  129.3 0.2 collective-permute-start.21
  129.5 0.6 shard_map.75
  130.1 0.1 collective-permute-start.16
  130.2 0.6 shard_map.77
  130.8 2.1 %collective-permute-start.19 = (bf16[256,128]{1,0:T(8,128)(2,1)S(1)}, bf16[256,128]{1,0:T(8,128)(2,1)S(1)}, u32[]{:S(2)}, u32[]{:S(2)}) collective-permute-start(bf16[256,128]{1,0:T(8,128)(2,1)S(1)} %shard_map.77), channel_id=1, source_target_pairs={{0,16},{8,24},{16,0},{24,8},{1,17},{9,25},{17,1},{25,9},{2,18},{10... | collective-permute-start | bytes 196616 | tf_op jit(solution)/shard_map/ppermute | solution.py:274
  132.9 0.6 shard_map.79
  133.4 0.1 collective-permute-start.22
  133.5 4.4 %collective-permute-done.19.refs_11_ = bf16[256,128]{1,0:T(8,128)(2,1)S(1)} collective-permute-done((bf16[256,128]{1,0:T(8,128)(2,1)S(1)}, bf16[256,128]{1,0:T(8,128)(2,1)S(1)}, u32[]{:S(2)}, u32[]{:S(2)}) %collective-permute-start.19) | collective-permute-done | bytes 65568 | tf_op jit(solution)/shard_map/ppermute | solution.py:274
  137.9 0.8 collective-permute-done.22.refs_14_
  138.8 2.6 %shard_map.80 = (f32[256,1024]{1,0:T(8,128)}, f32[256,1024]{1,0:T(8,128)}) custom-call(s32[6]{0:T(128)S(1)} %concatenate.3.info, bf16[1,256,1536]{2,1,0:T(8,128)(2,1)S(1)} %get-tuple-element.47.keep.refs_0_, bf16[1,256,1536]{2,1,0:T(8,128)(2,1)S(1)} %collective-permute-done.9.got.refs_1_, bf16[256,1536]{1,0:T(8,128)(2,1)S(1)} %collective-permute-done.10.refs_2_, ...), custom_call_target="tpu_custom_call" | custom-call | tf_op jit(solution)/shard_map/pallas_call | solution.py:18
  (27 shorter events, 0.1 us)
Async XLA Ops:
  0.6 29.8 %collective-permute-start.1 = (bf16[2048,256]{1,0:T(8,128)(2,1)}, bf16[2048,256]{1,0:T(8,128)(2,1)}, u32[]{:S(2)}, u32[]{:S(2)}) collective-permute-start(bf16[2048,256]{1,0:T(8,128)(2,1)} %own_rows.3), channel_id=1, source_target_pairs={{1,2},{2,1},{5,6},{6,5},{9,10},{10,9},{13,14},{14,13},{17,18},{18,... | collective-permute-start | bytes 3145736 | tf_op jit(solution)/shard_map/ppermute | solution.py:226
  2.4 28.1 %collective-permute-start = (bf16[2048,256]{1,0:T(8,128)(2,1)}, bf16[2048,256]{1,0:T(8,128)(2,1)S(1)}, u32[]{:S(2)}, u32[]{:S(2)}) collective-permute-start(bf16[2048,256]{1,0:T(8,128)(2,1)} %own_rows.3), channel_id=1, source_target_pairs={{0,1},{1,0},{2,3},{3,2},{4,5},{5,4},{6,7},{7,6},{8,9},{9,8},{10,11... | collective-permute-start | bytes 3145736 | tf_op jit(solution)/shard_map/ppermute | solution.py:225
  7.2 48.9 %collective-permute-start.6 = (bf16[2048,512]{1,0:T(8,128)(2,1)}, bf16[2048,512]{1,0:T(8,128)(2,1)}, u32[]{:S(2)}, u32[]{:S(2)}) collective-permute-start(bf16[2048,512]{1,0:T(8,128)(2,1)} %cols.3), channel_id=1, source_target_pairs={{0,4},{4,0},{1,5},{5,1},{2,6},{6,2},{3,7},{7,3},{8,12},{12,8},{9,1... | collective-permute-start | bytes 6291464 | tf_op jit(solution)/shard_map/ppermute | solution.py:224
  8.7 1.2 copy-start.2
  10.0 1.6 %copy-start.4 = (bf16[2048,512]{1,0:T(8,128)(2,1)S(1)}, bf16[2048,512]{1,0:T(8,128)(2,1)}, u32[]{:S(2)}) copy-start(bf16[2048,512]{1,0:T(8,128)(2,1)} %cols.3) | copy-start | bytes 6291460
  11.6 8.6 %copy-start.13 = (f32[2048]{0:T(1024)S(1)}, f32[2048]{0:T(1024)}, u32[]{:S(2)}) copy-start(f32[2048]{0:T(1024)} %param.8) | copy-start | bytes 24580
  18.2 12.1 %collective-permute-start.3 = (f32[1,768]{1,0:T(1,128)S(1)}, f32[1,768]{1,0:T(1,128)S(1)}, u32[]{:S(2)}, u32[]{:S(2)}) collective-permute-start(f32[1,768]{1,0:T(1,128)S(1)} %psum.7.sums.m0), channel_id=1, source_target_pairs={{0,2},{1,3},{2,0},{3,1},{4,6},{5,7},{6,4},{7,5},{8,10},{9,11},{10,... | collective-permute-start | bytes 9224 | tf_op jit(solution)/shard_map/ppermute | solution.py:231
  19.3 11.1 %collective-permute-start.2 = (f32[1,768]{1,0:T(1,128)S(1)}, f32[1,768]{1,0:T(1,128)S(1)}, u32[]{:S(2)}, u32[]{:S(2)}) collective-permute-start(f32[1,768]{1,0:T(1,128)S(1)} %psum.7.sums.m0), channel_id=1, source_target_pairs={{0,1},{1,0},{2,3},{3,2},{4,5},{5,4},{6,7},{7,6},{8,9},{9,8},{10,11... | collective-permute-start | bytes 9224 | tf_op jit(solution)/shard_map/ppermute | solution.py:230
  20.6 1.6 %copy-start.5 = (bf16[2048,512]{1,0:T(8,128)(2,1)S(1)}, bf16[2048,512]{1,0:T(8,128)(2,1)}, u32[]{:S(2)}) copy-start(bf16[2048,512]{1,0:T(8,128)(2,1)} %cols.3) | copy-start | bytes 6291460
  22.2 1.6 %copy-start.6 = (bf16[2048,512]{1,0:T(8,128)(2,1)S(1)}, bf16[2048,512]{1,0:T(8,128)(2,1)}, u32[]{:S(2)}) copy-start(bf16[2048,512]{1,0:T(8,128)(2,1)} %grads.1) | copy-start | bytes 6291460
  23.8 36.0 %copy-start.3 = (bf16[2048,256]{1,0:T(8,128)(2,1)S(1)}, bf16[2048,256]{1,0:T(8,128)(2,1)}, u32[]{:S(2)}) copy-start(bf16[2048,256]{1,0:T(8,128)(2,1)} %own_rows.3) | copy-start | bytes 3145732
  26.0 2.0 %copy-start = (bf16[2048,1024]{1,0:T(8,128)(2,1)}, bf16[2048,1024]{1,0:T(8,128)(2,1)S(1)}, u32[]{:S(2)}) copy-start(bf16[2048,1024]{1,0:T(8,128)(2,1)S(1)} %get-tuple-element.44.ow) | copy-start | bytes 12582916
  27.9 0.8 copy-start.9
  28.7 0.8 copy-start.11
  30.4 26.3 %collective-permute-start.4 = (bf16[2048,256]{1,0:T(8,128)(2,1)}, bf16[2048,256]{1,0:T(8,128)(2,1)S(1)}, u32[]{:S(2)}, u32[]{:S(2)}) collective-permute-start(bf16[2048,256]{1,0:T(8,128)(2,1)} %collective-permute-done.1.mid1), channel_id=1, source_target_pairs={{1,0},{2,3},{5,4},{6,7},{9,8},{10,11},{13,12},{14,15},{17,16},{18,... | collective-permute-start | bytes 3145736 | tf_op jit(solution)/shard_map/ppermute | solution.py:245
  31.7 25.9 %collective-permute-start.5 = (bf16[2048,256]{1,0:T(8,128)(2,1)S(1)}, bf16[2048,256]{1,0:T(8,128)(2,1)}, u32[]{:S(2)}, u32[]{:S(2)}) collective-permute-start(bf16[2048,256]{1,0:T(8,128)(2,1)S(1)} %collective-permute-done.near), channel_id=1, source_target_pairs={{1,2},{2,1},{5,6},{6,5},{9,10},{10,9},{13,14},{14,13},{17,18},{18,... | collective-permute-start | bytes 3145736 | tf_op jit(solution)/shard_map/ppermute | solution.py:246
  33.4 5.5 %collective-permute-start.8 = (f32[1,768]{1,0:T(1,128)S(1)}, f32[1,768]{1,0:T(1,128)S(1)}, u32[]{:S(2)}, u32[]{:S(2)}) collective-permute-start(f32[1,768]{1,0:T(1,128)S(1)} %psum.7.sums.m0), channel_id=1, source_target_pairs={{0,3},{1,2},{2,1},{3,0},{4,7},{5,6},{6,5},{7,4},{8,11},{9,10},{10,... | collective-permute-start | bytes 9224 | tf_op jit(solution)/shard_map/ppermute | solution.py:243
  35.6 20.5 %collective-permute-start.7 = (f32[1,768]{1,0:T(1,128)S(1)}, f32[1,768]{1,0:T(1,128)S(1)}, u32[]{:S(2)}, u32[]{:S(2)}) collective-permute-start(f32[1,768]{1,0:T(1,128)S(1)} %psum.7.sums.m0), channel_id=1, source_target_pairs={{0,4},{4,0},{1,5},{5,1},{2,6},{6,2},{3,7},{7,3},{8,12},{12,8},{9,1... | collective-permute-start | bytes 9224 | tf_op jit(solution)/shard_map/ppermute | solution.py:244
  38.9 38.0 %collective-permute-start.12 = (bf16[2048,256]{1,0:T(8,128)(2,1)}, bf16[2048,256]{1,0:T(8,128)(2,1)}, u32[]{:S(2)}, u32[]{:S(2)}) collective-permute-start(bf16[2048,256]{1,0:T(8,128)(2,1)} %get-tuple-element.51), channel_id=1, source_target_pairs={{0,4},{4,0},{1,5},{5,1},{2,6},{6,2},{3,7},{7,3},{8,12},{12,8},{9,1... | collective-permute-start | bytes 3145736 | tf_op jit(solution)/shard_map/ppermute | solution.py:247
  56.7 1.0 copy-start.7
  57.7 27.7 %collective-permute-start.11 = (bf16[2048,256]{1,0:T(8,128)(2,1)}, bf16[2048,256]{1,0:T(8,128)(2,1)}, u32[]{:S(2)}, u32[]{:S(2)}) collective-permute-start(bf16[2048,256]{1,0:T(8,128)(2,1)} %collective-permute-done.5.last1), channel_id=1, source_target_pairs={{1,0},{2,3},{5,4},{6,7},{9,8},{10,11},{13,12},{14,15},{17,16},{18,... | collective-permute-start | bytes 3145736 | tf_op jit(solution)/shard_map/ppermute | solution.py:252
  59.8 1.2 copy-start.8
  69.5 24.6 %collective-permute-start.9 = (bf16[1,256,1536]{2,1,0:T(8,128)(2,1)S(1)}, bf16[1,256,1536]{2,1,0:T(8,128)(2,1)S(1)}, u32[]{:S(2)}, u32[]{:S(2)}) collective-permute-start(bf16[1,256,1536]{2,1,0:T(8,128)(2,1)S(1)} %get-tuple-element.48), channel_id=1, source_target_pairs={{0,8},{8,0},{16,24},{24,16},{1,9},{9,1},{17,25},{25,17},{2,10},{10... | collective-permute-start | bytes 2359304 | tf_op jit(solution)/shard_map/ppermute | solution.py:267
  85.4 2.2 %copy-start.1 = (bf16[2048,1024]{1,0:T(8,128)(2,1)S(1)}, bf16[2048,1024]{1,0:T(8,128)(2,1)}, u32[]{:S(2)}) copy-start(bf16[2048,1024]{1,0:T(8,128)(2,1)} %copy-done) | copy-start | bytes 12582916
  94.0 4.5 %collective-permute-start.13 = (bf16[1,256,1536]{2,1,0:T(8,128)(2,1)S(1)}, bf16[1,256,1536]{2,1,0:T(8,128)(2,1)S(1)}, u32[]{:S(2)}, u32[]{:S(2)}) collective-permute-start(bf16[1,256,1536]{2,1,0:T(8,128)(2,1)S(1)} %get-tuple-element.56), channel_id=1, source_target_pairs={{0,8},{8,0},{16,24},{24,16},{1,9},{9,1},{17,25},{25,17},{2,10},{10... | collective-permute-start | bytes 2359304 | tf_op jit(solution)/shard_map/ppermute | solution.py:267
  94.1 6.4 %copy-start.12 = (bf16[2048,128]{1,0:T(8,128)(2,1)S(1)}, bf16[2048,128]{1,0:T(8,128)(2,1)}, u32[]{:S(2)}) copy-start(bf16[2048,128]{1,0:T(8,128)(2,1)} %copy-done.11) | copy-start | bytes 1572868
  94.1 7.0 %copy-start.10 = (bf16[2048,128]{1,0:T(8,128)(2,1)S(1)}, bf16[2048,128]{1,0:T(8,128)(2,1)}, u32[]{:S(2)}) copy-start(bf16[2048,128]{1,0:T(8,128)(2,1)} %copy-done.9) | copy-start | bytes 1572868
  94.9 43.1 %collective-permute-start.10 = (bf16[256,1536]{1,0:T(8,128)(2,1)S(1)}, bf16[256,1536]{1,0:T(8,128)(2,1)S(1)}, u32[]{:S(2)}, u32[]{:S(2)}) collective-permute-start(bf16[256,1536]{1,0:T(8,128)(2,1)S(1)} %shard_map.71), channel_id=1, source_target_pairs={{0,16},{24,8},{1,17},{25,9},{2,18},{26,10},{3,19},{27,11},{4,20},{... | collective-permute-start | bytes 2359304 | tf_op jit(solution)/shard_map/ppermute | solution.py:274
  99.2 39.6 %collective-permute-start.14 = (bf16[256,1536]{1,0:T(8,128)(2,1)S(1)}, bf16[256,1536]{1,0:T(8,128)(2,1)S(1)}, u32[]{:S(2)}, u32[]{:S(2)}) collective-permute-start(bf16[256,1536]{1,0:T(8,128)(2,1)S(1)} %shard_map.73), channel_id=1, source_target_pairs={{8,24},{16,0},{9,25},{17,1},{10,26},{18,2},{11,27},{19,3},{12,28},... | collective-permute-start | bytes 2359304 | tf_op jit(solution)/shard_map/ppermute | solution.py:274
  100.5 14.7 %collective-permute-start.17 = (bf16[2048,128]{1,0:T(8,128)(2,1)S(1)}, bf16[2048,128]{1,0:T(8,128)(2,1)S(1)}, u32[]{:S(2)}, u32[]{:S(2)}) collective-permute-start(bf16[2048,128]{1,0:T(8,128)(2,1)S(1)} %copy-done.12), channel_id=1, source_target_pairs={{0,4},{4,0},{1,5},{5,1},{2,6},{6,2},{3,7},{7,3},{8,12},{12,8},{9,1... | collective-permute-start | bytes 1572872 | tf_op jit(solution)/shard_map/ppermute | solution.py:253
  101.1 25.4 %collective-permute-start.20 = (bf16[2048,128]{1,0:T(8,128)(2,1)S(1)}, bf16[2048,128]{1,0:T(8,128)(2,1)S(1)}, u32[]{:S(2)}, u32[]{:S(2)}) collective-permute-start(bf16[2048,128]{1,0:T(8,128)(2,1)S(1)} %copy-done.10), channel_id=1, source_target_pairs={{0,4},{4,0},{1,5},{5,1},{2,6},{6,2},{3,7},{7,3},{8,12},{12,8},{9,1... | collective-permute-start | bytes 1572872 | tf_op jit(solution)/shard_map/ppermute | solution.py:286
  107.0 22.6 %collective-permute-start.15 = (bf16[2,256,256]{2,1,0:T(8,128)(2,1)S(1)}, bf16[2,256,256]{2,1,0:T(8,128)(2,1)S(1)}, u32[]{:S(2)}, u32[]{:S(2)}) collective-permute-start(bf16[2,256,256]{2,1,0:T(8,128)(2,1)S(1)} %get-tuple-element.61), channel_id=1, source_target_pairs={{0,8},{8,0},{16,24},{24,16},{1,9},{9,1},{17,25},{25,17},{2,10},{10... | collective-permute-start | bytes 786440 | tf_op jit(solution)/shard_map/ppermute | solution.py:267
  118.1 12.1 %collective-permute-start.18 = (bf16[2,256,128]{2,1,0:T(8,128)(2,1)S(1)}, bf16[2,256,128]{2,1,0:T(8,128)(2,1)S(1)}, u32[]{:S(2)}, u32[]{:S(2)}) collective-permute-start(bf16[2,256,128]{2,1,0:T(8,128)(2,1)S(1)} %get-tuple-element.64), channel_id=1, source_target_pairs={{0,8},{8,0},{16,24},{24,16},{1,9},{9,1},{17,25},{25,17},{2,10},{10... | collective-permute-start | bytes 393224 | tf_op jit(solution)/shard_map/ppermute | solution.py:267
  129.3 3.5 %collective-permute-start.21 = (bf16[2,256,128]{2,1,0:T(8,128)(2,1)S(1)}, bf16[2,256,128]{2,1,0:T(8,128)(2,1)S(1)}, u32[]{:S(2)}, u32[]{:S(2)}) collective-permute-start(bf16[2,256,128]{2,1,0:T(8,128)(2,1)S(1)} %get-tuple-element.67), channel_id=1, source_target_pairs={{0,8},{8,0},{16,24},{24,16},{1,9},{9,1},{17,25},{25,17},{2,10},{10... | collective-permute-start | bytes 393224 | tf_op jit(solution)/shard_map/ppermute | solution.py:267
  130.1 7.8 %collective-permute-start.16 = (bf16[256,256]{1,0:T(8,128)(2,1)S(1)}, bf16[256,256]{1,0:T(8,128)(2,1)S(1)}, u32[]{:S(2)}, u32[]{:S(2)}) collective-permute-start(bf16[256,256]{1,0:T(8,128)(2,1)S(1)} %shard_map.75), channel_id=1, source_target_pairs={{0,16},{8,24},{16,0},{24,8},{1,17},{9,25},{17,1},{25,9},{2,18},{10... | collective-permute-start | bytes 393224 | tf_op jit(solution)/shard_map/ppermute | solution.py:274
  130.8 7.2 %collective-permute-start.19 = (bf16[256,128]{1,0:T(8,128)(2,1)S(1)}, bf16[256,128]{1,0:T(8,128)(2,1)S(1)}, u32[]{:S(2)}, u32[]{:S(2)}) collective-permute-start(bf16[256,128]{1,0:T(8,128)(2,1)S(1)} %shard_map.77), channel_id=1, source_target_pairs={{0,16},{8,24},{16,0},{24,8},{1,17},{9,25},{17,1},{25,9},{2,18},{10... | collective-permute-start | bytes 196616 | tf_op jit(solution)/shard_map/ppermute | solution.py:274
  133.4 5.3 %collective-permute-start.22 = (bf16[256,128]{1,0:T(8,128)(2,1)S(1)}, bf16[256,128]{1,0:T(8,128)(2,1)S(1)}, u32[]{:S(2)}, u32[]{:S(2)}) collective-permute-start(bf16[256,128]{1,0:T(8,128)(2,1)S(1)} %shard_map.79), channel_id=1, source_target_pairs={{0,16},{8,24},{16,0},{24,8},{1,17},{9,25},{17,1},{25,9},{2,18},{10... | collective-permute-start | bytes 196616 | tf_op jit(solution)/shard_map/ppermute | solution.py:274

commit v2 on v1

v2 whole, which is shorter than its diff:
```python
import functools

import jax
import jax.numpy as jnp
from jax import lax
from jax.experimental import pallas as pl
from jax.experimental.pallas import tpu as pltpu
from jax.sharding import PartitionSpec as P

BF = jnp.bfloat16
F32 = jnp.float32
VMEM = pl.BlockSpec(memory_space=pltpu.VMEM)
SMEM = pl.BlockSpec(memory_space=pltpu.SMEM)
MID, LOW, CORE, STRAIGHT, TABLE = 0, 1, 2, 3, 4
MEAN_COST, FAR_COST, FIRST_COST, LAST_COST = 6, 3, 0, 4
WEIGH_COSTS, GATHER_COST = (0, 0, 12), 3


def call(kernel, outs, *args, scratch=(), limit=24, cost=0):
    return pl.pallas_call(
        kernel,
        out_shape=[jax.ShapeDtypeStruct(s, d) for s, d in outs],
        in_specs=[SMEM if a.dtype == jnp.int32 else VMEM for a in args],
        out_specs=[VMEM] * len(outs),
        scratch_shapes=list(scratch),
        compiler_params=pltpu.CompilerParams(vmem_limit_bytes=limit * 2**20),
        cost_estimate=pl.CostEstimate(
            flops=int(cost * 1.15e9), bytes_accessed=0, transcendentals=0
        ),
    )(*args)


def after(value, *others):
    return lax.optimization_barrier((value,) + others)[0]


def centred(values, mean):
    return (values.astype(F32) - mean).astype(BF)


def weigh(energy, cols, grads):
    return (energy * cols.astype(F32) + grads.astype(F32)).astype(BF)


def dot(rows, right):
    return lax.dot_general(rows, right, (((0,), (0,)), ((), ())), preferred_element_type=F32)


def sums_kernel(rows, cols, out):
    width = rows.shape[1]
    out[:, :width] = jnp.sum(rows[...].astype(F32), axis=0, keepdims=True)
    out[:, width:] = jnp.sum(cols[...].astype(F32), axis=0, keepdims=True)


def own_kernel(count, cuts, cols, grads, energy, sums, out, wide, *pieces):
    width = cols.shape[1]
    lanes = wide.shape[1]
    d = centred(cols[...], sums[:, -width:] / count)
    out[:, :width] = d
    spread = jnp.broadcast_to(energy[...], wide.shape)
    wide[...] = spread
    for a in range(0, width, lanes):
        b = a + lanes
        out[:, width + a : width + b] = weigh(spread, d[:, a:b], grads[:, a:b])
    for a, b, piece in zip(cuts[:-1], cuts[1:], pieces):
        piece[...] = grads[:, a:b]


def by_core(info, walker, slot, sends, keep, value):
    @pl.when(info[CORE] == walker % 2)
    def _():
        keep[slot] = value

    @pl.when(info[CORE] != walker % 2)
    def _():
        start = 0
        for send in sends:
            width = send.shape[-1]
            send[slot] = value[:, start : start + width]
            start += width


def products(tile, rights):
    return jnp.concatenate([dot(tile, right[...]).astype(BF) for right in rights], axis=1)


def by_block(info, block, axis, per, slots, sends, keep, value):
    piece = value.shape[axis] // per
    for i in range(per):
        at = slice(i * piece, (i + 1) * piece)
        walker = block * per + i
        part = value[at] if axis == 0 else value[:, at]
        by_core(info, walker, slots[walker], sends, keep, part)


def low_or_high(info, then):
    for low in (1, 0):
        pl.when(info[LOW] == low)(functools.partial(then, 0 if low else 3, 3 if low else 0))


def mean_kernel(count, sums, out):
    out[...] = sums[:, -out.shape[1] :] / count


def far_kernel(raw, mean, out):
    out[...] = centred(raw[...], mean[...])


def early_kernel(
    count, per, slots,
    info, own_rows, near, mid1, mid2, m0, m1, m2, m3, ow, far,
    keep, early, *sends,
):
    rw = own_rows.shape[1]

    def group(there, beside):
        @pl.when(info[LOW] == 1)
        def _():
            early[:, rw:] = there
            early[:, :rw] = beside

        @pl.when(info[LOW] == 0)
        def _():
            early[:, :rw] = there
            early[:, rw:] = beside

    @pl.when(info[MID] == 1)
    def _():
        own = centred(own_rows[...], m0[:, :rw] / count)
        group(centred(mid1[...], m3[:, :rw] / count), own)

    @pl.when(info[MID] == 0)
    def _():
        next_to = centred(near[...], m1[:, :rw] / count)
        group(centred(mid2[...], m2[:, :rw] / count), next_to)

    result = products(early[...], (ow, far))
    for j, block in enumerate((1, 2)):
        by_block(info, block, 0, per, slots, sends, keep, result[j * rw : (j + 1) * rw])


def second_kernel(count, info, own_rows, near, m0, m1, ow, far, second, held):
    rw = own_rows.shape[1]

    @pl.when(info[MID] == 1)
    def _():
        second[...] = centred(near[...], m1[:, :rw] / count)

    @pl.when(info[MID] == 0)
    def _():
        second[...] = centred(own_rows[...], m0[:, :rw] / count)

    held[...] = products(second[...], (ow, far))


def first_chunk_kernel(start, second, far, wide, grads, right, held):
    weigh_kernel(start, far, wide, grads, right)
    held[...] = products(second[...], (right,))


def early_chunk_kernel(per, slots, info, early, right, keep, send):
    rw = early.shape[1] // 2
    result = products(early[...], (right,))
    for j, block in enumerate((1, 2)):
        by_block(info, block, 0, per, slots, (send,), keep, result[j * rw : (j + 1) * rw])


def late_kernel(
    count, per, slots,
    info, last1, last2, m2, m3, ow, far, chunk, held, held_chunk,
    keep, tile, *sends,
):
    rw = last1.shape[1]

    @pl.when(info[MID] == 1)
    def _():
        tile[...] = centred(last1[...], m2[:, :rw] / count)

    @pl.when(info[MID] == 0)
    def _():
        tile[...] = centred(last2[...], m3[:, :rw] / count)

    result = products(tile[...], (ow, far, chunk))
    before = jnp.concatenate((held[...], held_chunk[...]), axis=1)

    @functools.partial(low_or_high, info)
    def _(second_block, last_block):
        by_block(info, second_block, 0, per, slots, sends, keep, before)
        by_block(info, last_block, 0, per, slots, sends, keep, result)


def weigh_kernel(start, far, wide, grads, out):
    n, lanes = grads.shape[1], wide.shape[1]
    for a in range(0, n, lanes):
        cols = far[:, start + a : start + a + lanes]
        out[:, a : a + lanes] = weigh(wide[...], cols, grads[:, a : a + lanes])


def chunk_kernel(per, slots, info, early, second, last, right_ref, send, keep):
    rw = last.shape[1]
    right = right_ref[...]
    result = dot(right, early[...]).astype(BF)
    for j, block in enumerate((1, 2)):
        by_block(info, block, 1, per, slots, (send,), keep, result[:, j * rw : (j + 1) * rw])
    of_second = dot(right, second[...]).astype(BF)
    of_last = dot(right, last[...]).astype(BF)

    @functools.partial(low_or_high, info)
    def _(second_block, last_block):
        by_block(info, second_block, 1, per, slots, (send,), keep, of_second)
        by_block(info, last_block, 1, per, slots, (send,), keep, of_last)


def pair(keep, gots, i):
    start, values = 0, []
    for got in gots:
        width = got.shape[2]
        values.append(keep[i, :, start : start + width].astype(F32) + got[i].astype(F32))
        start += width
    return jnp.concatenate(values, axis=1)


def pair_kernel(first, pieces, count, cuts, info, keep, *refs):
    gots, outs = refs[:count], refs[count:]
    parts = len(cuts) - 1
    for k in range(len(outs) // parts):
        i = jnp.clip(info[TABLE + k + 1] - first, 0, pieces - 1)
        value = pair(keep, gots, i).astype(BF)
        for part in range(parts):
            outs[k * parts + part][...] = value[:, cuts[part] : cuts[part + 1]]


def total(keep, gots, others, i, cuts):
    parts = len(cuts) - 1
    value = pair(keep, gots, i)
    for k in range(len(others) // parts):
        got = [other[...] for other in others[k * parts : (k + 1) * parts]]
        value = value + jnp.concatenate(got, axis=1).astype(F32)
    return value


def gather_kernel(count, shapes, info, *refs):
    ham, corr = refs[-2:]
    cw = ham.shape[1] // 2
    pos = info[TABLE]

    def put(out, near, start, value):
        @pl.when((info[STRAIGHT] == 1) == near)
        def _():
            out[:, start : start + value.shape[1]] = value

        @pl.when((info[STRAIGHT] == 1) != near)
        def _():
            out[:, cw + start : cw + start + value.shape[1]] = value

    at = 0
    for n_gots, n_others, first, pieces, parts, cuts in shapes:
        keep, gots = refs[at], refs[at + 1 : at + 1 + n_gots]
        others = refs[at + 1 + n_gots : at + 1 + n_gots + n_others]
        at += 1 + n_gots + n_others

        @pl.when((pos >= first) & (pos < first + pieces))
        def _():
            value = total(keep, gots, others, pos - first, cuts) / count
            start = 0
            for got, (out, near, to) in zip(gots, parts):
                width = got.shape[2]
                put((ham, corr)[out], near, to, value[:, start : start + width])
                start += width


def last_kernel(count, shapes, info, held, *refs):
    del held
    out = refs[-1]
    at = start = 0
    for n_others, n in shapes:
        keep, got, *others = refs[at : at + 2 + n_others]
        at += 2 + n_others
        value = total(keep, (got,), others, info[TABLE], (0, keep.shape[2]))
        out[:, start : start + n] = value.T / count
        start += n


def last_chunks(count, start, info, ham, messages):
    rows, width = ham.shape
    shapes = [(len(others), keep.shape[1]) for keep, _, others, *_ in messages]
    flat = [a for keep, gots, others, *_ in messages for a in (keep, *gots, *others)]
    n = sum(s[1] for s in shapes)
    ahead, behind = (width // 2 + start) // n, start // n
    vmem = pl.BlockSpec(memory_space=pltpu.VMEM)
    return pl.pallas_call(
        functools.partial(last_kernel, count, shapes),
        out_shape=jax.ShapeDtypeStruct(ham.shape, ham.dtype),
        grid_spec=pltpu.PrefetchScalarGridSpec(
            num_scalar_prefetch=1,
            grid=(1,),
            in_specs=[pl.BlockSpec(memory_space=pl.ANY)] + [vmem] * len(flat),
            out_specs=pl.BlockSpec(
                (rows, n), lambda i, info: (0, jnp.where(info[STRAIGHT] == 1, ahead, behind))
            ),
        ),
        input_output_aliases={1: 0},
        compiler_params=pltpu.CompilerParams(vmem_limit_bytes=16 * 2**20),
        cost_estimate=pl.CostEstimate(flops=0, bytes_accessed=0, transcendentals=0),
    )(info, ham, *flat)


def per_device(o_rows, o_cols, grad_energy, energy):
    samples, rw = o_rows.shape
    cw = o_cols.shape[1]
    walkers = lax.axis_size("walker")
    chips = walkers // 2
    per = walkers // 4
    piece = rw // per
    w, y, z = (lax.axis_index(a) for a in ("walker", "prow", "pcol"))
    count = samples * walkers
    flip = [(0, 1), (1, 0)]
    outer = [(0, 1), (1, 0), (2, 3), (3, 2)]
    inner = [(1, 2), (2, 1)]
    ends = [(1, 0), (2, 3)]
    other_core = [(v, v ^ 1) for v in range(walkers)]

    order = [b * per + i for b in (1, 2, 0, 3) for i in range(per)]
    place = {v: [u for u in order if u % 2 == v % 2].index(v) for v in order}
    late_slots = {v: place[v] - per for v in order}
    table = [[place[(v + 2 * k) % walkers] for k in range(chips)] for v in range(walkers)]
    info = jnp.concatenate(
        (
            jnp.stack(((z == 1) | (z == 2), z < 2, w % 2, y == 0)).astype(jnp.int32),
            jnp.asarray(table, jnp.int32)[w],
        )
    )

    def shift(k, first, pieces):
        return [
            (v, (v + 2 * k) % walkers)
            for v in range(walkers)
            if first <= table[v][k] < first + pieces
        ]

    far_raw = lax.ppermute(o_cols, "prow", flip)
    near = lax.ppermute(o_rows, "pcol", outer)
    mid1 = lax.ppermute(o_rows, "pcol", inner)

    (sums,) = call(sums_kernel, [((1, rw + cw), F32)], o_rows, o_cols)
    m0 = lax.psum(sums, "walker")
    m1 = lax.ppermute(m0, "pcol", outer)
    m2 = lax.ppermute(m0, "pcol", [(0, 2), (1, 3), (2, 0), (3, 1)])

    column = energy[:, None]
    cuts = [0, cw // 2, 3 * cw // 4, cw]
    widths = [b - a for a, b in zip(cuts[:-1], cuts[1:])]
    ow, wide, *grads = call(
        functools.partial(own_kernel, count, cuts),
        [((samples, 2 * cw), BF), ((samples, min(widths)), F32)]
        + [((samples, n), BF) for n in widths],
        o_cols, grad_energy, column, m0,
    )

    near, mid1, m1, m2, ow, m0, *grads = lax.optimization_barrier(
        (near, mid1, m1, m2, ow, m0, *grads)
    )
    m3 = lax.ppermute(m0, "pcol", [(0, 3), (1, 2), (2, 1), (3, 0)])
    far_sums = lax.ppermute(m0, "prow", flip)
    mid2 = lax.ppermute(mid1, "pcol", ends)
    last1 = lax.ppermute(near, "pcol", inner)
    far_grads = [lax.ppermute(grads[0], "prow", flip)]

    (far_mean,) = call(
        functools.partial(mean_kernel, count), [((1, cw), F32)], far_sums, cost=MEAN_COST
    )
    (far,) = call(far_kernel, [((samples, cw), BF)], far_raw, far_mean, cost=FAR_COST)
    second, held = call(
        functools.partial(second_kernel, count),
        [((samples, rw), BF), ((rw, 3 * cw), BF)],
        info, o_rows, near, m0, m1, ow, far,
    )
    mid2, last1, far, m3, second, held, *grads = lax.optimization_barrier(
        (mid2, last1, far, m3, second, held, *grads)
    )
    last2 = lax.ppermute(last1, "pcol", ends)
    far_grads += [lax.ppermute(g, "prow", flip) for g in grads[1:]]

    messages = []

    def reduce(sends, keep, first, pieces, parts, split=None):
        width = keep.shape[2]
        at = (0, split, width) if split else (0, width)
        gots = [lax.ppermute(send, "walker", other_core) for send in sends]
        shapes = [((keep.shape[1], b - a), BF) for a, b in zip(at[:-1], at[1:])]
        sent = call(
            functools.partial(pair_kernel, first, pieces, len(gots), at),
            shapes * (chips - 1),
            info, keep, *gots,
        )
        others = [
            lax.ppermute(s, "walker", shift(i // len(shapes) + 1, first, pieces))
            for i, s in enumerate(sent)
        ]
        messages.append([keep, gots, others, first, pieces, parts, at])
        return sent

    parts = [(1, True, 0), (0, True, 0), (1, False, 0)]
    n = widths[0]
    message, short = ((per, piece, cw), BF), ((per, piece, n), BF)
    e_keep, early, *sends = call(
        functools.partial(early_kernel, count, per, place),
        [((per, piece, 3 * cw), BF), ((samples, 2 * rw), BF)] + [message] * 3,
        info, o_rows, near, mid1, mid2, m0, m1, m2, m3, ow, far,
    )
    reduce(sends, e_keep, 0, per, parts, 2 * cw)

    chunk, held_chunk = call(
        functools.partial(first_chunk_kernel, 0),
        [((samples, n), BF), ((rw, n), BF)],
        second, far, wide, far_grads[0],
        cost=FIRST_COST,
    )
    early_x = messages[0][2]
    last2, held_chunk, chunk, far_grads[1], *early_x = lax.optimization_barrier(
        (last2, held_chunk, chunk, far_grads[1], *early_x)
    )
    messages[0][2] = early_x
    l_keep, last, *sends = call(
        functools.partial(late_kernel, count, per, late_slots),
        [((per, piece, 3 * cw + n), BF), ((samples, rw), BF)] + [message] * 3 + [short],
        info, last1, last2, m2, m3, ow, far, chunk, held, held_chunk,
        cost=LAST_COST,
    )
    sent = reduce(sends, l_keep, per, per, parts + [(0, False, 0)])

    c_keep, send = call(
        functools.partial(early_chunk_kernel, per, place),
        [short, short],
        info, early, after(chunk, *sent),
    )
    reduce([send], c_keep, 0, per, [(0, False, 0)])

    for j in (1, 2):
        n = widths[j]
        (right,) = call(
            functools.partial(weigh_kernel, cuts[j]),
            [((samples, n), BF)],
            far, wide, far_grads[j],
            cost=WEIGH_COSTS[j],
        )
        send, keep = call(
            functools.partial(chunk_kernel, per, place),
            [((2 * per, n, piece), BF)] * 2,
            info, early, second, last, after(right, *sent),
        )
        sent = reduce([send], keep, 0, 2 * per, None)

    tail = messages[-2:]
    messages[0][0] = after(messages[0][0], *sent)
    flat, shapes = [], []
    for k, g, o, *what in messages[:-2]:
        flat += [k, *g, *o]
        shapes.append((len(g), len(o), *what))
    ham, corr = call(
        functools.partial(gather_kernel, count, shapes),
        [((piece, 2 * cw), F32)] * 2,
        info, *flat,
        cost=GATHER_COST,
    )
    return last_chunks(count, cuts[1], info, ham, tail), corr


def solution(mesh):
    in_specs = (
        P("walker", ("prow", "pcol")),
        P("walker", ("pcol", "prow")),
        P("walker", ("pcol", "prow")),
        P("walker"),
    )
    out_specs = (P(("prow", "walker"), "pcol"), P(("prow", "walker"), "pcol"))

    def per(*args):
        return tuple(per_device(*args))

    return jax.shard_map(
        per, mesh=mesh, in_specs=in_specs, out_specs=out_specs, check_vma=False
    )
```

time: 142 us -> 116 us (0.82)
  waiting for transfers between devices: 55.5 us -> 27.9 us
  starting transfers between devices: 30.3 us -> 37.4 us
  Pallas kernels: 33.5 us -> 29.5 us
  local copies, waits for them, and re-layouts: 15.1 us -> 13.4 us
    ppermute x13 -> x19, waiting for transfers between devices: 28.1 us -> 15 us  [the longest x2 5.19 us: per_device(): far_grads += [lax.ppermute(g, 'prow', flip) for g in grads[1:]]]
    ppermute x1, waiting for transfers between devices: 8.48 us -> 0.01 us  [per_device(): last2 = lax.ppermute(last1, 'pcol', ends)]
    ppermute x13 -> x19, starting transfers between devices: 12.2 us -> 20.2 us  [the longest x6 10.7 us: reduce(): lax.ppermute(s, 'walker', shift(i // len(shapes) + 1, first, pieces))]
    pallas_call x13 -> x19, Pallas kernels: 33.5 us -> 28.1 us  [call(): pl.pallas_call(kernel, out_shape=[jax.ShapeDtypeStruct(s, d) for s, d in...]
    ppermute x1, waiting for transfers between devices: 15.7 us -> 11.4 us  [per_device(): far_sums = lax.ppermute(m0, 'prow', flip)]
    unnamed x28, local copies, waits for them, and re-layouts: 14 us -> 11.2 us
    ppermute x1, waiting for transfers between devices: 1.72 us -> 0.01 us  [per_device(): m3 = lax.ppermute(m0, 'pcol', [(0, 3), (1, 2), (2, 1), (3, 0)])]
    ppermute x1, starting transfers between devices: 1.52 us -> 3.03 us  [per_device(): far_raw = lax.ppermute(o_cols, 'prow', flip)]
  transfers between devices with their start and end apart: 23 -> 29, of which waited for: 11 -> 12; matrix products, arithmetic and copies ran while one was open for 1% -> 2% of each run, Pallas kernels for 22% -> 24%
where the time goes in v2:
time: 116 us; the launch traced here: 115 us
  starting transfers between devices  37.4 us (32%)
  Pallas kernels  29.5 us (25%)
  waiting for transfers between devices  27.9 us (24%)
  local copies, waits for them, and re-layouts  13.4 us (12%)
  blocking collectives  6.27 us (5%)
    pallas_call x19, Pallas kernels, call(): pl.pallas_call(kernel, out_shape=[jax.ShapeDtypeStruct(s, d) for s, d in...  28.1 us
    ppermute x1, waiting for transfers between devices, per_device(): far_sums = lax.ppermute(m0, 'prow', flip)  11.4 us
    unnamed x28, local copies, waits for them, and re-layouts  11.2 us
    ppermute x6, starting transfers between devices, reduce(): lax.ppermute(s, 'walker', shift(i // len(shapes) + 1, first, pieces))  10.7 us
    psum x1, blocking collectives, per_device(): m0 = lax.psum(sums, 'walker')  6.27 us
    ppermute x2, waiting for transfers between devices, per_device(): far_grads += [lax.ppermute(g, 'prow', flip) for g in grads[1:]]  5.19 us
    ppermute x6, waiting for transfers between devices, reduce(): lax.ppermute(s, 'walker', shift(i // len(shapes) + 1, first, pieces))  4.74 us
    ppermute x10, starting transfers between devices, reduce(): gots = [lax.ppermute(send, 'walker', other_core) for send in sends]  4.54 us
  transfers between devices with their start and end apart: 29, of which 12 were waited for; matrix products, arithmetic and copies ran while one was open for 2% of the time, Pallas kernels for 24%

profile of v2, /device:TPU:0, one launch (start us, length us, event | category | flops | bytes accessed | tf_op | source)
XLA Modules:
  0.0 115.3 jit_solution(9902502392250019291)
XLA Ops:
  0.6 3.0 %collective-permute-start.6 = (bf16[2048,512]{1,0:T(8,128)(2,1)}, bf16[2048,512]{1,0:T(8,128)(2,1)}, u32[]{:S(2)}, u32[]{:S(2)}) collective-permute-start(bf16[2048,512]{1,0:T(8,128)(2,1)} %cols.3), channel_id=1, source_target_pairs={{0,4},{4,0},{1,5},{5,1},{2,6},{6,2},{3,7},{7,3},{8,12},{12,8},{9,1... | collective-permute-start | bytes 6291464 | tf_op jit(solution)/shard_map/ppermute | solution.py:341
  3.7 1.7 %collective-permute-start.1 = (bf16[2048,256]{1,0:T(8,128)(2,1)}, bf16[2048,256]{1,0:T(8,128)(2,1)}, u32[]{:S(2)}, u32[]{:S(2)}) collective-permute-start(bf16[2048,256]{1,0:T(8,128)(2,1)} %own_rows.3), channel_id=1, source_target_pairs={{1,2},{2,1},{5,6},{6,5},{9,10},{10,9},{13,14},{14,13},{17,18},{18,... | collective-permute-start | bytes 3145736 | tf_op jit(solution)/shard_map/ppermute | solution.py:343
  5.4 3.4 %collective-permute-start = (bf16[2048,256]{1,0:T(8,128)(2,1)}, bf16[2048,256]{1,0:T(8,128)(2,1)}, u32[]{:S(2)}, u32[]{:S(2)}) collective-permute-start(bf16[2048,256]{1,0:T(8,128)(2,1)} %own_rows.3), channel_id=1, source_target_pairs={{0,1},{1,0},{2,3},{3,2},{4,5},{5,4},{6,7},{7,6},{8,9},{9,8},{10,11... | collective-permute-start | bytes 3145736 | tf_op jit(solution)/shard_map/ppermute | solution.py:342
  8.8 1.3 %copy-done.2 = bf16[2048,256]{1,0:T(8,128)(2,1)S(1)} copy-done((bf16[2048,256]{1,0:T(8,128)(2,1)S(1)}, bf16[2048,256]{1,0:T(8,128)(2,1)}, u32[]{:S(2)}) %copy-start.2) | copy-done | bytes 1048600
  10.0 1.6 %copy-done.4 = bf16[2048,512]{1,0:T(8,128)(2,1)S(1)} copy-done((bf16[2048,512]{1,0:T(8,128)(2,1)S(1)}, bf16[2048,512]{1,0:T(8,128)(2,1)}, u32[]{:S(2)}) %copy-start.4) | copy-done | bytes 2097176
  11.6 0.5 shard_map.68
  12.2 6.3 %psum.7.sums.m0 = f32[1,768]{1,0:T(1,128)S(1)} all-reduce(f32[1,768]{1,0:T(1,128)S(1)} %shard_map.68), channel_id=1, replica_groups=mesh['walker'=4,'prow'=2,'pcol'=4] {'walker'}, use_global_device_ids=true, to_apply=%region_0.1 | all-reduce | flops 768 | bytes 6144 | tf_op jit(solution)/shard_map/psum | solution.py:346
  18.5 1.1 collective-permute-start.3
  19.5 0.9 collective-permute-start.2
  20.4 1.3 %copy.8.energy = f32[2048,1]{1,0:T(8,128)} copy(f32[2048,1]{0,1:T(1,128)S(1)} %bitcast.7) | data formatting | bytes 16384 | tf_op jit(solution)/shard_map/broadcast_in_dim | solution.py:350
  21.8 1.2 %copy-done.6 = f32[2048,1]{1,0:T(8,128)S(1)} copy-done((f32[2048,1]{1,0:T(8,128)S(1)}, f32[2048,1]{1,0:T(8,128)}, u32[]{:S(2)}) %copy-start.6) | copy-done | bytes 8216
  23.0 1.6 %copy-done.7 = bf16[2048,512]{1,0:T(8,128)(2,1)S(1)} copy-done((bf16[2048,512]{1,0:T(8,128)(2,1)S(1)}, bf16[2048,512]{1,0:T(8,128)(2,1)}, u32[]{:S(2)}) %copy-start.7) | copy-done | bytes 2097176
  24.6 1.3 %shard_map.69 = (bf16[2048,1024]{1,0:T(8,128)(2,1)S(1)}, f32[2048,128]{1,0:T(8,128)S(1)}, bf16[2048,256]{1,0:T(8,128)(2,1)S(1)}, bf16[2048,128]{1,0:T(8,128)(2,1)S(1)}, bf16[2048,128]{1,0:T(8,128)(2,1)S(1)}) custom-call(bf16[2048,512]{1,0:T(8,128)(2,1)S(1)} %copy-done.5, bf16[2048,512]{1,0:T(8,128)(2,1)S(1)} %copy-done.7, f32[2048,1]{1,0:T(8,128)S(1)} %copy-done.6, ...), custom_call_target="tpu_custom_call" | custom-call | tf_op jit(solution)/shard_map/pallas_call | solution.py:20
  25.9 1.9 %copy-done = bf16[2048,1024]{1,0:T(8,128)(2,1)} copy-done((bf16[2048,1024]{1,0:T(8,128)(2,1)}, bf16[2048,1024]{1,0:T(8,128)(2,1)S(1)}, u32[]{:S(2)}) %copy-start) | copy-done | bytes 4194328
  27.9 1.0 copy-done.8
  28.8 0.8 copy-done.9
  29.6 0.8 copy-done.11
  30.4 1.2 %collective-permute-done.3.m2 = f32[1,768]{1,0:T(1,128)S(1)} collective-permute-done((f32[1,768]{1,0:T(1,128)S(1)}, f32[1,768]{1,0:T(1,128)S(1)}, u32[]{:S(2)}, u32[]{:S(2)}) %collective-permute-start.3) | collective-permute-done | bytes 3104 | tf_op jit(solution)/shard_map/ppermute | solution.py:348
  31.6 0.2 collective-permute-done.2.m1
  31.8 0.5 collective-permute-start.7
  32.3 1.3 %collective-permute-start.4 = (bf16[2048,256]{1,0:T(8,128)(2,1)}, bf16[2048,256]{1,0:T(8,128)(2,1)S(1)}, u32[]{:S(2)}, u32[]{:S(2)}) collective-permute-start(bf16[2048,256]{1,0:T(8,128)(2,1)} %collective-permute-done.1.mid1), channel_id=1, source_target_pairs={{1,0},{2,3},{5,4},{6,7},{9,8},{10,11},{13,12},{14,15},{17,16},{18,... | collective-permute-start | bytes 3145736 | tf_op jit(solution)/shard_map/ppermute | solution.py:365
  33.6 1.6 %collective-permute-start.5 = (bf16[2048,256]{1,0:T(8,128)(2,1)}, bf16[2048,256]{1,0:T(8,128)(2,1)}, u32[]{:S(2)}, u32[]{:S(2)}) collective-permute-start(bf16[2048,256]{1,0:T(8,128)(2,1)} %collective-permute-done.near), channel_id=1, source_target_pairs={{1,2},{2,1},{5,6},{6,5},{9,10},{10,9},{13,14},{14,13},{17,18},{18,... | collective-permute-start | bytes 3145736 | tf_op jit(solution)/shard_map/ppermute | solution.py:366
  35.2 0.7 dynamic-slice_bitcast_fusion
  36.0 2.2 %collective-permute-start.8 = (f32[1,768]{1,0:T(1,128)S(1)}, f32[1,768]{1,0:T(1,128)S(1)}, u32[]{:S(2)}, u32[]{:S(2)}) collective-permute-start(f32[1,768]{1,0:T(1,128)S(1)} %psum.7.sums.m0), channel_id=1, source_target_pairs={{0,3},{1,2},{2,1},{3,0},{4,7},{5,6},{6,5},{7,4},{8,11},{9,10},{10,... | collective-permute-start | bytes 9224 | tf_op jit(solution)/shard_map/ppermute | solution.py:363
  38.2 11.4 %collective-permute-done.7.sums = f32[1,768]{1,0:T(1,128)S(1)} collective-permute-done((f32[1,768]{1,0:T(1,128)S(1)}, f32[1,768]{1,0:T(1,128)S(1)}, u32[]{:S(2)}, u32[]{:S(2)}) %collective-permute-start.7) | collective-permute-done | bytes 3104 | tf_op jit(solution)/shard_map/ppermute | solution.py:364
  49.6 1.7 %collective-permute-start.10 = (bf16[2048,256]{1,0:T(8,128)(2,1)}, bf16[2048,256]{1,0:T(8,128)(2,1)S(1)}, u32[]{:S(2)}, u32[]{:S(2)}) collective-permute-start(bf16[2048,256]{1,0:T(8,128)(2,1)} %copy-done.8), channel_id=1, source_target_pairs={{0,4},{4,0},{1,5},{5,1},{2,6},{6,2},{3,7},{7,3},{8,12},{12,8},{9,1... | collective-permute-start | bytes 3145736 | tf_op jit(solution)/shard_map/ppermute | solution.py:367
  51.4 2.1 %shard_map.71.far = bf16[2048,512]{1,0:T(8,128)(2,1)S(1)} custom-call(bf16[2048,512]{1,0:T(8,128)(2,1)} %collective-permute-done.6.raw, f32[1,512]{1,0:T(1,128)S(1)} %shard_map.70.mean), custom_call_target="tpu_custom_call" | custom-call | flops 3449999872 | tf_op jit(solution)/shard_map/pallas_call | solution.py:20
  53.5 1.0 copy-done.1
  54.5 3.3 %shard_map.72 = (bf16[2048,256]{1,0:T(8,128)(2,1)S(1)}, bf16[256,1536]{1,0:T(8,128)(2,1)S(1)}) custom-call(s32[6]{0:T(128)S(1)} %concatenate.3.info, bf16[2048,256]{1,0:T(8,128)(2,1)S(1)} %copy-done.3, bf16[2048,256]{1,0:T(8,128)(2,1)} %collective-permute-done.near, f32[1,768]{1,0:T(1,128)S(1)} %psum.7.sums.m0, f32[1,768]{1,0:T(1,128)S(1)} %collective-permute-done.2.m1, ...), custom_call_target="tpu_custom_call" | custom-call | tf_op jit(solution)/shard_map/pallas_call | solution.py:20
  57.9 1.4 %collective-permute-start.9 = (bf16[2048,256]{1,0:T(8,128)(2,1)}, bf16[2048,256]{1,0:T(8,128)(2,1)S(1)}, u32[]{:S(2)}, u32[]{:S(2)}) collective-permute-start(bf16[2048,256]{1,0:T(8,128)(2,1)} %collective-permute-done.5.last1), channel_id=1, source_target_pairs={{1,0},{2,3},{5,4},{6,7},{9,8},{10,11},{13,12},{14,15},{17,16},{18,... | collective-permute-start | bytes 3145736 | tf_op jit(solution)/shard_map/ppermute | solution.py:381
  59.3 5.9 %shard_map.73 = (bf16[1,256,1536]{2,1,0:T(8,128)(2,1)S(1)}, bf16[2048,512]{1,0:T(8,128)(2,1)S(1)}, bf16[1,256,512]{2,1,0:T(8,128)(2,1)S(1)}, bf16[1,256,512]{2,1,0:T(8,128)(2,1)S(1)}, bf16[1,256,512]{2,1,0:T(8,128)(2,1)S(1)}) custom-call(s32[6]{0:T(128)S(1)} %concatenate.3.info, bf16[2048,256]{1,0:T(8,128)(2,1)S(1)} %copy-done.3, ...), custom_call_target="tpu_custom_call" | custom-call | tf_op jit(solution)/shard_map/pallas_call | solution.py:20
  65.3 0.5 collective-permute-start.13
  65.9 0.9 collective-permute-done.12.refs_0_.refs_1_
  66.9 1.5 %collective-permute-start.11 = (bf16[2048,128]{1,0:T(8,128)(2,1)S(1)}, bf16[2048,128]{1,0:T(8,128)(2,1)S(1)}, u32[]{:S(2)}, u32[]{:S(2)}) collective-permute-start(bf16[2048,128]{1,0:T(8,128)(2,1)S(1)} %copy-done.12), channel_id=1, source_target_pairs={{0,4},{4,0},{1,5},{5,1},{2,6},{6,2},{3,7},{7,3},{8,12},{12,8},{9,1... | collective-permute-start | bytes 1572872 | tf_op jit(solution)/shard_map/ppermute | solution.py:382
  68.4 0.7 shard_map.75
  69.1 3.4 %collective-permute-start.15 = (bf16[256,1024]{1,0:T(8,128)(2,1)S(1)}, bf16[256,1024]{1,0:T(8,128)(2,1)S(1)}, u32[]{:S(2)}, u32[]{:S(2)}) collective-permute-start(bf16[256,1024]{1,0:T(8,128)(2,1)S(1)} %get-tuple-element.88), channel_id=1, source_target_pairs={{0,16},{24,8},{1,17},{25,9},{2,18},{26,10},{3,19},{27,11},{4,20},{... | collective-permute-start | bytes 1572872 | tf_op jit(solution)/shard_map/ppermute | solution.py:397
  72.5 1.3 %collective-permute-start.16 = (bf16[256,512]{1,0:T(8,128)(2,1)S(1)}, bf16[256,512]{1,0:T(8,128)(2,1)S(1)}, u32[]{:S(2)}, u32[]{:S(2)}) collective-permute-start(bf16[256,512]{1,0:T(8,128)(2,1)S(1)} %get-tuple-element.89), channel_id=1, source_target_pairs={{0,16},{24,8},{1,17},{25,9},{2,18},{26,10},{3,19},{27,11},{4,20},{... | collective-permute-start | bytes 786440 | tf_op jit(solution)/shard_map/ppermute | solution.py:397
  73.9 2.1 %collective-permute-done.10.grads = bf16[2048,256]{1,0:T(8,128)(2,1)S(1)} collective-permute-done((bf16[2048,256]{1,0:T(8,128)(2,1)}, bf16[2048,256]{1,0:T(8,128)(2,1)S(1)}, u32[]{:S(2)}, u32[]{:S(2)}) %collective-permute-start.10) | collective-permute-done | bytes 1048608 | tf_op jit(solution)/shard_map/ppermute | solution.py:367
  76.0 1.7 %collective-permute-start.17 = (bf16[2048,128]{1,0:T(8,128)(2,1)S(1)}, bf16[2048,128]{1,0:T(8,128)(2,1)S(1)}, u32[]{:S(2)}, u32[]{:S(2)}) collective-permute-start(bf16[2048,128]{1,0:T(8,128)(2,1)S(1)} %copy-done.10), channel_id=1, source_target_pairs={{0,4},{4,0},{1,5},{5,1},{2,6},{6,2},{3,7},{7,3},{8,12},{12,8},{9,1... | collective-permute-start | bytes 1572872 | tf_op jit(solution)/shard_map/ppermute | solution.py:382
  77.7 0.7 shard_map.74
  78.4 3.6 %collective-permute-done.16.refs_5_ = bf16[256,512]{1,0:T(8,128)(2,1)S(1)} collective-permute-done((bf16[256,512]{1,0:T(8,128)(2,1)S(1)}, bf16[256,512]{1,0:T(8,128)(2,1)S(1)}, u32[]{:S(2)}, u32[]{:S(2)}) %collective-permute-start.16) | collective-permute-done | bytes 262176 | tf_op jit(solution)/shard_map/ppermute | solution.py:397
  82.0 5.2 %collective-permute-done.11.grads = bf16[2048,128]{1,0:T(8,128)(2,1)S(1)} collective-permute-done((bf16[2048,128]{1,0:T(8,128)(2,1)S(1)}, bf16[2048,128]{1,0:T(8,128)(2,1)S(1)}, u32[]{:S(2)}, u32[]{:S(2)}) %collective-permute-start.11) | collective-permute-done | bytes 524320 | tf_op jit(solution)/shard_map/ppermute | solution.py:382
  87.2 3.9 %shard_map.76 = (bf16[1,256,1792]{2,1,0:T(8,128)(2,1)S(1)}, bf16[2048,256]{1,0:T(8,128)(2,1)S(1)}, bf16[1,256,512]{2,1,0:T(8,128)(2,1)S(1)}, bf16[1,256,512]{2,1...) custom-call(s32[6]{0:T(128)S(1)} %concatenate.3.info, ...), custom_call_target="tpu_custom_call" | custom-call | flops 4600000000 | tf_op jit(solution)/shard_map/pallas_call | solution.py:20
  91.2 0.5 collective-permute-start.19
  91.8 0.4 collective-permute-start.21
  92.2 0.2 shard_map.78.right_ref
  92.4 1.3 %collective-permute-done.21.refs_3_.refs_10_ = bf16[1,256,256]{2,1,0:T(8,128)(2,1)S(1)} collective-permute-done((bf16[1,256,256]{2,1,0:T(8,128)(2,1)S(1)}, bf16[1,256,256]{2,1,0:T(8,128)(2,1)S(1)}, u32[]{:S(2)}, u32[]{:S(2)}) %collective-permute-start.21) | collective-permute-done | bytes 131104 | tf_op jit(solution)/shard_map/ppermute | solution.py:389
  93.7 0.8 shard_map.79
  94.4 1.3 %collective-permute-start.24 = (bf16[256,1792]{1,0:T(8,128)(2,1)S(1)}, bf16[256,1792]{1,0:T(8,128)(2,1)S(1)}, u32[]{:S(2)}, u32[]{:S(2)}) collective-permute-start(bf16[256,1792]{1,0:T(8,128)(2,1)S(1)} %shard_map.79), channel_id=1, source_target_pairs={{8,24},{16,0},{9,25},{17,1},{10,26},{18,2},{11,27},{19,3},{12,28},... | collective-permute-start | bytes 2752520 | tf_op jit(solution)/shard_map/ppermute | solution.py:397
  95.7 1.3 %shard_map.84 = (bf16[1,256,256]{2,1,0:T(8,128)(2,1)S(1)}, bf16[1,256,256]{2,1,0:T(8,128)(2,1)S(1)}) custom-call(s32[6]{0:T(128)S(1)} %concatenate.3.info, bf16[2048,512]{1,0:T(8,128)(2,1)S(1)} %get-tuple-element.78.early, bf16[2048,256]{1,0:T(8,128)(2,1)S(1)} %get-tuple-element.111.chunk.right), custom_call_target="tpu_custom_call" | custom-call | tf_op jit(solution)/shard_map/pallas_call | solution.py:20
  97.1 1.5 %shard_map.80 = (bf16[2,128,256]{2,1,0:T(8,128)(2,1)S(1)}, bf16[2,128,256]{2,1,0:T(8,128)(2,1)S(1)}) custom-call(s32[6]{0:T(128)S(1)} %concatenate.3.info, bf16[2048,512]{1,0:T(8,128)(2,1)S(1)} %get-tuple-element.78.early, bf16[2048,256]{1,0:T(8,128)(2,1)S(1)} %get-tuple-element.79.second, bf16[2048,256]{1,0:T(8,128)(2,1)S(1)} %get-tuple-element.94.last, ...), custom_call_target="tpu_custom_call" | custom-call | tf_op jit(solution)/shard_map/pallas_call | solution.py:20
  98.6 2.3 %collective-permute-start.22 = (bf16[2,128,256]{2,1,0:T(8,128)(2,1)S(1)}, bf16[2,128,256]{2,1,0:T(8,128)(2,1)S(1)}, u32[]{:S(2)}, u32[]{:S(2)}) collective-permute-start(bf16[2,128,256]{2,1,0:T(8,128)(2,1)S(1)} %get-tuple-element.104), channel_id=1, source_target_pairs={{0,8},{8,0},{16,24},{24,16},{1,9},{9,1},{17,25},{25,17},{2,10},{10... | collective-permute-start | bytes 393224 | tf_op jit(solution)/shard_map/ppermute | solution.py:389
  101.2 0.7 collective-permute-done.22.refs_0_.refs_1_
  101.9 0.6 shard_map.81
  102.5 1.5 %shard_map.82 = (bf16[2,128,256]{2,1,0:T(8,128)(2,1)S(1)}, bf16[2,128,256]{2,1,0:T(8,128)(2,1)S(1)}) custom-call(s32[6]{0:T(128)S(1)} %concatenate.3.info, bf16[2048,512]{1,0:T(8,128)(2,1)S(1)} %get-tuple-element.78.early, bf16[2048,256]{1,0:T(8,128)(2,1)S(1)} %get-tuple-element.79.second, bf16[2048,256]{1,0:T(8,128)(2,1)S(1)} %get-tuple-element.94.last, ...), custom_call_target="tpu_custom_call" | custom-call | tf_op jit(solution)/shard_map/pallas_call | solution.py:20
  104.0 0.4 collective-permute-start.23
  104.4 0.6 shard_map.85
  105.0 2.5 %collective-permute-start.26 = (bf16[256,256]{1,0:T(8,128)(2,1)S(1)}, bf16[256,256]{1,0:T(8,128)(2,1)S(1)}, u32[]{:S(2)}, u32[]{:S(2)}) collective-permute-start(bf16[256,256]{1,0:T(8,128)(2,1)S(1)} %shard_map.85), channel_id=1, source_target_pairs={{0,16},{24,8},{1,17},{25,9},{2,18},{26,10},{3,19},{27,11},{4,20},{... | collective-permute-start | bytes 393224 | tf_op jit(solution)/shard_map/ppermute | solution.py:397
  107.6 0.6 shard_map.83
  108.2 2.1 %collective-permute-start.28 = (bf16[128,256]{1,0:T(8,128)(2,1)S(1)}, bf16[128,256]{1,0:T(8,128)(2,1)S(1)}, u32[]{:S(2)}, u32[]{:S(2)}) collective-permute-start(bf16[128,256]{1,0:T(8,128)(2,1)S(1)} %shard_map.83), channel_id=1, source_target_pairs={{0,16},{8,24},{16,0},{24,8},{1,17},{9,25},{17,1},{25,9},{2,18},{10... | collective-permute-start | bytes 196616 | tf_op jit(solution)/shard_map/ppermute | solution.py:397
  110.3 0.8 collective-permute-done.26.refs_14_
  111.1 2.5 %shard_map.86 = (f32[256,1024]{1,0:T(8,128)}, f32[256,1024]{1,0:T(8,128)}) custom-call(s32[6]{0:T(128)S(1)} %concatenate.3.info, bf16[1,256,1536]{2,1,0:T(8,128)(2,1)S(1)} %get-tuple-element.108.keep.refs_0_, bf16[1,256,512]{2,1,0:T(8,128)(2,1)S(1)} %collective-permute-done.12.refs_0_.refs_1_, ...), custom_call_target="tpu_custom_call" | custom-call | flops 3449999872 | tf_op jit(solution)/shard_map/pallas_call | solution.py:20
  113.6 0.3 collective-permute-done.28.refs_5_
  113.9 1.4 %shard_map.87 = f32[256,1024]{1,0:T(8,128)} custom-call(s32[6]{0:T(128)S(1)} %concatenate.3.info, f32[256,1024]{1,0:T(8,128)} %get-tuple-element.114.held, bf16[2,128,256]{2,1,0:T(8,128)(2,1)S(1)} %get-tuple-element.103.keep.refs_0_, bf16[2,128,256]{2,1,0:T(8,128)(2,1)S(1)} %collective-permute-done.22.refs_0_.refs_1_, ...), custom_call_target="tpu_custom_call", output_to_operand_aliasing={{}: (1, {})} | custom-call | tf_op jit(solution)/shard_map/pallas_call | solution.py:291
  (46 shorter events, 0.9 us)
Async XLA Ops:
  0.6 50.8 %collective-permute-start.6 = (bf16[2048,512]{1,0:T(8,128)(2,1)}, bf16[2048,512]{1,0:T(8,128)(2,1)}, u32[]{:S(2)}, u32[]{:S(2)}) collective-permute-start(bf16[2048,512]{1,0:T(8,128)(2,1)} %cols.3), channel_id=1, source_target_pairs={{0,4},{4,0},{1,5},{5,1},{2,6},{6,2},{3,7},{7,3},{8,12},{12,8},{9,1... | collective-permute-start | bytes 6291464 | tf_op jit(solution)/shard_map/ppermute | solution.py:341
  3.7 28.1 %collective-permute-start.1 = (bf16[2048,256]{1,0:T(8,128)(2,1)}, bf16[2048,256]{1,0:T(8,128)(2,1)}, u32[]{:S(2)}, u32[]{:S(2)}) collective-permute-start(bf16[2048,256]{1,0:T(8,128)(2,1)} %own_rows.3), channel_id=1, source_target_pairs={{1,2},{2,1},{5,6},{6,5},{9,10},{10,9},{13,14},{14,13},{17,18},{18,... | collective-permute-start | bytes 3145736 | tf_op jit(solution)/shard_map/ppermute | solution.py:343
  5.4 26.5 %collective-permute-start = (bf16[2048,256]{1,0:T(8,128)(2,1)}, bf16[2048,256]{1,0:T(8,128)(2,1)}, u32[]{:S(2)}, u32[]{:S(2)}) collective-permute-start(bf16[2048,256]{1,0:T(8,128)(2,1)} %own_rows.3), channel_id=1, source_target_pairs={{0,1},{1,0},{2,3},{3,2},{4,5},{5,4},{6,7},{7,6},{8,9},{9,8},{10,11... | collective-permute-start | bytes 3145736 | tf_op jit(solution)/shard_map/ppermute | solution.py:342
  8.8 1.3 %copy-start.2 = (bf16[2048,256]{1,0:T(8,128)(2,1)S(1)}, bf16[2048,256]{1,0:T(8,128)(2,1)}, u32[]{:S(2)}) copy-start(bf16[2048,256]{1,0:T(8,128)(2,1)} %own_rows.3) | copy-start | bytes 3145732
  10.0 1.6 %copy-start.4 = (bf16[2048,512]{1,0:T(8,128)(2,1)S(1)}, bf16[2048,512]{1,0:T(8,128)(2,1)}, u32[]{:S(2)}) copy-start(bf16[2048,512]{1,0:T(8,128)(2,1)} %cols.3) | copy-start | bytes 6291460
  11.6 8.8 %copy-start.13 = (f32[2048]{0:T(1024)S(1)}, f32[2048]{0:T(1024)}, u32[]{:S(2)}) copy-start(f32[2048]{0:T(1024)} %param.8) | copy-start | bytes 24580
  11.6 10.1 %copy-start.5 = (bf16[2048,512]{1,0:T(8,128)(2,1)S(1)}, bf16[2048,512]{1,0:T(8,128)(2,1)}, u32[]{:S(2)}) copy-start(bf16[2048,512]{1,0:T(8,128)(2,1)} %cols.3) | copy-start | bytes 6291460
  18.5 13.1 %collective-permute-start.3 = (f32[1,768]{1,0:T(1,128)S(1)}, f32[1,768]{1,0:T(1,128)S(1)}, u32[]{:S(2)}, u32[]{:S(2)}) collective-permute-start(f32[1,768]{1,0:T(1,128)S(1)} %psum.7.sums.m0), channel_id=1, source_target_pairs={{0,2},{1,3},{2,0},{3,1},{4,6},{5,7},{6,4},{7,5},{8,10},{9,11},{10,... | collective-permute-start | bytes 9224 | tf_op jit(solution)/shard_map/ppermute | solution.py:348
  19.5 12.3 %collective-permute-start.2 = (f32[1,768]{1,0:T(1,128)S(1)}, f32[1,768]{1,0:T(1,128)S(1)}, u32[]{:S(2)}, u32[]{:S(2)}) collective-permute-start(f32[1,768]{1,0:T(1,128)S(1)} %psum.7.sums.m0), channel_id=1, source_target_pairs={{0,1},{1,0},{2,3},{3,2},{4,5},{5,4},{6,7},{7,6},{8,9},{9,8},{10,11... | collective-permute-start | bytes 9224 | tf_op jit(solution)/shard_map/ppermute | solution.py:347
  21.8 1.2 %copy-start.6 = (f32[2048,1]{1,0:T(8,128)S(1)}, f32[2048,1]{1,0:T(8,128)}, u32[]{:S(2)}) copy-start(f32[2048,1]{1,0:T(8,128)} %copy.8.energy) | copy-start | bytes 24580
  23.0 1.6 %copy-start.7 = (bf16[2048,512]{1,0:T(8,128)(2,1)S(1)}, bf16[2048,512]{1,0:T(8,128)(2,1)}, u32[]{:S(2)}) copy-start(bf16[2048,512]{1,0:T(8,128)(2,1)} %grads.1) | copy-start | bytes 6291460
  25.9 2.0 %copy-start = (bf16[2048,1024]{1,0:T(8,128)(2,1)}, bf16[2048,1024]{1,0:T(8,128)(2,1)S(1)}, u32[]{:S(2)}) copy-start(bf16[2048,1024]{1,0:T(8,128)(2,1)S(1)} %get-tuple-element.67.ow) | copy-start | bytes 12582916
  27.9 1.0 copy-start.8
  28.8 0.8 copy-start.9
  29.6 0.8 copy-start.11
  31.8 17.8 %collective-permute-start.7 = (f32[1,768]{1,0:T(1,128)S(1)}, f32[1,768]{1,0:T(1,128)S(1)}, u32[]{:S(2)}, u32[]{:S(2)}) collective-permute-start(f32[1,768]{1,0:T(1,128)S(1)} %psum.7.sums.m0), channel_id=1, source_target_pairs={{0,4},{4,0},{1,5},{5,1},{2,6},{6,2},{3,7},{7,3},{8,12},{12,8},{9,1... | collective-permute-start | bytes 9224 | tf_op jit(solution)/shard_map/ppermute | solution.py:364
  32.3 25.6 %collective-permute-start.4 = (bf16[2048,256]{1,0:T(8,128)(2,1)}, bf16[2048,256]{1,0:T(8,128)(2,1)S(1)}, u32[]{:S(2)}, u32[]{:S(2)}) collective-permute-start(bf16[2048,256]{1,0:T(8,128)(2,1)} %collective-permute-done.1.mid1), channel_id=1, source_target_pairs={{1,0},{2,3},{5,4},{6,7},{9,8},{10,11},{13,12},{14,15},{17,16},{18,... | collective-permute-start | bytes 3145736 | tf_op jit(solution)/shard_map/ppermute | solution.py:365
  33.6 24.3 %collective-permute-start.5 = (bf16[2048,256]{1,0:T(8,128)(2,1)}, bf16[2048,256]{1,0:T(8,128)(2,1)}, u32[]{:S(2)}, u32[]{:S(2)}) collective-permute-start(bf16[2048,256]{1,0:T(8,128)(2,1)} %collective-permute-done.near), channel_id=1, source_target_pairs={{1,2},{2,1},{5,6},{6,5},{9,10},{10,9},{13,14},{14,13},{17,18},{18,... | collective-permute-start | bytes 3145736 | tf_op jit(solution)/shard_map/ppermute | solution.py:366
  36.0 21.8 %collective-permute-start.8 = (f32[1,768]{1,0:T(1,128)S(1)}, f32[1,768]{1,0:T(1,128)S(1)}, u32[]{:S(2)}, u32[]{:S(2)}) collective-permute-start(f32[1,768]{1,0:T(1,128)S(1)} %psum.7.sums.m0), channel_id=1, source_target_pairs={{0,3},{1,2},{2,1},{3,0},{4,7},{5,6},{6,5},{7,4},{8,11},{9,10},{10,... | collective-permute-start | bytes 9224 | tf_op jit(solution)/shard_map/ppermute | solution.py:363
  49.6 26.3 %collective-permute-start.10 = (bf16[2048,256]{1,0:T(8,128)(2,1)}, bf16[2048,256]{1,0:T(8,128)(2,1)S(1)}, u32[]{:S(2)}, u32[]{:S(2)}) collective-permute-start(bf16[2048,256]{1,0:T(8,128)(2,1)} %copy-done.8), channel_id=1, source_target_pairs={{0,4},{4,0},{1,5},{5,1},{2,6},{6,2},{3,7},{7,3},{8,12},{12,8},{9,1... | collective-permute-start | bytes 3145736 | tf_op jit(solution)/shard_map/ppermute | solution.py:367
  51.4 2.1 %copy-start.3 = (bf16[2048,256]{1,0:T(8,128)(2,1)S(1)}, bf16[2048,256]{1,0:T(8,128)(2,1)}, u32[]{:S(2)}) copy-start(bf16[2048,256]{1,0:T(8,128)(2,1)} %own_rows.3) | copy-start | bytes 3145732
  51.4 3.1 %copy-start.1 = (bf16[2048,1024]{1,0:T(8,128)(2,1)S(1)}, bf16[2048,1024]{1,0:T(8,128)(2,1)}, u32[]{:S(2)}) copy-start(bf16[2048,1024]{1,0:T(8,128)(2,1)} %copy-done) | copy-start | bytes 12582916
  57.9 8.9 %copy-start.12 = (bf16[2048,128]{1,0:T(8,128)(2,1)S(1)}, bf16[2048,128]{1,0:T(8,128)(2,1)}, u32[]{:S(2)}) copy-start(bf16[2048,128]{1,0:T(8,128)(2,1)} %copy-done.11) | copy-start | bytes 1572868
  57.9 18.0 %copy-start.10 = (bf16[2048,128]{1,0:T(8,128)(2,1)S(1)}, bf16[2048,128]{1,0:T(8,128)(2,1)}, u32[]{:S(2)}) copy-start(bf16[2048,128]{1,0:T(8,128)(2,1)} %copy-done.9) | copy-start | bytes 1572868
  57.9 29.3 %collective-permute-start.9 = (bf16[2048,256]{1,0:T(8,128)(2,1)}, bf16[2048,256]{1,0:T(8,128)(2,1)S(1)}, u32[]{:S(2)}, u32[]{:S(2)}) collective-permute-start(bf16[2048,256]{1,0:T(8,128)(2,1)} %collective-permute-done.5.last1), channel_id=1, source_target_pairs={{1,0},{2,3},{5,4},{6,7},{9,8},{10,11},{13,12},{14,15},{17,16},{18,... | collective-permute-start | bytes 3145736 | tf_op jit(solution)/shard_map/ppermute | solution.py:381
  65.2 1.6 %collective-permute-start.12 = (bf16[1,256,512]{2,1,0:T(8,128)(2,1)S(1)}, bf16[1,256,512]{2,1,0:T(8,128)(2,1)S(1)}, u32[]{:S(2)}, u32[]{:S(2)}) collective-permute-start(bf16[1,256,512]{2,1,0:T(8,128)(2,1)S(1)} %get-tuple-element.85), channel_id=1, source_target_pairs={{0,8},{8,0},{16,24},{24,16},{1,9},{9,1},{17,25},{25,17},{2,10},{10... | collective-permute-start | bytes 786440 | tf_op jit(solution)/shard_map/ppermute | solution.py:389
  65.3 3.0 %collective-permute-start.13 = (bf16[1,256,512]{2,1,0:T(8,128)(2,1)S(1)}, bf16[1,256,512]{2,1,0:T(8,128)(2,1)S(1)}, u32[]{:S(2)}, u32[]{:S(2)}) collective-permute-start(bf16[1,256,512]{2,1,0:T(8,128)(2,1)S(1)} %get-tuple-element.86), channel_id=1, source_target_pairs={{0,8},{8,0},{16,24},{24,16},{1,9},{9,1},{17,25},{25,17},{2,10},{10... | collective-permute-start | bytes 786440 | tf_op jit(solution)/shard_map/ppermute | solution.py:389
  65.8 2.5 %collective-permute-start.14 = (bf16[1,256,512]{2,1,0:T(8,128)(2,1)S(1)}, bf16[1,256,512]{2,1,0:T(8,128)(2,1)S(1)}, u32[]{:S(2)}, u32[]{:S(2)}) collective-permute-start(bf16[1,256,512]{2,1,0:T(8,128)(2,1)S(1)} %get-tuple-element.87), channel_id=1, source_target_pairs={{0,8},{8,0},{16,24},{24,16},{1,9},{9,1},{17,25},{25,17},{2,10},{10... | collective-permute-start | bytes 786440 | tf_op jit(solution)/shard_map/ppermute | solution.py:389
  66.9 20.3 %collective-permute-start.11 = (bf16[2048,128]{1,0:T(8,128)(2,1)S(1)}, bf16[2048,128]{1,0:T(8,128)(2,1)S(1)}, u32[]{:S(2)}, u32[]{:S(2)}) collective-permute-start(bf16[2048,128]{1,0:T(8,128)(2,1)S(1)} %copy-done.12), channel_id=1, source_target_pairs={{0,4},{4,0},{1,5},{5,1},{2,6},{6,2},{3,7},{7,3},{8,12},{12,8},{9,1... | collective-permute-start | bytes 1572872 | tf_op jit(solution)/shard_map/ppermute | solution.py:382
  69.1 18.1 %collective-permute-start.15 = (bf16[256,1024]{1,0:T(8,128)(2,1)S(1)}, bf16[256,1024]{1,0:T(8,128)(2,1)S(1)}, u32[]{:S(2)}, u32[]{:S(2)}) collective-permute-start(bf16[256,1024]{1,0:T(8,128)(2,1)S(1)} %get-tuple-element.88), channel_id=1, source_target_pairs={{0,16},{24,8},{1,17},{25,9},{2,18},{26,10},{3,19},{27,11},{4,20},{... | collective-permute-start | bytes 1572872 | tf_op jit(solution)/shard_map/ppermute | solution.py:397
  72.5 9.5 %collective-permute-start.16 = (bf16[256,512]{1,0:T(8,128)(2,1)S(1)}, bf16[256,512]{1,0:T(8,128)(2,1)S(1)}, u32[]{:S(2)}, u32[]{:S(2)}) collective-permute-start(bf16[256,512]{1,0:T(8,128)(2,1)S(1)} %get-tuple-element.89), channel_id=1, source_target_pairs={{0,16},{24,8},{1,17},{25,9},{2,18},{26,10},{3,19},{27,11},{4,20},{... | collective-permute-start | bytes 786440 | tf_op jit(solution)/shard_map/ppermute | solution.py:397
  76.0 25.0 %collective-permute-start.17 = (bf16[2048,128]{1,0:T(8,128)(2,1)S(1)}, bf16[2048,128]{1,0:T(8,128)(2,1)S(1)}, u32[]{:S(2)}, u32[]{:S(2)}) collective-permute-start(bf16[2048,128]{1,0:T(8,128)(2,1)S(1)} %copy-done.10), channel_id=1, source_target_pairs={{0,4},{4,0},{1,5},{5,1},{2,6},{6,2},{3,7},{7,3},{8,12},{12,8},{9,1... | collective-permute-start | bytes 1572872 | tf_op jit(solution)/shard_map/ppermute | solution.py:382
  91.1 2.5 %collective-permute-start.18 = (bf16[1,256,512]{2,1,0:T(8,128)(2,1)S(1)}, bf16[1,256,512]{2,1,0:T(8,128)(2,1)S(1)}, u32[]{:S(2)}, u32[]{:S(2)}) collective-permute-start(bf16[1,256,512]{2,1,0:T(8,128)(2,1)S(1)} %get-tuple-element.98), channel_id=1, source_target_pairs={{0,8},{8,0},{16,24},{24,16},{1,9},{9,1},{17,25},{25,17},{2,10},{10... | collective-permute-start | bytes 786440 | tf_op jit(solution)/shard_map/ppermute | solution.py:389
  91.2 2.5 %collective-permute-start.19 = (bf16[1,256,512]{2,1,0:T(8,128)(2,1)S(1)}, bf16[1,256,512]{2,1,0:T(8,128)(2,1)S(1)}, u32[]{:S(2)}, u32[]{:S(2)}) collective-permute-start(bf16[1,256,512]{2,1,0:T(8,128)(2,1)S(1)} %get-tuple-element.99), channel_id=1, source_target_pairs={{0,8},{8,0},{16,24},{24,16},{1,9},{9,1},{17,25},{25,17},{2,10},{10... | collective-permute-start | bytes 786440 | tf_op jit(solution)/shard_map/ppermute | solution.py:389
  91.7 2.0 %collective-permute-start.20 = (bf16[1,256,512]{2,1,0:T(8,128)(2,1)S(1)}, bf16[1,256,512]{2,1,0:T(8,128)(2,1)S(1)}, u32[]{:S(2)}, u32[]{:S(2)}) collective-permute-start(bf16[1,256,512]{2,1,0:T(8,128)(2,1)S(1)} %get-tuple-element.100), channel_id=1, source_target_pairs={{0,8},{8,0},{16,24},{24,16},{1,9},{9,1},{17,25},{25,17},{2,10},{10... | collective-permute-start | bytes 786440 | tf_op jit(solution)/shard_map/ppermute | solution.py:389
  91.8 1.9 %collective-permute-start.21 = (bf16[1,256,256]{2,1,0:T(8,128)(2,1)S(1)}, bf16[1,256,256]{2,1,0:T(8,128)(2,1)S(1)}, u32[]{:S(2)}, u32[]{:S(2)}) collective-permute-start(bf16[1,256,256]{2,1,0:T(8,128)(2,1)S(1)} %get-tuple-element.101), channel_id=1, source_target_pairs={{0,8},{8,0},{16,24},{24,16},{1,9},{9,1},{17,25},{25,17},{2,10},{10... | collective-permute-start | bytes 393224 | tf_op jit(solution)/shard_map/ppermute | solution.py:389
  94.4 16.7 %collective-permute-start.24 = (bf16[256,1792]{1,0:T(8,128)(2,1)S(1)}, bf16[256,1792]{1,0:T(8,128)(2,1)S(1)}, u32[]{:S(2)}, u32[]{:S(2)}) collective-permute-start(bf16[256,1792]{1,0:T(8,128)(2,1)S(1)} %shard_map.79), channel_id=1, source_target_pairs={{8,24},{16,0},{9,25},{17,1},{10,26},{18,2},{11,27},{19,3},{12,28},... | collective-permute-start | bytes 2752520 | tf_op jit(solution)/shard_map/ppermute | solution.py:397
  98.6 3.3 %collective-permute-start.22 = (bf16[2,128,256]{2,1,0:T(8,128)(2,1)S(1)}, bf16[2,128,256]{2,1,0:T(8,128)(2,1)S(1)}, u32[]{:S(2)}, u32[]{:S(2)}) collective-permute-start(bf16[2,128,256]{2,1,0:T(8,128)(2,1)S(1)} %get-tuple-element.104), channel_id=1, source_target_pairs={{0,8},{8,0},{16,24},{24,16},{1,9},{9,1},{17,25},{25,17},{2,10},{10... | collective-permute-start | bytes 393224 | tf_op jit(solution)/shard_map/ppermute | solution.py:389
  100.9 3.5 %collective-permute-start.25 = (bf16[1,256,256]{2,1,0:T(8,128)(2,1)S(1)}, bf16[1,256,256]{2,1,0:T(8,128)(2,1)S(1)}, u32[]{:S(2)}, u32[]{:S(2)}) collective-permute-start(bf16[1,256,256]{2,1,0:T(8,128)(2,1)S(1)} %get-tuple-element.113), channel_id=1, source_target_pairs={{0,8},{8,0},{16,24},{24,16},{1,9},{9,1},{17,25},{25,17},{2,10},{10... | collective-permute-start | bytes 393224 | tf_op jit(solution)/shard_map/ppermute | solution.py:389
  104.0 3.6 %collective-permute-start.23 = (bf16[2,128,256]{2,1,0:T(8,128)(2,1)S(1)}, bf16[2,128,256]{2,1,0:T(8,128)(2,1)S(1)}, u32[]{:S(2)}, u32[]{:S(2)}) collective-permute-start(bf16[2,128,256]{2,1,0:T(8,128)(2,1)S(1)} %get-tuple-element.107), channel_id=1, source_target_pairs={{0,8},{8,0},{16,24},{24,16},{1,9},{9,1},{17,25},{25,17},{2,10},{10... | collective-permute-start | bytes 393224 | tf_op jit(solution)/shard_map/ppermute | solution.py:389
  105.0 6.1 %collective-permute-start.26 = (bf16[256,256]{1,0:T(8,128)(2,1)S(1)}, bf16[256,256]{1,0:T(8,128)(2,1)S(1)}, u32[]{:S(2)}, u32[]{:S(2)}) collective-permute-start(bf16[256,256]{1,0:T(8,128)(2,1)S(1)} %shard_map.85), channel_id=1, source_target_pairs={{0,16},{24,8},{1,17},{25,9},{2,18},{26,10},{3,19},{27,11},{4,20},{... | collective-permute-start | bytes 393224 | tf_op jit(solution)/shard_map/ppermute | solution.py:397
  107.5 6.1 %collective-permute-start.27 = (bf16[128,256]{1,0:T(8,128)(2,1)S(1)}, bf16[128,256]{1,0:T(8,128)(2,1)S(1)}, u32[]{:S(2)}, u32[]{:S(2)}) collective-permute-start(bf16[128,256]{1,0:T(8,128)(2,1)S(1)} %shard_map.81), channel_id=1, source_target_pairs={{0,16},{8,24},{16,0},{24,8},{1,17},{9,25},{17,1},{25,9},{2,18},{10... | collective-permute-start | bytes 196616 | tf_op jit(solution)/shard_map/ppermute | solution.py:397
  108.2 5.7 %collective-permute-start.28 = (bf16[128,256]{1,0:T(8,128)(2,1)S(1)}, bf16[128,256]{1,0:T(8,128)(2,1)S(1)}, u32[]{:S(2)}, u32[]{:S(2)}) collective-permute-start(bf16[128,256]{1,0:T(8,128)(2,1)S(1)} %shard_map.83), channel_id=1, source_target_pairs={{0,16},{8,24},{16,0},{24,8},{1,17},{9,25},{17,1},{25,9},{2,18},{10... | collective-permute-start | bytes 196616 | tf_op jit(solution)/shard_map/ppermute | solution.py:397

commit v3 on v2

--- a/solution.py
+++ b/solution.py
@@ -12,8 +12,8 @@
 VMEM = pl.BlockSpec(memory_space=pltpu.VMEM)
 SMEM = pl.BlockSpec(memory_space=pltpu.SMEM)
 MID, LOW, CORE, STRAIGHT, TABLE = 0, 1, 2, 3, 4
-MEAN_COST, FAR_COST, FIRST_COST, LAST_COST = 6, 3, 0, 4
-WEIGH_COSTS, GATHER_COST = (0, 0, 12), 3
+MEAN_COST, FAR_COST, EARLY_COST, FIRST_COST, LAST_COST = 6, 3, 4, 0, 4
+WEIGH_COST, FOLD_COST = 12, 6
 
 
 def call(kernel, outs, *args, scratch=(), limit=24, cost=0):
@@ -66,18 +66,22 @@
         piece[...] = grads[:, a:b]
 
 
-def by_core(info, walker, slot, sends, keep, value):
-    @pl.when(info[CORE] == walker % 2)
-    def _():
-        keep[slot] = value
-
-    @pl.when(info[CORE] != walker % 2)
-    def _():
-        start = 0
-        for send in sends:
-            width = send.shape[-1]
-            send[slot] = value[:, start : start + width]
-            start += width
+def by_core(info, walker, slot, sends, keep, value, turn=None):
+    width = value.shape[-1]
+    turn = width if turn is None else turn
+    for core in (0, 1):
+
+        @pl.when(info[CORE] == core)
+        def _():
+            for a, b, kept in ((0, turn, core == walker % 2), (turn, width, core != walker % 2)):
+                if kept and a < b:
+                    keep[slot, :, a:b] = value[:, a:b]
+                start = 0
+                for send in sends:
+                    lo, hi = max(a, start), min(b, start + send.shape[-1])
+                    if not kept and lo < hi:
+                        send[slot, :, lo - start : hi - start] = value[:, lo:hi]
+                    start += send.shape[-1]
 
 
 def products(tile, rights):
@@ -86,11 +90,12 @@
 
 def by_block(info, block, axis, per, slots, sends, keep, value):
     piece = value.shape[axis] // per
+    turn = value.shape[1] // 2 if axis == 0 and per == 1 else None
     for i in range(per):
         at = slice(i * piece, (i + 1) * piece)
         walker = block * per + i
         part = value[at] if axis == 0 else value[:, at]
-        by_core(info, walker, slots[walker], sends, keep, part)
+        by_core(info, walker, slots[walker], sends, keep, part, turn)
 
 
 def low_or_high(info, then):
@@ -98,8 +103,11 @@
         pl.when(info[LOW] == low)(functools.partial(then, 0 if low else 3, 3 if low else 0))
 
 
-def mean_kernel(count, sums, out):
+def mean_kernel(count, sums, m1, m2, out, near_mean, next_mean):
+    rw = near_mean.shape[1]
     out[...] = sums[:, -out.shape[1] :] / count
+    near_mean[...] = m1[:, :rw] / count
+    next_mean[...] = m2[:, :rw] / count
 
 
 def far_kernel(raw, mean, out):
@@ -131,8 +139,8 @@
 
     @pl.when(info[MID] == 0)
     def _():
-        next_to = centred(near[...], m1[:, :rw] / count)
-        group(centred(mid2[...], m2[:, :rw] / count), next_to)
+        next_to = centred(near[...], m1[...])
+        group(centred(mid2[...], m2[...]), next_to)
 
     result = products(early[...], (ow, far))
     for j, block in enumerate((1, 2)):
@@ -144,7 +152,7 @@
 
     @pl.when(info[MID] == 1)
     def _():
-        second[...] = centred(near[...], m1[:, :rw] / count)
+        second[...] = centred(near[...], m1[...])
 
     @pl.when(info[MID] == 0)
     def _():
@@ -174,7 +182,7 @@
 
     @pl.when(info[MID] == 1)
     def _():
-        tile[...] = centred(last1[...], m2[:, :rw] / count)
+        tile[...] = centred(last1[...], m2[...])
 
     @pl.when(info[MID] == 0)
     def _():
@@ -220,27 +228,59 @@
     return jnp.concatenate(values, axis=1)
 
 
-def pair_kernel(first, pieces, count, cuts, info, keep, *refs):
+def pair_kernel(first, pieces, count, info, keep, *refs):
     gots, outs = refs[:count], refs[count:]
-    parts = len(cuts) - 1
-    for k in range(len(outs) // parts):
-        i = jnp.clip(info[TABLE + k + 1] - first, 0, pieces - 1)
-        value = pair(keep, gots, i).astype(BF)
-        for part in range(parts):
-            outs[k * parts + part][...] = value[:, cuts[part] : cuts[part + 1]]
-
-
-def total(keep, gots, others, i, cuts):
-    parts = len(cuts) - 1
+    for k, out in enumerate(outs, 1):
+        i = jnp.clip(info[TABLE + k] - first, 0, pieces - 1)
+        out[...] = pair(keep, gots, i).astype(BF)
+
+
+def total(keep, gots, others, i):
     value = pair(keep, gots, i)
-    for k in range(len(others) // parts):
-        got = [other[...] for other in others[k * parts : (k + 1) * parts]]
-        value = value + jnp.concatenate(got, axis=1).astype(F32)
+    for other in others:
+        value = value + other[...].astype(F32)
     return value
 
 
+def columns(keep, gots, lo, hi):
+    start, values = 0, []
+    for got in gots:
+        a, b = max(lo, start), min(hi, start + got.shape[2])
+        if a < b:
+            values.append(keep[0, :, a:b].astype(F32) + got[0, :, a - start : b - start].astype(F32))
+        start += got.shape[2]
+    return jnp.concatenate(values, axis=1)
+
+
+def away_kernel(first, count, info, keep, *refs):
+    gots, out = refs[:count], refs[count]
+    width = keep.shape[2]
+
+    @pl.when(info[TABLE] == first)
+    def _():
+        out[...] = columns(keep, gots, width // 2, width).astype(BF)
+
+    @pl.when(info[TABLE] != first)
+    def _():
+        out[...] = columns(keep, gots, 0, width // 2).astype(BF)
+
+
+def home_kernel(count, info, keep, *refs):
+    gots, got_x, outs = refs[:count], refs[count], refs[count + 1 :]
+    width = keep.shape[2]
+    value = (columns(keep, gots, width // 2, width) + got_x[...].astype(F32)).astype(BF)
+    start = 0
+    for out in outs:
+        out[...] = value[:, start : start + out.shape[1]]
+        start += out.shape[1]
+
+
+def fold_kernel(count, info, keep, got, *refs):
+    refs[-1][...] = total(keep, (got,), refs[:-1], info[TABLE]).T / count
+
+
 def gather_kernel(count, shapes, info, *refs):
-    ham, corr = refs[-2:]
+    *refs, chunk, ham, corr = refs
     cw = ham.shape[1] // 2
     pos = info[TABLE]
 
@@ -253,56 +293,40 @@
         def _():
             out[:, cw + start : cw + start + value.shape[1]] = value
 
+    def spans(refs, start=0):
+        for ref in refs:
+            yield start, start + ref.shape[-1], ref
+            start += ref.shape[-1]
+
+    put(ham, False, cw - chunk.shape[1], chunk[...])
     at = 0
-    for n_gots, n_others, first, pieces, parts, cuts in shapes:
+    for n_gots, n_others, turned, first, pieces, parts in shapes:
         keep, gots = refs[at], refs[at + 1 : at + 1 + n_gots]
         others = refs[at + 1 + n_gots : at + 1 + n_gots + n_others]
         at += 1 + n_gots + n_others
+        width = keep.shape[2]
+
+        def place(a, b, value):
+            start = 0
+            for size, (out, near, to) in parts:
+                lo, hi = max(a, start), min(b, start + size)
+                if lo < hi:
+                    put((ham, corr)[out], near, to + lo - start, value[:, lo - a : hi - a] / count)
+                start += size
 
         @pl.when((pos >= first) & (pos < first + pieces))
         def _():
-            value = total(keep, gots, others, pos - first, cuts) / count
-            start = 0
-            for got, (out, near, to) in zip(gots, parts):
-                width = got.shape[2]
-                put((ham, corr)[out], near, to, value[:, start : start + width])
-                start += width
-
-
-def last_kernel(count, shapes, info, held, *refs):
-    del held
-    out = refs[-1]
-    at = start = 0
-    for n_others, n in shapes:
-        keep, got, *others = refs[at : at + 2 + n_others]
-        at += 2 + n_others
-        value = total(keep, (got,), others, info[TABLE], (0, keep.shape[2]))
-        out[:, start : start + n] = value.T / count
-        start += n
-
-
-def last_chunks(count, start, info, ham, messages):
-    rows, width = ham.shape
-    shapes = [(len(others), keep.shape[1]) for keep, _, others, *_ in messages]
-    flat = [a for keep, gots, others, *_ in messages for a in (keep, *gots, *others)]
-    n = sum(s[1] for s in shapes)
-    ahead, behind = (width // 2 + start) // n, start // n
-    vmem = pl.BlockSpec(memory_space=pltpu.VMEM)
-    return pl.pallas_call(
-        functools.partial(last_kernel, count, shapes),
-        out_shape=jax.ShapeDtypeStruct(ham.shape, ham.dtype),
-        grid_spec=pltpu.PrefetchScalarGridSpec(
-            num_scalar_prefetch=1,
-            grid=(1,),
-            in_specs=[pl.BlockSpec(memory_space=pl.ANY)] + [vmem] * len(flat),
-            out_specs=pl.BlockSpec(
-                (rows, n), lambda i, info: (0, jnp.where(info[STRAIGHT] == 1, ahead, behind))
-            ),
-        ),
-        input_output_aliases={1: 0},
-        compiler_params=pltpu.CompilerParams(vmem_limit_bytes=16 * 2**20),
-        cost_estimate=pl.CostEstimate(flops=0, bytes_accessed=0, transcendentals=0),
-    )(info, ham, *flat)
+            i = pos - first
+            for a, b, got in spans(gots):
+                b = min(b, width // 2) if turned else b
+                if a < b:
+                    value = keep[i, :, a:b].astype(F32) + got[i, :, : b - a].astype(F32)
+                    for other in others[:1] if turned else others:
+                        value = value + other[:, a:b].astype(F32)
+                    place(a, b, value)
+            if turned:
+                for a, b, home in spans(others[1:], width // 2):
+                    place(a, b, home[...].astype(F32))
 
 
 def per_device(o_rows, o_cols, grad_energy, energy):
@@ -348,7 +372,7 @@
     m2 = lax.ppermute(m0, "pcol", [(0, 2), (1, 3), (2, 0), (3, 1)])
 
     column = energy[:, None]
-    cuts = [0, cw // 2, 3 * cw // 4, cw]
+    cuts = [0, cw // 2, cw]
     widths = [b - a for a, b in zip(cuts[:-1], cuts[1:])]
     ow, wide, *grads = call(
         functools.partial(own_kernel, count, cuts),
@@ -357,17 +381,18 @@
         o_cols, grad_energy, column, m0,
     )
 
-    near, mid1, m1, m2, ow, m0, *grads = lax.optimization_barrier(
-        (near, mid1, m1, m2, ow, m0, *grads)
-    )
+    near, mid1, ow, m0, *grads = lax.optimization_barrier((near, mid1, ow, m0, *grads))
     m3 = lax.ppermute(m0, "pcol", [(0, 3), (1, 2), (2, 1), (3, 0)])
     far_sums = lax.ppermute(m0, "prow", flip)
     mid2 = lax.ppermute(mid1, "pcol", ends)
     last1 = lax.ppermute(near, "pcol", inner)
     far_grads = [lax.ppermute(grads[0], "prow", flip)]
 
-    (far_mean,) = call(
-        functools.partial(mean_kernel, count), [((1, cw), F32)], far_sums, cost=MEAN_COST
+    far_mean, m1, m2 = call(
+        functools.partial(mean_kernel, count),
+        [((1, cw), F32), ((1, rw), F32), ((1, rw), F32)],
+        far_sums, m1, m2,
+        cost=MEAN_COST,
     )
     (far,) = call(far_kernel, [((samples, cw), BF)], far_raw, far_mean, cost=FAR_COST)
     second, held = call(
@@ -375,40 +400,63 @@
         [((samples, rw), BF), ((rw, 3 * cw), BF)],
         info, o_rows, near, m0, m1, ow, far,
     )
-    mid2, last1, far, m3, second, held, *grads = lax.optimization_barrier(
-        (mid2, last1, far, m3, second, held, *grads)
+    last1, far, m3, second, held, *grads = lax.optimization_barrier(
+        (last1, far, m3, second, held, *grads)
     )
     last2 = lax.ppermute(last1, "pcol", ends)
     far_grads += [lax.ppermute(g, "prow", flip) for g in grads[1:]]
 
     messages = []
 
-    def reduce(sends, keep, first, pieces, parts, split=None):
-        width = keep.shape[2]
-        at = (0, split, width) if split else (0, width)
+    def reduce(sends, keep, first, pieces, parts):
         gots = [lax.ppermute(send, "walker", other_core) for send in sends]
-        shapes = [((keep.shape[1], b - a), BF) for a, b in zip(at[:-1], at[1:])]
         sent = call(
-            functools.partial(pair_kernel, first, pieces, len(gots), at),
-            shapes * (chips - 1),
+            functools.partial(pair_kernel, first, pieces, len(gots)),
+            [(keep.shape[1:], BF)] * (chips - 1),
             info, keep, *gots,
         )
         others = [
-            lax.ppermute(s, "walker", shift(i // len(shapes) + 1, first, pieces))
-            for i, s in enumerate(sent)
+            lax.ppermute(s, "walker", shift(k, first, pieces)) for k, s in enumerate(sent, 1)
         ]
-        messages.append([keep, gots, others, first, pieces, parts, at])
+        messages.append([keep, gots, others, False, first, pieces, parts])
         return sent
 
-    parts = [(1, True, 0), (0, True, 0), (1, False, 0)]
+    def reduce_rows(sends, keep, first, parts):
+        if per > 1:
+            return reduce(sends, keep, first, per, parts)
+        gots = [lax.ppermute(send, "walker", other_core) for send in sends]
+        shape = (keep.shape[1], keep.shape[2] // 2)
+        sent = call(
+            functools.partial(away_kernel, first, len(gots)), [(shape, BF)], info, keep, *gots
+        )
+        got_x = lax.ppermute(sent[0], "walker", [(v, v ^ 2) for v in range(4)])
+        messages.append([keep, gots, [got_x], True, first, 1, parts])
+        return sent
+
+    def bring_home(message, sizes, *earlier):
+        keep, gots, others, turned, *_ = message
+        if turned:
+            homes = call(
+                functools.partial(home_kernel, len(gots)),
+                [((keep.shape[1], size), BF) for size in sizes],
+                info, keep, *gots, after(others[0], *earlier),
+            )
+            others += [lax.ppermute(h, "walker", other_core) for h in homes]
+
     n = widths[0]
-    message, short = ((per, piece, cw), BF), ((per, piece, n), BF)
+    parts = [(cw, (1, True, 0)), (cw, (0, True, 0)), (cw, (1, False, 0))]
+    chunk_part = [(n, (0, False, 0))]
+
+    def message_shapes(*sizes):
+        return [((per, piece, size), BF) for size in sizes]
+
     e_keep, early, *sends = call(
         functools.partial(early_kernel, count, per, place),
-        [((per, piece, 3 * cw), BF), ((samples, 2 * rw), BF)] + [message] * 3,
+        message_shapes(3 * cw) + [((samples, 2 * rw), BF)] + message_shapes(*[3 * cw // 4] * 4),
         info, o_rows, near, mid1, mid2, m0, m1, m2, m3, ow, far,
-    )
-    reduce(sends, e_keep, 0, per, parts, 2 * cw)
+        cost=EARLY_COST,
+    )
+    reduce_rows(sends, e_keep, 0, parts)
 
     chunk, held_chunk = call(
         functools.partial(first_chunk_kernel, 0),
@@ -416,54 +464,59 @@
         second, far, wide, far_grads[0],
         cost=FIRST_COST,
     )
-    early_x = messages[0][2]
-    last2, held_chunk, chunk, far_grads[1], *early_x = lax.optimization_barrier(
-        (last2, held_chunk, chunk, far_grads[1], *early_x)
-    )
-    messages[0][2] = early_x
+    c_keep, send = call(
+        functools.partial(early_chunk_kernel, per, place), message_shapes(n, n), info, early, chunk
+    )
+    reduce_rows([send], c_keep, 0, chunk_part)
+
+    last2, held_chunk, chunk, messages[0][2], messages[1][2] = lax.optimization_barrier(
+        (last2, held_chunk, chunk, messages[0][2], messages[1][2])
+    )
+    size = (3 * cw + n) // 2
     l_keep, last, *sends = call(
         functools.partial(late_kernel, count, per, late_slots),
-        [((per, piece, 3 * cw + n), BF), ((samples, rw), BF)] + [message] * 3 + [short],
+        message_shapes(2 * size) + [((samples, rw), BF)] + message_shapes(*[cw, size - cw] * 2),
         info, last1, last2, m2, m3, ow, far, chunk, held, held_chunk,
         cost=LAST_COST,
     )
-    sent = reduce(sends, l_keep, per, per, parts + [(0, False, 0)])
-
-    c_keep, send = call(
-        functools.partial(early_chunk_kernel, per, place),
-        [short, short],
-        info, early, after(chunk, *sent),
-    )
-    reduce([send], c_keep, 0, per, [(0, False, 0)])
-
-    for j in (1, 2):
-        n = widths[j]
-        (right,) = call(
-            functools.partial(weigh_kernel, cuts[j]),
-            [((samples, n), BF)],
-            far, wide, far_grads[j],
-            cost=WEIGH_COSTS[j],
-        )
-        send, keep = call(
-            functools.partial(chunk_kernel, per, place),
-            [((2 * per, n, piece), BF)] * 2,
-            info, early, second, last, after(right, *sent),
-        )
-        sent = reduce([send], keep, 0, 2 * per, None)
-
-    tail = messages[-2:]
-    messages[0][0] = after(messages[0][0], *sent)
+    sent = reduce_rows(sends, l_keep, per, parts + chunk_part)
+
+    bring_home(messages[0], [3 * cw // 2], *sent)
+    bring_home(messages[1], [n // 2], *sent)
+    n = widths[1]
+    (right,) = call(
+        functools.partial(weigh_kernel, cuts[1]),
+        [((samples, n), BF)],
+        far, wide, far_grads[1],
+        cost=WEIGH_COST,
+    )
+    messages[0][2], messages[1][2], right = lax.optimization_barrier(
+        (messages[0][2], messages[1][2], right)
+    )
+    send, keep = call(
+        functools.partial(chunk_kernel, per, place),
+        [((2 * per, n, piece), BF)] * 2,
+        info, early, second, last, after(right, *sent),
+    )
+    sent = reduce([send], keep, 0, 2 * per, None)
+    keep, gots, others, *_ = messages.pop()
+    (folded,) = call(
+        functools.partial(fold_kernel, count),
+        [((piece, n), F32)],
+        info, keep, *gots, *others,
+        cost=FOLD_COST,
+    )
+    bring_home(messages[2], [min(256, size - a) for a in range(0, size, 256)], *sent)
+
     flat, shapes = [], []
-    for k, g, o, *what in messages[:-2]:
+    for k, g, o, *what in messages:
         flat += [k, *g, *o]
         shapes.append((len(g), len(o), *what))
-    ham, corr = call(
+    return call(
         functools.partial(gather_kernel, count, shapes),
         [((piece, 2 * cw), F32)] * 2,
-        info, *flat,
-        cost=GATHER_COST,
-    )
-    return last_chunks(count, cuts[1], info, ham, tail), corr
+        info, *flat, folded,
+    )
 
 
 def solution(mesh):

time: 116 us -> 110 us (0.948)
  starting transfers between devices: 37.4 us -> 30.2 us
  waiting for transfers between devices: 27.9 us -> 32.2 us
  local copies, waits for them, and re-layouts: 13.4 us -> 11.9 us
  Pallas kernels: 29.5 us -> 28.3 us
    ppermute x6 -> x19, waiting for transfers between devices: 4.74 us -> 9.71 us  [the longest x9 4.94 us: reduce_rows(): gots = [lax.ppermute(send, 'walker', other_core) for send in sends]]
    ppermute x10 -> x1, starting transfers between devices: 4.54 us -> 0.07 us  [reduce(): gots = [lax.ppermute(send, 'walker', other_core) for send in sends]]
    ppermute x1, waiting for transfers between devices: 11.4 us -> 14.1 us  [per_device(): far_sums = lax.ppermute(m0, 'prow', flip)]
    ppermute x1, starting transfers between devices: 0.9 us -> 3.21 us  [per_device(): m1 = lax.ppermute(m0, 'pcol', outer)]
    ppermute x2 -> x1, waiting for transfers between devices: 5.19 us -> 2.88 us  [per_device(): far_grads += [lax.ppermute(g, 'prow', flip) for g in grads[1:]]]
    ppermute x1, starting transfers between devices: 3.43 us -> 1.58 us  [per_device(): near = lax.ppermute(o_rows, 'pcol', outer)]
    ppermute x2 -> x1, starting transfers between devices: 3.25 us -> 1.49 us  [per_device(): far_grads += [lax.ppermute(g, 'prow', flip) for g in grads[1:]]]
    ppermute x10 -> x1, waiting for transfers between devices: 2.99 us -> 1.52 us  [reduce(): gots = [lax.ppermute(send, 'walker', other_core) for send in sends]]
  transfers between devices with their start and end apart: 29 -> 32, of which waited for: 12 -> 16; matrix products, arithmetic and copies ran while one was open for 2% -> 1% of each run, Pallas kernels for 24% -> 24%
where the time goes in v3:
time: 110 us
  waiting for transfers between devices  32.2 us (29%)
  starting transfers between devices  30.2 us (27%)
  Pallas kernels  28.3 us (26%)
  local copies, waits for them, and re-layouts  11.9 us (11%)
  blocking collectives  6.55 us (6%)
    pallas_call x20, Pallas kernels, call(): pl.pallas_call(kernel, out_shape=[jax.ShapeDtypeStruct(s, d) for s, d in...  28.3 us
    ppermute x1, waiting for transfers between devices, per_device(): far_sums = lax.ppermute(m0, 'prow', flip)  14.1 us
    unnamed x26, local copies, waits for them, and re-layouts  10.7 us
    psum x1, blocking collectives, per_device(): m0 = lax.psum(sums, 'walker')  6.55 us
    ppermute x3, starting transfers between devices, reduce_rows(): got_x = lax.ppermute(sent[0], 'walker', [(v, v ^ 2) for v in range(4)])  5.78 us
    ppermute x9, waiting for transfers between devices, reduce_rows(): gots = [lax.ppermute(send, 'walker', other_core) for send in sends]  4.94 us
    ppermute x1, starting transfers between devices, per_device(): m1 = lax.ppermute(m0, 'pcol', outer)  3.21 us
    ppermute x1, starting transfers between devices, per_device(): far_raw = lax.ppermute(o_cols, 'prow', flip)  3.03 us
  transfers between devices with their start and end apart: 32, of which 16 were waited for; matrix products, arithmetic and copies ran while one was open for 1% of the time, Pallas kernels for 24%

profile of v3, /device:TPU:0, one launch (start us, length us, event | category | flops | bytes accessed | tf_op | source)
XLA Modules:
  0.0 110.0 jit_solution(14023968190923265737)
XLA Ops:
  0.6 3.0 %collective-permute-start.7 = (bf16[2048,512]{1,0:T(8,128)(2,1)}, bf16[2048,512]{1,0:T(8,128)(2,1)}, u32[]{:S(2)}, u32[]{:S(2)}) collective-permute-start(bf16[2048,512]{1,0:T(8,128)(2,1)} %cols.3), channel_id=1, source_target_pairs={{0,4},{4,0},{1,5},{5,1},{2,6},{6,2},{3,7},{7,3},{8,12},{12,8},{9,1... | collective-permute-start | bytes 6291464 | tf_op jit(solution)/shard_map/ppermute | solution.py:365
  3.7 1.6 %collective-permute-start = (bf16[2048,256]{1,0:T(8,128)(2,1)}, bf16[2048,256]{1,0:T(8,128)(2,1)}, u32[]{:S(2)}, u32[]{:S(2)}) collective-permute-start(bf16[2048,256]{1,0:T(8,128)(2,1)} %own_rows.3), channel_id=1, source_target_pairs={{0,1},{1,0},{2,3},{3,2},{4,5},{5,4},{6,7},{7,6},{8,9},{9,8},{10,11... | collective-permute-start | bytes 3145736 | tf_op jit(solution)/shard_map/ppermute | solution.py:366
  5.2 1.6 %collective-permute-start.1 = (bf16[2048,256]{1,0:T(8,128)(2,1)}, bf16[2048,256]{1,0:T(8,128)(2,1)}, u32[]{:S(2)}, u32[]{:S(2)}) collective-permute-start(bf16[2048,256]{1,0:T(8,128)(2,1)} %own_rows.3), channel_id=1, source_target_pairs={{1,2},{2,1},{5,6},{6,5},{9,10},{10,9},{13,14},{14,13},{17,18},{18,... | collective-permute-start | bytes 3145736 | tf_op jit(solution)/shard_map/ppermute | solution.py:367
  6.9 1.6 %copy-done = bf16[2048,512]{1,0:T(8,128)(2,1)S(1)} copy-done((bf16[2048,512]{1,0:T(8,128)(2,1)S(1)}, bf16[2048,512]{1,0:T(8,128)(2,1)}, u32[]{:S(2)}) %copy-start) | copy-done | bytes 2097176
  8.5 1.2 %copy-done.4 = bf16[2048,256]{1,0:T(8,128)(2,1)S(1)} copy-done((bf16[2048,256]{1,0:T(8,128)(2,1)S(1)}, bf16[2048,256]{1,0:T(8,128)(2,1)}, u32[]{:S(2)}) %copy-start.4) | copy-done | bytes 1048600
  9.7 0.5 shard_map.68
  10.2 6.6 %psum.7.sums.m0 = f32[1,768]{1,0:T(1,128)S(1)} all-reduce(f32[1,768]{1,0:T(1,128)S(1)} %shard_map.68), channel_id=1, replica_groups=mesh['walker'=4,'prow'=2,'pcol'=4] {'walker'}, use_global_device_ids=true, to_apply=%region_0.1 | all-reduce | flops 768 | bytes 6144 | tf_op jit(solution)/shard_map/psum | solution.py:370
  16.8 3.2 %collective-permute-start.4 = (f32[1,768]{1,0:T(1,128)S(1)}, f32[1,768]{1,0:T(1,128)S(1)}, u32[]{:S(2)}, u32[]{:S(2)}) collective-permute-start(f32[1,768]{1,0:T(1,128)S(1)} %psum.7.sums.m0), channel_id=1, source_target_pairs={{0,1},{1,0},{2,3},{3,2},{4,5},{5,4},{6,7},{7,6},{8,9},{9,8},{10,11... | collective-permute-start | bytes 9224 | tf_op jit(solution)/shard_map/ppermute | solution.py:371
  20.0 0.4 copy.7.energy
  20.4 1.6 %copy-done.8 = bf16[2048,512]{1,0:T(8,128)(2,1)S(1)} copy-done((bf16[2048,512]{1,0:T(8,128)(2,1)S(1)}, bf16[2048,512]{1,0:T(8,128)(2,1)}, u32[]{:S(2)}) %copy-start.8) | copy-done | bytes 2097176
  22.0 1.2 %shard_map.69 = (bf16[2048,1024]{1,0:T(8,128)(2,1)S(1)}, f32[2048,256]{1,0:T(8,128)S(1)}, bf16[2048,256]{1,0:T(8,128)(2,1)S(1)}, bf16[2048,256]{1,0:T(8,128)(2,1)S(1)}) custom-call(bf16[2048,512]{1,0:T(8,128)(2,1)S(1)} %copy-done.1, bf16[2048,512]{1,0:T(8,128)(2,1)S(1)} %copy-done.8, f32[2048,1]{1,0:T(8,128)S(1)} %copy.7.energy, f32[1,768]{1,0:T(1,128)S(1)} %psum.7.sums.m0), custom_call_target="tpu_custom_call" | custom-call | tf_op jit(solution)/shard_map/pallas_call | solution.py:20
  23.2 2.0 %copy-done.2 = bf16[2048,1024]{1,0:T(8,128)(2,1)} copy-done((bf16[2048,1024]{1,0:T(8,128)(2,1)}, bf16[2048,1024]{1,0:T(8,128)(2,1)S(1)}, u32[]{:S(2)}) %copy-start.2) | copy-done | bytes 4194328
  25.1 1.4 %copy-done.6 = f32[2048,256]{1,0:T(8,128)} copy-done((f32[2048,256]{1,0:T(8,128)}, f32[2048,256]{1,0:T(8,128)S(1)}, u32[]{:S(2)}) %copy-start.6) | copy-done | bytes 2097176
  26.5 1.0 copy-done.9
  27.5 1.0 copy-done.11
  28.6 0.4 collective-permute-start.3
  29.0 0.7 collective-permute-start.6
  29.7 1.3 %collective-permute-start.2 = (bf16[2048,256]{1,0:T(8,128)(2,1)}, bf16[2048,256]{1,0:T(8,128)(2,1)S(1)}, u32[]{:S(2)}, u32[]{:S(2)}) collective-permute-start(bf16[2048,256]{1,0:T(8,128)(2,1)} %collective-permute-done.1.mid1), channel_id=1, source_target_pairs={{1,0},{2,3},{5,4},{6,7},{9,8},{10,11},{13,12},{14,15},{17,16},{18,... | collective-permute-start | bytes 3145736 | tf_op jit(solution)/shard_map/ppermute | solution.py:387
  31.0 0.7 dynamic-slice_bitcast_fusion
  31.8 0.9 collective-permute-done.5.m2
  32.7 2.9 %collective-permute-start.8 = (f32[1,768]{1,0:T(1,128)S(1)}, f32[1,768]{1,0:T(1,128)S(1)}, u32[]{:S(2)}, u32[]{:S(2)}) collective-permute-start(f32[1,768]{1,0:T(1,128)S(1)} %psum.7.sums.m0), channel_id=1, source_target_pairs={{0,3},{1,2},{2,1},{3,0},{4,7},{5,6},{6,5},{7,4},{8,11},{9,10},{10,... | collective-permute-start | bytes 9224 | tf_op jit(solution)/shard_map/ppermute | solution.py:385
  35.6 14.1 %collective-permute-done.3.sums = f32[1,768]{1,0:T(1,128)S(1)} collective-permute-done((f32[1,768]{1,0:T(1,128)S(1)}, f32[1,768]{1,0:T(1,128)S(1)}, u32[]{:S(2)}, u32[]{:S(2)}) %collective-permute-start.3) | collective-permute-done | bytes 3104 | tf_op jit(solution)/shard_map/ppermute | solution.py:386
  49.6 1.7 %collective-permute-start.14 = (bf16[2048,256]{1,0:T(8,128)(2,1)}, bf16[2048,256]{1,0:T(8,128)(2,1)S(1)}, u32[]{:S(2)}, u32[]{:S(2)}) collective-permute-start(bf16[2048,256]{1,0:T(8,128)(2,1)} %copy-done.11), channel_id=1, source_target_pairs={{0,4},{4,0},{1,5},{5,1},{2,6},{6,2},{3,7},{7,3},{8,12},{12,8},{9,1... | collective-permute-start | bytes 3145736 | tf_op jit(solution)/shard_map/ppermute | solution.py:389
  51.4 2.1 %shard_map.71.far = bf16[2048,512]{1,0:T(8,128)(2,1)S(1)} custom-call(bf16[2048,512]{1,0:T(8,128)(2,1)} %collective-permute-done.7.raw, f32[1,512]{1,0:T(1,128)S(1)} %get-tuple-element.67.mean), custom_call_target="tpu_custom_call" | custom-call | flops 3449999872 | tf_op jit(solution)/shard_map/pallas_call | solution.py:20
  53.5 0.7 copy-done.3
  54.2 0.3 copy-done.5
  54.5 3.3 %shard_map.72 = (bf16[2048,256]{1,0:T(8,128)(2,1)S(1)}, bf16[256,1536]{1,0:T(8,128)(2,1)S(1)}) custom-call(s32[6]{0:T(128)S(1)} %concatenate.3.info, bf16[2048,256]{1,0:T(8,128)(2,1)S(1)} %copy-done.5, bf16[2048,256]{1,0:T(8,128)(2,1)} %collective-permute-done.near, f32[1,768]{1,0:T(1,128)S(1)} %psum.7.sums.m0, f32[1,256]{1,0:T(1,128)S(1)} %get-tuple-element.65.m1, ...), custom_call_target="tpu_custom_call" | custom-call | tf_op jit(solution)/shard_map/pallas_call | solution.py:20
  57.8 1.3 %collective-permute-start.13 = (bf16[2048,256]{1,0:T(8,128)(2,1)S(1)}, bf16[2048,256]{1,0:T(8,128)(2,1)S(1)}, u32[]{:S(2)}, u32[]{:S(2)}) collective-permute-start(bf16[2048,256]{1,0:T(8,128)(2,1)S(1)} %collective-permute-done.6.last1), channel_id=1, source_target_pairs={{1,0},{2,3},{5,4},{6,7},{9,8},{10,11},{13,12},{14,15},{17,16},{18,... | collective-permute-start | bytes 3145736 | tf_op jit(solution)/shard_map/ppermute | solution.py:406
  59.1 1.0 collective-permute-done.2.mid2
  60.1 6.0 %shard_map.73 = (bf16[1,256,1536]{2,1,0:T(8,128)(2,1)S(1)}, bf16[2048,512]{1,0:T(8,128)(2,1)S(1)}, bf16[1,256,384]{2,1,0:T(8,128)(2,1)S(1)}, bf16[1,256,384]{2,1...) custom-call(s32[6]{0:T(128)S(1)} %concatenate.3.info, ...), custom_call_target="tpu_custom_call" | custom-call | flops 4600000000 | tf_op jit(solution)/shard_map/pallas_call | solution.py:20
  66.2 0.5 collective-permute-start.11
  66.7 0.9 collective-permute-done.10.refs_1_.refs_2_
  68.2 0.9 collective-permute-done.9.refs_0_.refs_1_
  69.0 0.6 shard_map.75
  69.7 1.6 %collective-permute-start.15 = (bf16[256,768]{1,0:T(8,128)(2,1)S(1)}, bf16[256,768]{1,0:T(8,128)(2,1)S(1)}, u32[]{:S(2)}, u32[]{:S(2)}) collective-permute-start(bf16[256,768]{1,0:T(8,128)(2,1)S(1)} %shard_map.75), channel_id=1, source_target_pairs={{0,16},{8,24},{16,0},{24,8},{1,17},{9,25},{17,1},{25,9},{2,18},{10... | collective-permute-start | bytes 1179656 | tf_op jit(solution)/shard_map/ppermute | solution.py:432
  71.3 1.5 %collective-permute-start.24 = (bf16[2048,256]{1,0:T(8,128)(2,1)S(1)}, bf16[2048,256]{1,0:T(8,128)(2,1)S(1)}, u32[]{:S(2)}, u32[]{:S(2)}) collective-permute-start(bf16[2048,256]{1,0:T(8,128)(2,1)S(1)} %copy-done.10), channel_id=1, source_target_pairs={{0,4},{4,0},{1,5},{5,1},{2,6},{6,2},{3,7},{7,3},{8,12},{12,8},{9,1... | collective-permute-start | bytes 3145736 | tf_op jit(solution)/shard_map/ppermute | solution.py:407
  72.7 1.9 %collective-permute-done.14.grads = bf16[2048,256]{1,0:T(8,128)(2,1)S(1)} collective-permute-done((bf16[2048,256]{1,0:T(8,128)(2,1)}, bf16[2048,256]{1,0:T(8,128)(2,1)S(1)}, u32[]{:S(2)}, u32[]{:S(2)}) %collective-permute-start.14) | collective-permute-done | bytes 1048608 | tf_op jit(solution)/shard_map/ppermute | solution.py:389
  74.7 0.7 shard_map.74
  75.4 1.3 %shard_map.76 = (bf16[1,256,256]{2,1,0:T(8,128)(2,1)S(1)}, bf16[1,256,256]{2,1,0:T(8,128)(2,1)S(1)}) custom-call(s32[6]{0:T(128)S(1)} %concatenate.3.info, bf16[2048,512]{1,0:T(8,128)(2,1)S(1)} %get-tuple-element.85.early, bf16[2048,256]{1,0:T(8,128)(2,1)S(1)} %get-tuple-element.90.right.chunk), custom_call_target="tpu_custom_call" | custom-call | tf_op jit(solution)/shard_map/pallas_call | solution.py:20
  76.8 1.3 %collective-permute-done.16.refs_0_.refs_8_ = bf16[1,256,256]{2,1,0:T(8,128)(2,1)S(1)} collective-permute-done((bf16[1,256,256]{2,1,0:T(8,128)(2,1)S(1)}, bf16[1,256,256]{2,1,0:T(8,128)(2,1)S(1)}, u32[]{:S(2)}, u32[]{:S(2)}) %collective-permute-start.16) | collective-permute-done | bytes 131104 | tf_op jit(solution)/shard_map/ppermute | solution.py:427
  78.1 0.6 shard_map.77
  78.7 2.3 %collective-permute-start.17 = (bf16[256,128]{1,0:T(8,128)(2,1)S(1)}, bf16[256,128]{1,0:T(8,128)(2,1)S(1)}, u32[]{:S(2)}, u32[]{:S(2)}) collective-permute-start(bf16[256,128]{1,0:T(8,128)(2,1)S(1)} %shard_map.77), channel_id=1, source_target_pairs={{0,16},{8,24},{16,0},{24,8},{1,17},{9,25},{17,1},{25,9},{2,18},{10... | collective-permute-start | bytes 196616 | tf_op jit(solution)/shard_map/ppermute | solution.py:432
  81.0 2.4 %collective-permute-done.17.refs_1_.refs_9_ = bf16[256,128]{1,0:T(8,128)(2,1)S(1)} collective-permute-done((bf16[256,128]{1,0:T(8,128)(2,1)S(1)}, bf16[256,128]{1,0:T(8,128)(2,1)S(1)}, u32[]{:S(2)}, u32[]{:S(2)}) %collective-permute-start.17) | collective-permute-done | bytes 65568 | tf_op jit(solution)/shard_map/ppermute | solution.py:432
  83.5 3.3 %shard_map.78 = (bf16[1,256,1792]{2,1,0:T(8,128)(2,1)S(1)}, bf16[2048,256]{1,0:T(8,128)(2,1)S(1)}, bf16[1,256,512]{2,1,0:T(8,128)(2,1)S(1)}, bf16[1,256,384]{2,1...) custom-call(s32[6]{0:T(128)S(1)} %concatenate.3.info, ...), custom_call_target="tpu_custom_call" | custom-call | flops 4600000000 | tf_op jit(solution)/shard_map/pallas_call | solution.py:20
  86.9 0.5 collective-permute-start.20
  87.4 0.4 collective-permute-start.21
  87.9 1.2 %collective-permute-done.19.refs_1_.refs_13_ = bf16[1,256,384]{2,1,0:T(8,128)(2,1)S(1)} collective-permute-done((bf16[1,256,384]{2,1,0:T(8,128)(2,1)S(1)}, bf16[1,256,384]{2,1,0:T(8,128)(2,1)S(1)}, u32[]{:S(2)}, u32[]{:S(2)}) %collective-permute-start.19) | collective-permute-done | bytes 196640 | tf_op jit(solution)/shard_map/ppermute | solution.py:427
  89.3 0.7 shard_map.79
  90.0 1.9 %collective-permute-start.25 = (bf16[256,896]{1,0:T(8,128)(2,1)S(1)}, bf16[256,896]{1,0:T(8,128)(2,1)S(1)}, u32[]{:S(2)}, u32[]{:S(2)}) collective-permute-start(bf16[256,896]{1,0:T(8,128)(2,1)S(1)} %shard_map.79), channel_id=1, source_target_pairs={{0,16},{8,24},{16,0},{24,8},{1,17},{9,25},{17,1},{25,9},{2,18},{10... | collective-permute-start | bytes 1376264 | tf_op jit(solution)/shard_map/ppermute | solution.py:432
  91.9 0.6 shard_map.81
  92.6 0.7 shard_map.80
  93.3 0.6 collective-permute-start.22
  93.8 2.9 %collective-permute-done.24.grads = bf16[2048,256]{1,0:T(8,128)(2,1)S(1)} collective-permute-done((bf16[2048,256]{1,0:T(8,128)(2,1)S(1)}, bf16[2048,256]{1,0:T(8,128)(2,1)S(1)}, u32[]{:S(2)}, u32[]{:S(2)}) %collective-permute-start.24) | collective-permute-done | bytes 1048608 | tf_op jit(solution)/shard_map/ppermute | solution.py:407
  96.7 0.3 shard_map.82.right_ref
  97.0 2.1 %shard_map.83 = (bf16[2,256,256]{2,1,0:T(8,128)(2,1)S(1)}, bf16[2,256,256]{2,1,0:T(8,128)(2,1)S(1)}) custom-call(s32[6]{0:T(128)S(1)} %concatenate.3.info, bf16[2048,512]{1,0:T(8,128)(2,1)S(1)} %get-tuple-element.85.early, bf16[2048,256]{1,0:T(8,128)(2,1)S(1)} %get-tuple-element.81.second, bf16[2048,256]{1,0:T(8,128)(2,1)S(1)} %get-tuple-element.106.last, ...), custom_call_target="tpu_custom_call" | custom-call | tf_op jit(solution)/shard_map/pallas_call | solution.py:20
  99.2 1.5 %collective-permute-done.26.refs_0_.got = bf16[2,256,256]{2,1,0:T(8,128)(2,1)S(1)} collective-permute-done((bf16[2,256,256]{2,1,0:T(8,128)(2,1)S(1)}, bf16[2,256,256]{2,1,0:T(8,128)(2,1)S(1)}, u32[]{:S(2)}, u32[]{:S(2)}) %collective-permute-start.26) | collective-permute-done | bytes 262176 | tf_op jit(solution)/shard_map/ppermute | solution.py:412
  100.7 0.6 shard_map.84
  101.3 1.5 %collective-permute-start.31 = (bf16[256,256]{1,0:T(8,128)(2,1)S(1)}, bf16[256,256]{1,0:T(8,128)(2,1)S(1)}, u32[]{:S(2)}, u32[]{:S(2)}) collective-permute-start(bf16[256,256]{1,0:T(8,128)(2,1)S(1)} %shard_map.84), channel_id=1, source_target_pairs={{0,16},{8,24},{16,0},{24,8},{1,17},{9,25},{17,1},{25,9},{2,18},{10... | collective-permute-start | bytes 393224 | tf_op jit(solution)/shard_map/ppermute | solution.py:419
  102.8 0.7 shard_map.85
  103.6 0.5 collective-permute-start.28
  104.1 0.4 collective-permute-start.30
  104.6 2.3 %collective-permute-done.31.refs_0_ = bf16[256,256]{1,0:T(8,128)(2,1)S(1)} collective-permute-done((bf16[256,256]{1,0:T(8,128)(2,1)S(1)}, bf16[256,256]{1,0:T(8,128)(2,1)S(1)}, u32[]{:S(2)}, u32[]{:S(2)}) %collective-permute-start.31) | collective-permute-done | bytes 131104 | tf_op jit(solution)/shard_map/ppermute | solution.py:419
  106.9 0.7 shard_map.86.refs_21_
  107.6 2.4 %shard_map.87 = (f32[256,1024]{1,0:T(8,128)}, f32[256,1024]{1,0:T(8,128)}) custom-call(s32[6]{0:T(128)S(1)} %concatenate.3.info, bf16[1,256,1536]{2,1,0:T(8,128)(2,1)S(1)} %get-tuple-element.75.keep.refs_0_, bf16[1,256,384]{2,1,0:T(8,128)(2,1)S(1)} %collective-permute-done.9.refs_0_.refs_1_, ...), custom_call_target="tpu_custom_call" | custom-call | tf_op jit(solution)/shard_map/pallas_call | solution.py:20
  (50 shorter events, 1.9 us)
Async XLA Ops:
  0.6 50.8 %collective-permute-start.7 = (bf16[2048,512]{1,0:T(8,128)(2,1)}, bf16[2048,512]{1,0:T(8,128)(2,1)}, u32[]{:S(2)}, u32[]{:S(2)}) collective-permute-start(bf16[2048,512]{1,0:T(8,128)(2,1)} %cols.3), channel_id=1, source_target_pairs={{0,4},{4,0},{1,5},{5,1},{2,6},{6,2},{3,7},{7,3},{8,12},{12,8},{9,1... | collective-permute-start | bytes 6291464 | tf_op jit(solution)/shard_map/ppermute | solution.py:365
  3.7 25.0 %collective-permute-start = (bf16[2048,256]{1,0:T(8,128)(2,1)}, bf16[2048,256]{1,0:T(8,128)(2,1)}, u32[]{:S(2)}, u32[]{:S(2)}) collective-permute-start(bf16[2048,256]{1,0:T(8,128)(2,1)} %own_rows.3), channel_id=1, source_target_pairs={{0,1},{1,0},{2,3},{3,2},{4,5},{5,4},{6,7},{7,6},{8,9},{9,8},{10,11... | collective-permute-start | bytes 3145736 | tf_op jit(solution)/shard_map/ppermute | solution.py:366
  5.2 23.4 %collective-permute-start.1 = (bf16[2048,256]{1,0:T(8,128)(2,1)}, bf16[2048,256]{1,0:T(8,128)(2,1)}, u32[]{:S(2)}, u32[]{:S(2)}) collective-permute-start(bf16[2048,256]{1,0:T(8,128)(2,1)} %own_rows.3), channel_id=1, source_target_pairs={{1,2},{2,1},{5,6},{6,5},{9,10},{10,9},{13,14},{14,13},{17,18},{18,... | collective-permute-start | bytes 3145736 | tf_op jit(solution)/shard_map/ppermute | solution.py:367
  6.9 1.6 %copy-start = (bf16[2048,512]{1,0:T(8,128)(2,1)S(1)}, bf16[2048,512]{1,0:T(8,128)(2,1)}, u32[]{:S(2)}) copy-start(bf16[2048,512]{1,0:T(8,128)(2,1)} %cols.3) | copy-start | bytes 6291460
  8.4 1.2 %copy-start.4 = (bf16[2048,256]{1,0:T(8,128)(2,1)S(1)}, bf16[2048,256]{1,0:T(8,128)(2,1)}, u32[]{:S(2)}) copy-start(bf16[2048,256]{1,0:T(8,128)(2,1)} %own_rows.3) | copy-start | bytes 3145732
  9.7 10.3 %copy-start.12 = (f32[2048]{0:T(1024)S(1)}, f32[2048]{0:T(1024)}, u32[]{:S(2)}) copy-start(f32[2048]{0:T(1024)} %param.8) | copy-start | bytes 24580
  9.7 10.7 %copy-start.1 = (bf16[2048,512]{1,0:T(8,128)(2,1)S(1)}, bf16[2048,512]{1,0:T(8,128)(2,1)}, u32[]{:S(2)}) copy-start(bf16[2048,512]{1,0:T(8,128)(2,1)} %cols.3) | copy-start | bytes 6291460
  16.8 12.9 %collective-permute-start.4 = (f32[1,768]{1,0:T(1,128)S(1)}, f32[1,768]{1,0:T(1,128)S(1)}, u32[]{:S(2)}, u32[]{:S(2)}) collective-permute-start(f32[1,768]{1,0:T(1,128)S(1)} %psum.7.sums.m0), channel_id=1, source_target_pairs={{0,1},{1,0},{2,3},{3,2},{4,5},{5,4},{6,7},{7,6},{8,9},{9,8},{10,11... | collective-permute-start | bytes 9224 | tf_op jit(solution)/shard_map/ppermute | solution.py:371
  20.0 12.7 %collective-permute-start.5 = (f32[1,768]{1,0:T(1,128)S(1)}, f32[1,768]{1,0:T(1,128)S(1)}, u32[]{:S(2)}, u32[]{:S(2)}) collective-permute-start(f32[1,768]{1,0:T(1,128)S(1)} %psum.7.sums.m0), channel_id=1, source_target_pairs={{0,2},{1,3},{2,0},{3,1},{4,6},{5,7},{6,4},{7,5},{8,10},{9,11},{10,... | collective-permute-start | bytes 9224 | tf_op jit(solution)/shard_map/ppermute | solution.py:372
  20.4 1.6 %copy-start.8 = (bf16[2048,512]{1,0:T(8,128)(2,1)S(1)}, bf16[2048,512]{1,0:T(8,128)(2,1)}, u32[]{:S(2)}) copy-start(bf16[2048,512]{1,0:T(8,128)(2,1)} %grads.1) | copy-start | bytes 6291460
  23.1 2.0 %copy-start.2 = (bf16[2048,1024]{1,0:T(8,128)(2,1)}, bf16[2048,1024]{1,0:T(8,128)(2,1)S(1)}, u32[]{:S(2)}) copy-start(bf16[2048,1024]{1,0:T(8,128)(2,1)S(1)} %get-tuple-element.68.ow) | copy-start | bytes 12582916
  25.1 1.4 %copy-start.6 = (f32[2048,256]{1,0:T(8,128)}, f32[2048,256]{1,0:T(8,128)S(1)}, u32[]{:S(2)}) copy-start(f32[2048,256]{1,0:T(8,128)S(1)} %get-tuple-element.82.wide) | copy-start | bytes 6291460
  26.5 1.0 copy-start.9
  27.5 1.0 copy-start.11
  28.6 21.0 %collective-permute-start.3 = (f32[1,768]{1,0:T(1,128)S(1)}, f32[1,768]{1,0:T(1,128)S(1)}, u32[]{:S(2)}, u32[]{:S(2)}) collective-permute-start(f32[1,768]{1,0:T(1,128)S(1)} %psum.7.sums.m0), channel_id=1, source_target_pairs={{0,4},{4,0},{1,5},{5,1},{2,6},{6,2},{3,7},{7,3},{8,12},{12,8},{9,1... | collective-permute-start | bytes 9224 | tf_op jit(solution)/shard_map/ppermute | solution.py:386
  29.0 28.8 %collective-permute-start.6 = (bf16[2048,256]{1,0:T(8,128)(2,1)}, bf16[2048,256]{1,0:T(8,128)(2,1)S(1)}, u32[]{:S(2)}, u32[]{:S(2)}) collective-permute-start(bf16[2048,256]{1,0:T(8,128)(2,1)} %collective-permute-done.near), channel_id=1, source_target_pairs={{1,2},{2,1},{5,6},{6,5},{9,10},{10,9},{13,14},{14,13},{17,18},{18,... | collective-permute-start | bytes 3145736 | tf_op jit(solution)/shard_map/ppermute | solution.py:388
  29.7 30.3 %collective-permute-start.2 = (bf16[2048,256]{1,0:T(8,128)(2,1)}, bf16[2048,256]{1,0:T(8,128)(2,1)S(1)}, u32[]{:S(2)}, u32[]{:S(2)}) collective-permute-start(bf16[2048,256]{1,0:T(8,128)(2,1)} %collective-permute-done.1.mid1), channel_id=1, source_target_pairs={{1,0},{2,3},{5,4},{6,7},{9,8},{10,11},{13,12},{14,15},{17,16},{18,... | collective-permute-start | bytes 3145736 | tf_op jit(solution)/shard_map/ppermute | solution.py:387
  32.7 25.1 %collective-permute-start.8 = (f32[1,768]{1,0:T(1,128)S(1)}, f32[1,768]{1,0:T(1,128)S(1)}, u32[]{:S(2)}, u32[]{:S(2)}) collective-permute-start(f32[1,768]{1,0:T(1,128)S(1)} %psum.7.sums.m0), channel_id=1, source_target_pairs={{0,3},{1,2},{2,1},{3,0},{4,7},{5,6},{6,5},{7,4},{8,11},{9,10},{10,... | collective-permute-start | bytes 9224 | tf_op jit(solution)/shard_map/ppermute | solution.py:385
  49.6 25.0 %collective-permute-start.14 = (bf16[2048,256]{1,0:T(8,128)(2,1)}, bf16[2048,256]{1,0:T(8,128)(2,1)S(1)}, u32[]{:S(2)}, u32[]{:S(2)}) collective-permute-start(bf16[2048,256]{1,0:T(8,128)(2,1)} %copy-done.11), channel_id=1, source_target_pairs={{0,4},{4,0},{1,5},{5,1},{2,6},{6,2},{3,7},{7,3},{8,12},{12,8},{9,1... | collective-permute-start | bytes 3145736 | tf_op jit(solution)/shard_map/ppermute | solution.py:389
  51.4 2.8 %copy-start.3 = (bf16[2048,1024]{1,0:T(8,128)(2,1)S(1)}, bf16[2048,1024]{1,0:T(8,128)(2,1)}, u32[]{:S(2)}) copy-start(bf16[2048,1024]{1,0:T(8,128)(2,1)} %copy-done.2) | copy-start | bytes 12582916
  51.4 3.1 %copy-start.5 = (bf16[2048,256]{1,0:T(8,128)(2,1)S(1)}, bf16[2048,256]{1,0:T(8,128)(2,1)}, u32[]{:S(2)}) copy-start(bf16[2048,256]{1,0:T(8,128)(2,1)} %own_rows.3) | copy-start | bytes 3145732
  57.8 25.7 %collective-permute-start.13 = (bf16[2048,256]{1,0:T(8,128)(2,1)S(1)}, bf16[2048,256]{1,0:T(8,128)(2,1)S(1)}, u32[]{:S(2)}, u32[]{:S(2)}) collective-permute-start(bf16[2048,256]{1,0:T(8,128)(2,1)S(1)} %collective-permute-done.6.last1), channel_id=1, source_target_pairs={{1,0},{2,3},{5,4},{6,7},{9,8},{10,11},{13,12},{14,15},{17,16},{18,... | collective-permute-start | bytes 3145736 | tf_op jit(solution)/shard_map/ppermute | solution.py:406
  60.0 11.2 %copy-start.10 = (bf16[2048,256]{1,0:T(8,128)(2,1)S(1)}, bf16[2048,256]{1,0:T(8,128)(2,1)}, u32[]{:S(2)}) copy-start(bf16[2048,256]{1,0:T(8,128)(2,1)} %copy-done.9) | copy-start | bytes 3145732
  60.1 14.6 %copy-start.7 = (f32[2048,256]{1,0:T(8,128)S(1)}, f32[2048,256]{1,0:T(8,128)}, u32[]{:S(2)}) copy-start(f32[2048,256]{1,0:T(8,128)} %copy-done.6) | copy-start | bytes 6291460
  66.1 1.5 %collective-permute-start.10 = (bf16[1,256,384]{2,1,0:T(8,128)(2,1)S(1)}, bf16[1,256,384]{2,1,0:T(8,128)(2,1)S(1)}, u32[]{:S(2)}, u32[]{:S(2)}) collective-permute-start(bf16[1,256,384]{2,1,0:T(8,128)(2,1)S(1)} %get-tuple-element.77), channel_id=1, source_target_pairs={{0,8},{8,0},{16,24},{24,16},{1,9},{9,1},{17,25},{25,17},{2,10},{10... | collective-permute-start | bytes 589832 | tf_op jit(solution)/shard_map/ppermute | solution.py:427
  66.2 1.7 %collective-permute-start.11 = (bf16[1,256,384]{2,1,0:T(8,128)(2,1)S(1)}, bf16[1,256,384]{2,1,0:T(8,128)(2,1)S(1)}, u32[]{:S(2)}, u32[]{:S(2)}) collective-permute-start(bf16[1,256,384]{2,1,0:T(8,128)(2,1)S(1)} %get-tuple-element.78), channel_id=1, source_target_pairs={{0,8},{8,0},{16,24},{24,16},{1,9},{9,1},{17,25},{25,17},{2,10},{10... | collective-permute-start | bytes 589832 | tf_op jit(solution)/shard_map/ppermute | solution.py:427
  66.7 1.5 %collective-permute-start.12 = (bf16[1,256,384]{2,1,0:T(8,128)(2,1)S(1)}, bf16[1,256,384]{2,1,0:T(8,128)(2,1)S(1)}, u32[]{:S(2)}, u32[]{:S(2)}) collective-permute-start(bf16[1,256,384]{2,1,0:T(8,128)(2,1)S(1)} %get-tuple-element.79), channel_id=1, source_target_pairs={{0,8},{8,0},{16,24},{24,16},{1,9},{9,1},{17,25},{25,17},{2,10},{10... | collective-permute-start | bytes 589832 | tf_op jit(solution)/shard_map/ppermute | solution.py:427
  67.6 1.4 %collective-permute-start.9 = (bf16[1,256,384]{2,1,0:T(8,128)(2,1)S(1)}, bf16[1,256,384]{2,1,0:T(8,128)(2,1)S(1)}, u32[]{:S(2)}, u32[]{:S(2)}) collective-permute-start(bf16[1,256,384]{2,1,0:T(8,128)(2,1)S(1)} %get-tuple-element.76), channel_id=1, source_target_pairs={{0,8},{8,0},{16,24},{24,16},{1,9},{9,1},{17,25},{25,17},{2,10},{10... | collective-permute-start | bytes 589832 | tf_op jit(solution)/shard_map/ppermute | solution.py:427
  69.7 13.7 %collective-permute-start.15 = (bf16[256,768]{1,0:T(8,128)(2,1)S(1)}, bf16[256,768]{1,0:T(8,128)(2,1)S(1)}, u32[]{:S(2)}, u32[]{:S(2)}) collective-permute-start(bf16[256,768]{1,0:T(8,128)(2,1)S(1)} %shard_map.75), channel_id=1, source_target_pairs={{0,16},{8,24},{16,0},{24,8},{1,17},{9,25},{17,1},{25,9},{2,18},{10... | collective-permute-start | bytes 1179656 | tf_op jit(solution)/shard_map/ppermute | solution.py:432
  71.3 25.4 %collective-permute-start.24 = (bf16[2048,256]{1,0:T(8,128)(2,1)S(1)}, bf16[2048,256]{1,0:T(8,128)(2,1)S(1)}, u32[]{:S(2)}, u32[]{:S(2)}) collective-permute-start(bf16[2048,256]{1,0:T(8,128)(2,1)S(1)} %copy-done.10), channel_id=1, source_target_pairs={{0,4},{4,0},{1,5},{5,1},{2,6},{6,2},{3,7},{7,3},{8,12},{12,8},{9,1... | collective-permute-start | bytes 3145736 | tf_op jit(solution)/shard_map/ppermute | solution.py:407
  76.7 1.4 %collective-permute-start.16 = (bf16[1,256,256]{2,1,0:T(8,128)(2,1)S(1)}, bf16[1,256,256]{2,1,0:T(8,128)(2,1)S(1)}, u32[]{:S(2)}, u32[]{:S(2)}) collective-permute-start(bf16[1,256,256]{2,1,0:T(8,128)(2,1)S(1)} %get-tuple-element.87), channel_id=1, source_target_pairs={{0,8},{8,0},{16,24},{24,16},{1,9},{9,1},{17,25},{25,17},{2,10},{10... | collective-permute-start | bytes 393224 | tf_op jit(solution)/shard_map/ppermute | solution.py:427
  78.7 4.7 %collective-permute-start.17 = (bf16[256,128]{1,0:T(8,128)(2,1)S(1)}, bf16[256,128]{1,0:T(8,128)(2,1)S(1)}, u32[]{:S(2)}, u32[]{:S(2)}) collective-permute-start(bf16[256,128]{1,0:T(8,128)(2,1)S(1)} %shard_map.77), channel_id=1, source_target_pairs={{0,16},{8,24},{16,0},{24,8},{1,17},{9,25},{17,1},{25,9},{2,18},{10... | collective-permute-start | bytes 196616 | tf_op jit(solution)/shard_map/ppermute | solution.py:432
  86.8 2.5 %collective-permute-start.18 = (bf16[1,256,512]{2,1,0:T(8,128)(2,1)S(1)}, bf16[1,256,512]{2,1,0:T(8,128)(2,1)S(1)}, u32[]{:S(2)}, u32[]{:S(2)}) collective-permute-start(bf16[1,256,512]{2,1,0:T(8,128)(2,1)S(1)} %get-tuple-element.94), channel_id=1, source_target_pairs={{0,8},{8,0},{16,24},{24,16},{1,9},{9,1},{17,25},{25,17},{2,10},{10... | collective-permute-start | bytes 786440 | tf_op jit(solution)/shard_map/ppermute | solution.py:427
  86.9 2.5 %collective-permute-start.20 = (bf16[1,256,512]{2,1,0:T(8,128)(2,1)S(1)}, bf16[1,256,512]{2,1,0:T(8,128)(2,1)S(1)}, u32[]{:S(2)}, u32[]{:S(2)}) collective-permute-start(bf16[1,256,512]{2,1,0:T(8,128)(2,1)S(1)} %get-tuple-element.96), channel_id=1, source_target_pairs={{0,8},{8,0},{16,24},{24,16},{1,9},{9,1},{17,25},{25,17},{2,10},{10... | collective-permute-start | bytes 786440 | tf_op jit(solution)/shard_map/ppermute | solution.py:427
  87.4 1.7 %collective-permute-start.19 = (bf16[1,256,384]{2,1,0:T(8,128)(2,1)S(1)}, bf16[1,256,384]{2,1,0:T(8,128)(2,1)S(1)}, u32[]{:S(2)}, u32[]{:S(2)}) collective-permute-start(bf16[1,256,384]{2,1,0:T(8,128)(2,1)S(1)} %get-tuple-element.95), channel_id=1, source_target_pairs={{0,8},{8,0},{16,24},{24,16},{1,9},{9,1},{17,25},{25,17},{2,10},{10... | collective-permute-start | bytes 589832 | tf_op jit(solution)/shard_map/ppermute | solution.py:427
  87.4 1.9 %collective-permute-start.21 = (bf16[1,256,384]{2,1,0:T(8,128)(2,1)S(1)}, bf16[1,256,384]{2,1,0:T(8,128)(2,1)S(1)}, u32[]{:S(2)}, u32[]{:S(2)}) collective-permute-start(bf16[1,256,384]{2,1,0:T(8,128)(2,1)S(1)} %get-tuple-element.97), channel_id=1, source_target_pairs={{0,8},{8,0},{16,24},{24,16},{1,9},{9,1},{17,25},{25,17},{2,10},{10... | collective-permute-start | bytes 589832 | tf_op jit(solution)/shard_map/ppermute | solution.py:427
  90.0 12.8 %collective-permute-start.25 = (bf16[256,896]{1,0:T(8,128)(2,1)S(1)}, bf16[256,896]{1,0:T(8,128)(2,1)S(1)}, u32[]{:S(2)}, u32[]{:S(2)}) collective-permute-start(bf16[256,896]{1,0:T(8,128)(2,1)S(1)} %shard_map.79), channel_id=1, source_target_pairs={{0,16},{8,24},{16,0},{24,8},{1,17},{9,25},{17,1},{25,9},{2,18},{10... | collective-permute-start | bytes 1376264 | tf_op jit(solution)/shard_map/ppermute | solution.py:432
  92.5 4.5 %collective-permute-start.23 = (bf16[256,128]{1,0:T(8,128)(2,1)S(1)}, bf16[256,128]{1,0:T(8,128)(2,1)S(1)}, u32[]{:S(2)}, u32[]{:S(2)}) collective-permute-start(bf16[256,128]{1,0:T(8,128)(2,1)S(1)} %shard_map.81), channel_id=1, source_target_pairs={{0,8},{8,0},{16,24},{24,16},{1,9},{9,1},{17,25},{25,17},{2,10},{10... | collective-permute-start | bytes 196616 | tf_op jit(solution)/shard_map/ppermute | solution.py:444
  93.3 3.8 %collective-permute-start.22 = (bf16[256,768]{1,0:T(8,128)(2,1)S(1)}, bf16[256,768]{1,0:T(8,128)(2,1)S(1)}, u32[]{:S(2)}, u32[]{:S(2)}) collective-permute-start(bf16[256,768]{1,0:T(8,128)(2,1)S(1)} %shard_map.80), channel_id=1, source_target_pairs={{0,8},{8,0},{16,24},{24,16},{1,9},{9,1},{17,25},{25,17},{2,10},{10... | collective-permute-start | bytes 1179656 | tf_op jit(solution)/shard_map/ppermute | solution.py:444
  99.1 1.6 %collective-permute-start.26 = (bf16[2,256,256]{2,1,0:T(8,128)(2,1)S(1)}, bf16[2,256,256]{2,1,0:T(8,128)(2,1)S(1)}, u32[]{:S(2)}, u32[]{:S(2)}) collective-permute-start(bf16[2,256,256]{2,1,0:T(8,128)(2,1)S(1)} %get-tuple-element.110), channel_id=1, source_target_pairs={{0,8},{8,0},{16,24},{24,16},{1,9},{9,1},{17,25},{25,17},{2,10},{10... | collective-permute-start | bytes 786440 | tf_op jit(solution)/shard_map/ppermute | solution.py:412
  101.3 5.6 %collective-permute-start.31 = (bf16[256,256]{1,0:T(8,128)(2,1)S(1)}, bf16[256,256]{1,0:T(8,128)(2,1)S(1)}, u32[]{:S(2)}, u32[]{:S(2)}) collective-permute-start(bf16[256,256]{1,0:T(8,128)(2,1)S(1)} %shard_map.84), channel_id=1, source_target_pairs={{0,16},{8,24},{16,0},{24,8},{1,17},{9,25},{17,1},{25,9},{2,18},{10... | collective-permute-start | bytes 393224 | tf_op jit(solution)/shard_map/ppermute | solution.py:419
  103.5 4.1 %collective-permute-start.27 = (bf16[256,256]{1,0:T(8,128)(2,1)S(1)}, bf16[256,256]{1,0:T(8,128)(2,1)S(1)}, u32[]{:S(2)}, u32[]{:S(2)}) collective-permute-start(bf16[256,256]{1,0:T(8,128)(2,1)S(1)} %get-tuple-element.112), channel_id=1, source_target_pairs={{0,8},{8,0},{16,24},{24,16},{1,9},{9,1},{17,25},{25,17},{2,10},{10... | collective-permute-start | bytes 393224 | tf_op jit(solution)/shard_map/ppermute | solution.py:444
  103.6 4.1 %collective-permute-start.28 = (bf16[256,256]{1,0:T(8,128)(2,1)S(1)}, bf16[256,256]{1,0:T(8,128)(2,1)S(1)}, u32[]{:S(2)}, u32[]{:S(2)}) collective-permute-start(bf16[256,256]{1,0:T(8,128)(2,1)S(1)} %get-tuple-element.113), channel_id=1, source_target_pairs={{0,8},{8,0},{16,24},{24,16},{1,9},{9,1},{17,25},{25,17},{2,10},{10... | collective-permute-start | bytes 393224 | tf_op jit(solution)/shard_map/ppermute | solution.py:444
  104.1 3.6 %collective-permute-start.29 = (bf16[256,256]{1,0:T(8,128)(2,1)S(1)}, bf16[256,256]{1,0:T(8,128)(2,1)S(1)}, u32[]{:S(2)}, u32[]{:S(2)}) collective-permute-start(bf16[256,256]{1,0:T(8,128)(2,1)S(1)} %get-tuple-element.114), channel_id=1, source_target_pairs={{0,8},{8,0},{16,24},{24,16},{1,9},{9,1},{17,25},{25,17},{2,10},{10... | collective-permute-start | bytes 393224 | tf_op jit(solution)/shard_map/ppermute | solution.py:444
  104.1 3.5 %collective-permute-start.30 = (bf16[256,128]{1,0:T(8,128)(2,1)S(1)}, bf16[256,128]{1,0:T(8,128)(2,1)S(1)}, u32[]{:S(2)}, u32[]{:S(2)}) collective-permute-start(bf16[256,128]{1,0:T(8,128)(2,1)S(1)} %get-tuple-element.115), channel_id=1, source_target_pairs={{0,8},{8,0},{16,24},{24,16},{1,9},{9,1},{17,25},{25,17},{2,10},{10... | collective-permute-start | bytes 196616 | tf_op jit(solution)/shard_map/ppermute | solution.py:444

commit v4 on v3

--- a/solution.py
+++ b/solution.py
@@ -13,15 +13,15 @@
 SMEM = pl.BlockSpec(memory_space=pltpu.SMEM)
 MID, LOW, CORE, STRAIGHT, TABLE = 0, 1, 2, 3, 4
 MEAN_COST, FAR_COST, EARLY_COST, FIRST_COST, LAST_COST = 6, 3, 4, 0, 4
-WEIGH_COST, FOLD_COST = 12, 6
-
-
-def call(kernel, outs, *args, scratch=(), limit=24, cost=0):
+WEIGH_COST, HOPS = 12, 4
+
+
+def call(kernel, outs, *args, scratch=(), limit=24, cost=0, out_spec=VMEM):
     return pl.pallas_call(
         kernel,
         out_shape=[jax.ShapeDtypeStruct(s, d) for s, d in outs],
         in_specs=[SMEM if a.dtype == jnp.int32 else VMEM for a in args],
-        out_specs=[VMEM] * len(outs),
+        out_specs=[out_spec] * len(outs),
         scratch_shapes=list(scratch),
         compiler_params=pltpu.CompilerParams(vmem_limit_bytes=limit * 2**20),
         cost_estimate=pl.CostEstimate(
@@ -55,7 +55,7 @@
 def own_kernel(count, cuts, cols, grads, energy, sums, out, wide, *pieces):
     width = cols.shape[1]
     lanes = wide.shape[1]
-    d = centred(cols[...], sums[:, -width:] / count)
+    d = centred(cols[...], sums[:, -width:] * (1 / count))
     out[:, :width] = d
     spread = jnp.broadcast_to(energy[...], wide.shape)
     wide[...] = spread
@@ -105,9 +105,9 @@
 
 def mean_kernel(count, sums, m1, m2, out, near_mean, next_mean):
     rw = near_mean.shape[1]
-    out[...] = sums[:, -out.shape[1] :] / count
-    near_mean[...] = m1[:, :rw] / count
-    next_mean[...] = m2[:, :rw] / count
+    out[...] = sums[:, -out.shape[1] :] * (1 / count)
+    near_mean[...] = m1[:, :rw] * (1 / count)
+    next_mean[...] = m2[:, :rw] * (1 / count)
 
 
 def far_kernel(raw, mean, out):
@@ -134,8 +134,8 @@
 
     @pl.when(info[MID] == 1)
     def _():
-        own = centred(own_rows[...], m0[:, :rw] / count)
-        group(centred(mid1[...], m3[:, :rw] / count), own)
+        own = centred(own_rows[...], m0[:, :rw] * (1 / count))
+        group(centred(mid1[...], m3[:, :rw] * (1 / count)), own)
 
     @pl.when(info[MID] == 0)
     def _():
@@ -156,7 +156,7 @@
 
     @pl.when(info[MID] == 0)
     def _():
-        second[...] = centred(own_rows[...], m0[:, :rw] / count)
+        second[...] = centred(own_rows[...], m0[:, :rw] * (1 / count))
 
     held[...] = products(second[...], (ow, far))
 
@@ -186,7 +186,7 @@
 
     @pl.when(info[MID] == 0)
     def _():
-        tile[...] = centred(last2[...], m3[:, :rw] / count)
+        tile[...] = centred(last2[...], m3[:, :rw] * (1 / count))
 
     result = products(tile[...], (ow, far, chunk))
     before = jnp.concatenate((held[...], held_chunk[...]), axis=1)
@@ -269,64 +269,85 @@
     gots, got_x, outs = refs[:count], refs[count], refs[count + 1 :]
     width = keep.shape[2]
     value = (columns(keep, gots, width // 2, width) + got_x[...].astype(F32)).astype(BF)
-    start = 0
-    for out in outs:
-        out[...] = value[:, start : start + out.shape[1]]
-        start += out.shape[1]
-
-
-def fold_kernel(count, info, keep, got, *refs):
-    refs[-1][...] = total(keep, (got,), refs[:-1], info[TABLE]).T / count
+    rows = value.shape[0] // len(outs)
+    for i, out in enumerate(outs):
+        out[...] = value[i * rows : (i + 1) * rows]
 
 
 def gather_kernel(count, shapes, info, *refs):
-    *refs, chunk, ham, corr = refs
-    cw = ham.shape[1] // 2
+    *refs, ham_out, corr_out, ham, corr, sems = refs
+    rows, cw = ham.shape[0], ham.shape[1] // 2
     pos = info[TABLE]
-
-    def put(out, near, start, value):
+    step = rows // HOPS
+
+    def put(out, near, at, start, value):
         @pl.when((info[STRAIGHT] == 1) == near)
         def _():
-            out[:, start : start + value.shape[1]] = value
+            out[at, start : start + value.shape[1]] = value
 
         @pl.when((info[STRAIGHT] == 1) != near)
         def _():
-            out[:, cw + start : cw + start + value.shape[1]] = value
+            out[at, cw + start : cw + start + value.shape[1]] = value
 
     def spans(refs, start=0):
         for ref in refs:
             yield start, start + ref.shape[-1], ref
             start += ref.shape[-1]
 
-    put(ham, False, cw - chunk.shape[1], chunk[...])
-    at = 0
+    def place(parts, at, a, b, value):
+        start = 0
+        for size, (out, near, to) in parts:
+            lo, hi = max(a, start), min(b, start + size)
+            if lo < hi:
+                some = value[:, lo - a : hi - a] * (1 / count)
+                put((ham, corr)[out], near, at, to + lo - start, some)
+            start += size
+
+    def fill(k, keep, gots, others, turned, i, parts):
+        at, width = slice(k * step, (k + 1) * step), keep.shape[2]
+        for a, b, got in spans(gots):
+            b = min(b, width // 2) if turned else b
+            if a < b:
+                value = keep[i, at, a:b].astype(F32) + got[i, at, : b - a].astype(F32)
+                for other in others[:1] if turned else others:
+                    value = value + other[at, a:b].astype(F32)
+                place(parts, at, a, b, value)
+        if turned:
+            homes = others[1:]
+            home = homes[k * len(homes) // HOPS]
+            start = k * step % home.shape[0]
+            place(parts, at, width // 2, width, home[start : start + step].astype(F32))
+
+    def copies(k):
+        at = slice(k * step, (k + 1) * step)
+        return [
+            pltpu.make_async_copy(ham.at[at], ham_out.at[at], sems.at[k, 0]),
+            pltpu.make_async_copy(corr.at[at], corr_out.at[at], sems.at[k, 1]),
+        ]
+
+    start, messages = 0, []
     for n_gots, n_others, turned, first, pieces, parts in shapes:
-        keep, gots = refs[at], refs[at + 1 : at + 1 + n_gots]
-        others = refs[at + 1 + n_gots : at + 1 + n_gots + n_others]
-        at += 1 + n_gots + n_others
-        width = keep.shape[2]
-
-        def place(a, b, value):
-            start = 0
-            for size, (out, near, to) in parts:
-                lo, hi = max(a, start), min(b, start + size)
-                if lo < hi:
-                    put((ham, corr)[out], near, to + lo - start, value[:, lo - a : hi - a] / count)
-                start += size
-
-        @pl.when((pos >= first) & (pos < first + pieces))
-        def _():
-            i = pos - first
-            for a, b, got in spans(gots):
-                b = min(b, width // 2) if turned else b
-                if a < b:
-                    value = keep[i, :, a:b].astype(F32) + got[i, :, : b - a].astype(F32)
-                    for other in others[:1] if turned else others:
-                        value = value + other[:, a:b].astype(F32)
-                    place(a, b, value)
-            if turned:
-                for a, b, home in spans(others[1:], width // 2):
-                    place(a, b, home[...].astype(F32))
+        keep, gots = refs[start], refs[start + 1 : start + 1 + n_gots]
+        others = refs[start + 1 + n_gots : start + 1 + n_gots + n_others]
+        start += 1 + n_gots + n_others
+        if parts[0][0] is None:
+            out, near, to = parts[0][1]
+            value = total(keep, gots, others, pos).T * (1 / count)
+            put((ham, corr)[out], near, slice(None), to, value)
+        else:
+            messages.append((first, pieces, keep, gots, others, turned, parts))
+    for k in range(HOPS):
+        for first, pieces, keep, gots, others, turned, parts in messages:
+
+            @pl.when((pos >= first) & (pos < first + pieces))
+            def _():
+                fill(k, keep, gots, others, turned, pos - first, parts)
+
+        for copy in copies(k):
+            copy.start()
+    for k in range(HOPS):
+        for copy in copies(k):
+            copy.wait()
 
 
 def per_device(o_rows, o_cols, grad_energy, energy):
@@ -381,7 +402,7 @@
         o_cols, grad_energy, column, m0,
     )
 
-    near, mid1, ow, m0, *grads = lax.optimization_barrier((near, mid1, ow, m0, *grads))
+    near, mid1, m1, ow, m0, *grads = lax.optimization_barrier((near, mid1, m1, ow, m0, *grads))
     m3 = lax.ppermute(m0, "pcol", [(0, 3), (1, 2), (2, 1), (3, 0)])
     far_sums = lax.ppermute(m0, "prow", flip)
     mid2 = lax.ppermute(mid1, "pcol", ends)
@@ -433,12 +454,12 @@
         messages.append([keep, gots, [got_x], True, first, 1, parts])
         return sent
 
-    def bring_home(message, sizes, *earlier):
+    def bring_home(message, n_parts, *earlier):
         keep, gots, others, turned, *_ = message
         if turned:
             homes = call(
                 functools.partial(home_kernel, len(gots)),
-                [((keep.shape[1], size), BF) for size in sizes],
+                [((keep.shape[1] // n_parts, keep.shape[2] // 2), BF)] * n_parts,
                 info, keep, *gots, after(others[0], *earlier),
             )
             others += [lax.ppermute(h, "walker", other_core) for h in homes]
@@ -481,8 +502,8 @@
     )
     sent = reduce_rows(sends, l_keep, per, parts + chunk_part)
 
-    bring_home(messages[0], [3 * cw // 2], *sent)
-    bring_home(messages[1], [n // 2], *sent)
+    bring_home(messages[0], 1, *sent)
+    bring_home(messages[1], 1, *sent)
     n = widths[1]
     (right,) = call(
         functools.partial(weigh_kernel, cuts[1]),
@@ -498,15 +519,8 @@
         [((2 * per, n, piece), BF)] * 2,
         info, early, second, last, after(right, *sent),
     )
-    sent = reduce([send], keep, 0, 2 * per, None)
-    keep, gots, others, *_ = messages.pop()
-    (folded,) = call(
-        functools.partial(fold_kernel, count),
-        [((piece, n), F32)],
-        info, keep, *gots, *others,
-        cost=FOLD_COST,
-    )
-    bring_home(messages[2], [min(256, size - a) for a in range(0, size, 256)], *sent)
+    sent = reduce([send], keep, 0, 2 * per, [(None, (0, False, cuts[1]))])
+    bring_home(messages[2], HOPS, *sent)
 
     flat, shapes = [], []
     for k, g, o, *what in messages:
@@ -515,7 +529,9 @@
     return call(
         functools.partial(gather_kernel, count, shapes),
         [((piece, 2 * cw), F32)] * 2,
-        info, *flat, folded,
+        info, *flat,
+        scratch=[pltpu.VMEM((piece, 2 * cw), F32)] * 2 + [pltpu.SemaphoreType.DMA((HOPS, 2))],
+        out_spec=pl.BlockSpec(memory_space=pl.ANY),
     )
 
 

time: 110 us -> 110 us (level)
    pallas_call x20 -> x19, Pallas kernels: 28.3 us -> 27.5 us  [call(): pl.pallas_call(kernel, out_shape=[jax.ShapeDtypeStruct(s, d) for s, d in...]
  transfers between devices with their start and end apart: 32 -> 32, of which waited for: 16 -> 20; matrix products, arithmetic and copies ran while one was open for 1% -> 1% of each run, Pallas kernels for 24% -> 23%
where the time goes in v4:
time: 110 us; the launch traced here: 109 us
  waiting for transfers between devices  32.1 us (29%)
  starting transfers between devices  30.2 us (27%)
  Pallas kernels  27.5 us (25%)
  local copies, waits for them, and re-layouts  11.9 us (11%)
  blocking collectives  6.55 us (6%)
    pallas_call x19, Pallas kernels, call(): pl.pallas_call(kernel, out_shape=[jax.ShapeDtypeStruct(s, d) for s, d in...  27.5 us
    ppermute x1, waiting for transfers between devices, per_device(): far_sums = lax.ppermute(m0, 'prow', flip)  14.1 us
    unnamed x26, local copies, waits for them, and re-layouts  10.7 us
    psum x1, blocking collectives, per_device(): m0 = lax.psum(sums, 'walker')  6.55 us
    ppermute x3, starting transfers between devices, reduce_rows(): got_x = lax.ppermute(sent[0], 'walker', [(v, v ^ 2) for v in range(4)])  5.78 us
    ppermute x9, waiting for transfers between devices, reduce_rows(): gots = [lax.ppermute(send, 'walker', other_core) for send in sends]  4.94 us
    ppermute x1, starting transfers between devices, per_device(): m1 = lax.ppermute(m0, 'pcol', outer)  3.21 us
    ppermute x1, starting transfers between devices, per_device(): far_raw = lax.ppermute(o_cols, 'prow', flip)  3.03 us
  transfers between devices with their start and end apart: 32, of which 20 were waited for; matrix products, arithmetic and copies ran while one was open for 1% of the time, Pallas kernels for 23%

profile of v4, /device:TPU:0, one launch (start us, length us, event | category | flops | bytes accessed | tf_op | source)
XLA Modules:
  0.0 109.3 jit_solution(10706304737114529304)
XLA Ops:
  0.6 3.0 %collective-permute-start.7 = (bf16[2048,512]{1,0:T(8,128)(2,1)}, bf16[2048,512]{1,0:T(8,128)(2,1)}, u32[]{:S(2)}, u32[]{:S(2)}) collective-permute-start(bf16[2048,512]{1,0:T(8,128)(2,1)} %cols.3), channel_id=1, source_target_pairs={{0,4},{4,0},{1,5},{5,1},{2,6},{6,2},{3,7},{7,3},{8,12},{12,8},{9,1... | collective-permute-start | bytes 6291464 | tf_op jit(solution)/shard_map/ppermute | solution.py:386
  3.7 1.6 %collective-permute-start = (bf16[2048,256]{1,0:T(8,128)(2,1)}, bf16[2048,256]{1,0:T(8,128)(2,1)}, u32[]{:S(2)}, u32[]{:S(2)}) collective-permute-start(bf16[2048,256]{1,0:T(8,128)(2,1)} %own_rows.3), channel_id=1, source_target_pairs={{0,1},{1,0},{2,3},{3,2},{4,5},{5,4},{6,7},{7,6},{8,9},{9,8},{10,11... | collective-permute-start | bytes 3145736 | tf_op jit(solution)/shard_map/ppermute | solution.py:387
  5.2 1.6 %collective-permute-start.1 = (bf16[2048,256]{1,0:T(8,128)(2,1)}, bf16[2048,256]{1,0:T(8,128)(2,1)}, u32[]{:S(2)}, u32[]{:S(2)}) collective-permute-start(bf16[2048,256]{1,0:T(8,128)(2,1)} %own_rows.3), channel_id=1, source_target_pairs={{1,2},{2,1},{5,6},{6,5},{9,10},{10,9},{13,14},{14,13},{17,18},{18,... | collective-permute-start | bytes 3145736 | tf_op jit(solution)/shard_map/ppermute | solution.py:388
  6.9 1.6 %copy-done = bf16[2048,512]{1,0:T(8,128)(2,1)S(1)} copy-done((bf16[2048,512]{1,0:T(8,128)(2,1)S(1)}, bf16[2048,512]{1,0:T(8,128)(2,1)}, u32[]{:S(2)}) %copy-start) | copy-done | bytes 2097176
  8.5 1.2 %copy-done.4 = bf16[2048,256]{1,0:T(8,128)(2,1)S(1)} copy-done((bf16[2048,256]{1,0:T(8,128)(2,1)S(1)}, bf16[2048,256]{1,0:T(8,128)(2,1)}, u32[]{:S(2)}) %copy-start.4) | copy-done | bytes 1048600
  9.7 0.5 shard_map.68
  10.2 6.6 %psum.7.sums.m0 = f32[1,768]{1,0:T(1,128)S(1)} all-reduce(f32[1,768]{1,0:T(1,128)S(1)} %shard_map.68), channel_id=1, replica_groups=mesh['walker'=4,'prow'=2,'pcol'=4] {'walker'}, use_global_device_ids=true, to_apply=%region_0.1 | all-reduce | flops 768 | bytes 6144 | tf_op jit(solution)/shard_map/psum | solution.py:391
  16.8 3.2 %collective-permute-start.2 = (f32[1,768]{1,0:T(1,128)S(1)}, f32[1,768]{1,0:T(1,128)S(1)}, u32[]{:S(2)}, u32[]{:S(2)}) collective-permute-start(f32[1,768]{1,0:T(1,128)S(1)} %psum.7.sums.m0), channel_id=1, source_target_pairs={{0,1},{1,0},{2,3},{3,2},{4,5},{5,4},{6,7},{7,6},{8,9},{9,8},{10,11... | collective-permute-start | bytes 9224 | tf_op jit(solution)/shard_map/ppermute | solution.py:392
  20.0 0.4 copy.7.energy
  20.4 1.6 %copy-done.8 = bf16[2048,512]{1,0:T(8,128)(2,1)S(1)} copy-done((bf16[2048,512]{1,0:T(8,128)(2,1)S(1)}, bf16[2048,512]{1,0:T(8,128)(2,1)}, u32[]{:S(2)}) %copy-start.8) | copy-done | bytes 2097176
  22.0 1.2 %shard_map.69 = (bf16[2048,1024]{1,0:T(8,128)(2,1)S(1)}, f32[2048,256]{1,0:T(8,128)S(1)}, bf16[2048,256]{1,0:T(8,128)(2,1)S(1)}, bf16[2048,256]{1,0:T(8,128)(2,1)S(1)}) custom-call(bf16[2048,512]{1,0:T(8,128)(2,1)S(1)} %copy-done.1, bf16[2048,512]{1,0:T(8,128)(2,1)S(1)} %copy-done.8, f32[2048,1]{1,0:T(8,128)S(1)} %copy.7.energy, f32[1,768]{1,0:T(1,128)S(1)} %psum.7.sums.m0), custom_call_target="tpu_custom_call" | custom-call | tf_op jit(solution)/shard_map/pallas_call | solution.py:20
  23.2 2.0 %copy-done.2 = bf16[2048,1024]{1,0:T(8,128)(2,1)} copy-done((bf16[2048,1024]{1,0:T(8,128)(2,1)}, bf16[2048,1024]{1,0:T(8,128)(2,1)S(1)}, u32[]{:S(2)}) %copy-start.2) | copy-done | bytes 4194328
  25.1 1.4 %copy-done.6 = f32[2048,256]{1,0:T(8,128)} copy-done((f32[2048,256]{1,0:T(8,128)}, f32[2048,256]{1,0:T(8,128)S(1)}, u32[]{:S(2)}) %copy-start.6) | copy-done | bytes 2097176
  26.5 1.0 copy-done.9
  27.5 1.0 copy-done.11
  28.6 0.4 collective-permute-start.4
  29.0 0.7 collective-permute-start.6
  29.8 1.3 %collective-permute-start.3 = (bf16[2048,256]{1,0:T(8,128)(2,1)}, bf16[2048,256]{1,0:T(8,128)(2,1)S(1)}, u32[]{:S(2)}, u32[]{:S(2)}) collective-permute-start(bf16[2048,256]{1,0:T(8,128)(2,1)} %collective-permute-done.1.mid1), channel_id=1, source_target_pairs={{1,0},{2,3},{5,4},{6,7},{9,8},{10,11},{13,12},{14,15},{17,16},{18,... | collective-permute-start | bytes 3145736 | tf_op jit(solution)/shard_map/ppermute | solution.py:408
  31.1 0.7 dynamic-slice_bitcast_fusion
  31.8 0.8 collective-permute-done.5.m2
  32.7 2.9 %collective-permute-start.8 = (f32[1,768]{1,0:T(1,128)S(1)}, f32[1,768]{1,0:T(1,128)S(1)}, u32[]{:S(2)}, u32[]{:S(2)}) collective-permute-start(f32[1,768]{1,0:T(1,128)S(1)} %psum.7.sums.m0), channel_id=1, source_target_pairs={{0,3},{1,2},{2,1},{3,0},{4,7},{5,6},{6,5},{7,4},{8,11},{9,10},{10,... | collective-permute-start | bytes 9224 | tf_op jit(solution)/shard_map/ppermute | solution.py:406
  35.6 14.1 %collective-permute-done.4.sums = f32[1,768]{1,0:T(1,128)S(1)} collective-permute-done((f32[1,768]{1,0:T(1,128)S(1)}, f32[1,768]{1,0:T(1,128)S(1)}, u32[]{:S(2)}, u32[]{:S(2)}) %collective-permute-start.4) | collective-permute-done | bytes 3104 | tf_op jit(solution)/shard_map/ppermute | solution.py:407
  49.6 1.7 %collective-permute-start.14 = (bf16[2048,256]{1,0:T(8,128)(2,1)}, bf16[2048,256]{1,0:T(8,128)(2,1)S(1)}, u32[]{:S(2)}, u32[]{:S(2)}) collective-permute-start(bf16[2048,256]{1,0:T(8,128)(2,1)} %copy-done.11), channel_id=1, source_target_pairs={{0,4},{4,0},{1,5},{5,1},{2,6},{6,2},{3,7},{7,3},{8,12},{12,8},{9,1... | collective-permute-start | bytes 3145736 | tf_op jit(solution)/shard_map/ppermute | solution.py:410
  51.4 2.1 %shard_map.71.far = bf16[2048,512]{1,0:T(8,128)(2,1)S(1)} custom-call(bf16[2048,512]{1,0:T(8,128)(2,1)} %collective-permute-done.7.raw, f32[1,512]{1,0:T(1,128)S(1)} %get-tuple-element.69.mean), custom_call_target="tpu_custom_call" | custom-call | flops 3449999872 | tf_op jit(solution)/shard_map/pallas_call | solution.py:20
  53.5 0.7 copy-done.3
  54.5 3.3 %shard_map.72 = (bf16[2048,256]{1,0:T(8,128)(2,1)S(1)}, bf16[256,1536]{1,0:T(8,128)(2,1)S(1)}) custom-call(s32[6]{0:T(128)S(1)} %concatenate.3.info, bf16[2048,256]{1,0:T(8,128)(2,1)S(1)} %copy-done.5, bf16[2048,256]{1,0:T(8,128)(2,1)} %collective-permute-done.near, f32[1,768]{1,0:T(1,128)S(1)} %psum.7.sums.m0, f32[1,256]{1,0:T(1,128)S(1)} %get-tuple-element.67.m1, ...), custom_call_target="tpu_custom_call" | custom-call | tf_op jit(solution)/shard_map/pallas_call | solution.py:20
  57.8 1.3 %collective-permute-start.13 = (bf16[2048,256]{1,0:T(8,128)(2,1)S(1)}, bf16[2048,256]{1,0:T(8,128)(2,1)S(1)}, u32[]{:S(2)}, u32[]{:S(2)}) collective-permute-start(bf16[2048,256]{1,0:T(8,128)(2,1)S(1)} %collective-permute-done.6.last1), channel_id=1, source_target_pairs={{1,0},{2,3},{5,4},{6,7},{9,8},{10,11},{13,12},{14,15},{17,16},{18,... | collective-permute-start | bytes 3145736 | tf_op jit(solution)/shard_map/ppermute | solution.py:427
  59.1 1.0 collective-permute-done.3.mid2
  60.0 6.0 %shard_map.73 = (bf16[1,256,1536]{2,1,0:T(8,128)(2,1)S(1)}, bf16[2048,512]{1,0:T(8,128)(2,1)S(1)}, bf16[1,256,384]{2,1,0:T(8,128)(2,1)S(1)}, bf16[1,256,384]{2,1...) custom-call(s32[6]{0:T(128)S(1)} %concatenate.3.info, ...), custom_call_target="tpu_custom_call" | custom-call | flops 4600000000 | tf_op jit(solution)/shard_map/pallas_call | solution.py:20
  66.2 0.5 collective-permute-start.11
  66.7 0.9 collective-permute-done.10.refs_1_.refs_2_
  68.2 0.9 collective-permute-done.9.refs_0_.refs_1_
  69.0 0.6 shard_map.75
  69.7 1.6 %collective-permute-start.15 = (bf16[256,768]{1,0:T(8,128)(2,1)S(1)}, bf16[256,768]{1,0:T(8,128)(2,1)S(1)}, u32[]{:S(2)}, u32[]{:S(2)}) collective-permute-start(bf16[256,768]{1,0:T(8,128)(2,1)S(1)} %shard_map.75), channel_id=1, source_target_pairs={{0,16},{8,24},{16,0},{24,8},{1,17},{9,25},{17,1},{25,9},{2,18},{10... | collective-permute-start | bytes 1179656 | tf_op jit(solution)/shard_map/ppermute | solution.py:453
  71.2 1.5 %collective-permute-start.24 = (bf16[2048,256]{1,0:T(8,128)(2,1)S(1)}, bf16[2048,256]{1,0:T(8,128)(2,1)S(1)}, u32[]{:S(2)}, u32[]{:S(2)}) collective-permute-start(bf16[2048,256]{1,0:T(8,128)(2,1)S(1)} %copy-done.10), channel_id=1, source_target_pairs={{0,4},{4,0},{1,5},{5,1},{2,6},{6,2},{3,7},{7,3},{8,12},{12,8},{9,1... | collective-permute-start | bytes 3145736 | tf_op jit(solution)/shard_map/ppermute | solution.py:428
  72.7 2.0 %collective-permute-done.14.grads = bf16[2048,256]{1,0:T(8,128)(2,1)S(1)} collective-permute-done((bf16[2048,256]{1,0:T(8,128)(2,1)}, bf16[2048,256]{1,0:T(8,128)(2,1)S(1)}, u32[]{:S(2)}, u32[]{:S(2)}) %collective-permute-start.14) | collective-permute-done | bytes 1048608 | tf_op jit(solution)/shard_map/ppermute | solution.py:410
  74.7 0.7 shard_map.74
  75.4 1.3 %shard_map.76 = (bf16[1,256,256]{2,1,0:T(8,128)(2,1)S(1)}, bf16[1,256,256]{2,1,0:T(8,128)(2,1)S(1)}) custom-call(s32[6]{0:T(128)S(1)} %concatenate.3.info, bf16[2048,512]{1,0:T(8,128)(2,1)S(1)} %get-tuple-element.87.early, bf16[2048,256]{1,0:T(8,128)(2,1)S(1)} %get-tuple-element.92.right.chunk), custom_call_target="tpu_custom_call" | custom-call | tf_op jit(solution)/shard_map/pallas_call | solution.py:20
  76.8 1.3 %collective-permute-done.16.refs_0_.refs_8_ = bf16[1,256,256]{2,1,0:T(8,128)(2,1)S(1)} collective-permute-done((bf16[1,256,256]{2,1,0:T(8,128)(2,1)S(1)}, bf16[1,256,256]{2,1,0:T(8,128)(2,1)S(1)}, u32[]{:S(2)}, u32[]{:S(2)}) %collective-permute-start.16) | collective-permute-done | bytes 131104 | tf_op jit(solution)/shard_map/ppermute | solution.py:448
  78.1 0.6 shard_map.77
  78.7 2.3 %collective-permute-start.17 = (bf16[256,128]{1,0:T(8,128)(2,1)S(1)}, bf16[256,128]{1,0:T(8,128)(2,1)S(1)}, u32[]{:S(2)}, u32[]{:S(2)}) collective-permute-start(bf16[256,128]{1,0:T(8,128)(2,1)S(1)} %shard_map.77), channel_id=1, source_target_pairs={{0,16},{8,24},{16,0},{24,8},{1,17},{9,25},{17,1},{25,9},{2,18},{10... | collective-permute-start | bytes 196616 | tf_op jit(solution)/shard_map/ppermute | solution.py:453
  81.0 2.4 %collective-permute-done.17.refs_1_.refs_9_ = bf16[256,128]{1,0:T(8,128)(2,1)S(1)} collective-permute-done((bf16[256,128]{1,0:T(8,128)(2,1)S(1)}, bf16[256,128]{1,0:T(8,128)(2,1)S(1)}, u32[]{:S(2)}, u32[]{:S(2)}) %collective-permute-start.17) | collective-permute-done | bytes 65568 | tf_op jit(solution)/shard_map/ppermute | solution.py:453
  83.5 3.3 %shard_map.78 = (bf16[1,256,1792]{2,1,0:T(8,128)(2,1)S(1)}, bf16[2048,256]{1,0:T(8,128)(2,1)S(1)}, bf16[1,256,512]{2,1,0:T(8,128)(2,1)S(1)}, bf16[1,256,384]{2,1...) custom-call(s32[6]{0:T(128)S(1)} %concatenate.3.info, ...), custom_call_target="tpu_custom_call" | custom-call | flops 4600000000 | tf_op jit(solution)/shard_map/pallas_call | solution.py:20
  86.9 0.5 collective-permute-start.20
  87.4 0.4 collective-permute-start.21
  87.9 1.2 %collective-permute-done.19.refs_1_.refs_13_ = bf16[1,256,384]{2,1,0:T(8,128)(2,1)S(1)} collective-permute-done((bf16[1,256,384]{2,1,0:T(8,128)(2,1)S(1)}, bf16[1,256,384]{2,1,0:T(8,128)(2,1)S(1)}, u32[]{:S(2)}, u32[]{:S(2)}) %collective-permute-start.19) | collective-permute-done | bytes 196640 | tf_op jit(solution)/shard_map/ppermute | solution.py:448
  89.3 0.7 shard_map.79
  90.0 1.9 %collective-permute-start.25 = (bf16[256,896]{1,0:T(8,128)(2,1)S(1)}, bf16[256,896]{1,0:T(8,128)(2,1)S(1)}, u32[]{:S(2)}, u32[]{:S(2)}) collective-permute-start(bf16[256,896]{1,0:T(8,128)(2,1)S(1)} %shard_map.79), channel_id=1, source_target_pairs={{0,16},{8,24},{16,0},{24,8},{1,17},{9,25},{17,1},{25,9},{2,18},{10... | collective-permute-start | bytes 1376264 | tf_op jit(solution)/shard_map/ppermute | solution.py:453
  91.9 0.6 shard_map.81
  92.6 0.7 shard_map.80
  93.3 0.6 collective-permute-start.22
  93.8 2.9 %collective-permute-done.24.grads = bf16[2048,256]{1,0:T(8,128)(2,1)S(1)} collective-permute-done((bf16[2048,256]{1,0:T(8,128)(2,1)S(1)}, bf16[2048,256]{1,0:T(8,128)(2,1)S(1)}, u32[]{:S(2)}, u32[]{:S(2)}) %collective-permute-start.24) | collective-permute-done | bytes 1048608 | tf_op jit(solution)/shard_map/ppermute | solution.py:428
  96.7 0.3 shard_map.82.right_ref
  97.0 2.1 %shard_map.83 = (bf16[2,256,256]{2,1,0:T(8,128)(2,1)S(1)}, bf16[2,256,256]{2,1,0:T(8,128)(2,1)S(1)}) custom-call(s32[6]{0:T(128)S(1)} %concatenate.3.info, bf16[2048,512]{1,0:T(8,128)(2,1)S(1)} %get-tuple-element.87.early, bf16[2048,256]{1,0:T(8,128)(2,1)S(1)} %get-tuple-element.83.second, bf16[2048,256]{1,0:T(8,128)(2,1)S(1)} %get-tuple-element.108.last, ...), custom_call_target="tpu_custom_call" | custom-call | tf_op jit(solution)/shard_map/pallas_call | solution.py:20
  99.2 1.5 %collective-permute-done.26.refs_0_.refs_22_ = bf16[2,256,256]{2,1,0:T(8,128)(2,1)S(1)} collective-permute-done((bf16[2,256,256]{2,1,0:T(8,128)(2,1)S(1)}, bf16[2,256,256]{2,1,0:T(8,128)(2,1)S(1)}, u32[]{:S(2)}, u32[]{:S(2)}) %collective-permute-start.26) | collective-permute-done | bytes 262176 | tf_op jit(solution)/shard_map/ppermute | solution.py:433
  100.7 0.6 shard_map.84
  101.3 1.5 %collective-permute-start.31 = (bf16[256,256]{1,0:T(8,128)(2,1)S(1)}, bf16[256,256]{1,0:T(8,128)(2,1)S(1)}, u32[]{:S(2)}, u32[]{:S(2)}) collective-permute-start(bf16[256,256]{1,0:T(8,128)(2,1)S(1)} %shard_map.84), channel_id=1, source_target_pairs={{0,16},{8,24},{16,0},{24,8},{1,17},{9,25},{17,1},{25,9},{2,18},{10... | collective-permute-start | bytes 393224 | tf_op jit(solution)/shard_map/ppermute | solution.py:440
  102.8 0.7 shard_map.85
  103.6 0.5 collective-permute-start.28
  104.2 0.4 collective-permute-start.30
  104.6 0.3 collective-permute-done.27.refs_17_
  105.0 0.3 collective-permute-done.29.refs_19_
  105.6 1.4 %collective-permute-done.31.refs_23_ = bf16[256,256]{1,0:T(8,128)(2,1)S(1)} collective-permute-done((bf16[256,256]{1,0:T(8,128)(2,1)S(1)}, bf16[256,256]{1,0:T(8,128)(2,1)S(1)}, u32[]{:S(2)}, u32[]{:S(2)}) %collective-permute-start.31) | collective-permute-done | bytes 131104 | tf_op jit(solution)/shard_map/ppermute | solution.py:440
  106.9 2.2 %shard_map.86 = (f32[256,1024]{1,0:T(8,128)}, f32[256,1024]{1,0:T(8,128)}) custom-call(s32[6]{0:T(128)S(1)} %concatenate.3.info, bf16[1,256,1536]{2,1,0:T(8,128)(2,1)S(1)} %get-tuple-element.77.keep.refs_0_, bf16[1,256,384]{2,1,0:T(8,128)(2,1)S(1)} %collective-permute-done.9.refs_0_.refs_1_, ...), custom_call_target="tpu_custom_call" | custom-call | tf_op jit(solution)/shard_map/pallas_call | solution.py:20
  (49 shorter events, 2.5 us)
Async XLA Ops:
  0.6 50.8 %collective-permute-start.7 = (bf16[2048,512]{1,0:T(8,128)(2,1)}, bf16[2048,512]{1,0:T(8,128)(2,1)}, u32[]{:S(2)}, u32[]{:S(2)}) collective-permute-start(bf16[2048,512]{1,0:T(8,128)(2,1)} %cols.3), channel_id=1, source_target_pairs={{0,4},{4,0},{1,5},{5,1},{2,6},{6,2},{3,7},{7,3},{8,12},{12,8},{9,1... | collective-permute-start | bytes 6291464 | tf_op jit(solution)/shard_map/ppermute | solution.py:386
  3.7 25.0 %collective-permute-start = (bf16[2048,256]{1,0:T(8,128)(2,1)}, bf16[2048,256]{1,0:T(8,128)(2,1)}, u32[]{:S(2)}, u32[]{:S(2)}) collective-permute-start(bf16[2048,256]{1,0:T(8,128)(2,1)} %own_rows.3), channel_id=1, source_target_pairs={{0,1},{1,0},{2,3},{3,2},{4,5},{5,4},{6,7},{7,6},{8,9},{9,8},{10,11... | collective-permute-start | bytes 3145736 | tf_op jit(solution)/shard_map/ppermute | solution.py:387
  5.2 23.4 %collective-permute-start.1 = (bf16[2048,256]{1,0:T(8,128)(2,1)}, bf16[2048,256]{1,0:T(8,128)(2,1)}, u32[]{:S(2)}, u32[]{:S(2)}) collective-permute-start(bf16[2048,256]{1,0:T(8,128)(2,1)} %own_rows.3), channel_id=1, source_target_pairs={{1,2},{2,1},{5,6},{6,5},{9,10},{10,9},{13,14},{14,13},{17,18},{18,... | collective-permute-start | bytes 3145736 | tf_op jit(solution)/shard_map/ppermute | solution.py:388
  6.9 1.6 %copy-start = (bf16[2048,512]{1,0:T(8,128)(2,1)S(1)}, bf16[2048,512]{1,0:T(8,128)(2,1)}, u32[]{:S(2)}) copy-start(bf16[2048,512]{1,0:T(8,128)(2,1)} %cols.3) | copy-start | bytes 6291460
  8.4 1.2 %copy-start.4 = (bf16[2048,256]{1,0:T(8,128)(2,1)S(1)}, bf16[2048,256]{1,0:T(8,128)(2,1)}, u32[]{:S(2)}) copy-start(bf16[2048,256]{1,0:T(8,128)(2,1)} %own_rows.3) | copy-start | bytes 3145732
  9.7 10.3 %copy-start.12 = (f32[2048]{0:T(1024)S(1)}, f32[2048]{0:T(1024)}, u32[]{:S(2)}) copy-start(f32[2048]{0:T(1024)} %param.8) | copy-start | bytes 24580
  9.7 10.7 %copy-start.1 = (bf16[2048,512]{1,0:T(8,128)(2,1)S(1)}, bf16[2048,512]{1,0:T(8,128)(2,1)}, u32[]{:S(2)}) copy-start(bf16[2048,512]{1,0:T(8,128)(2,1)} %cols.3) | copy-start | bytes 6291460
  16.8 11.9 %collective-permute-start.2 = (f32[1,768]{1,0:T(1,128)S(1)}, f32[1,768]{1,0:T(1,128)S(1)}, u32[]{:S(2)}, u32[]{:S(2)}) collective-permute-start(f32[1,768]{1,0:T(1,128)S(1)} %psum.7.sums.m0), channel_id=1, source_target_pairs={{0,1},{1,0},{2,3},{3,2},{4,5},{5,4},{6,7},{7,6},{8,9},{9,8},{10,11... | collective-permute-start | bytes 9224 | tf_op jit(solution)/shard_map/ppermute | solution.py:392
  20.0 12.7 %collective-permute-start.5 = (f32[1,768]{1,0:T(1,128)S(1)}, f32[1,768]{1,0:T(1,128)S(1)}, u32[]{:S(2)}, u32[]{:S(2)}) collective-permute-start(f32[1,768]{1,0:T(1,128)S(1)} %psum.7.sums.m0), channel_id=1, source_target_pairs={{0,2},{1,3},{2,0},{3,1},{4,6},{5,7},{6,4},{7,5},{8,10},{9,11},{10,... | collective-permute-start | bytes 9224 | tf_op jit(solution)/shard_map/ppermute | solution.py:393
  20.4 1.6 %copy-start.8 = (bf16[2048,512]{1,0:T(8,128)(2,1)S(1)}, bf16[2048,512]{1,0:T(8,128)(2,1)}, u32[]{:S(2)}) copy-start(bf16[2048,512]{1,0:T(8,128)(2,1)} %grads.1) | copy-start | bytes 6291460
  23.1 2.0 %copy-start.2 = (bf16[2048,1024]{1,0:T(8,128)(2,1)}, bf16[2048,1024]{1,0:T(8,128)(2,1)S(1)}, u32[]{:S(2)}) copy-start(bf16[2048,1024]{1,0:T(8,128)(2,1)S(1)} %get-tuple-element.70.ow) | copy-start | bytes 12582916
  25.1 1.4 %copy-start.6 = (f32[2048,256]{1,0:T(8,128)}, f32[2048,256]{1,0:T(8,128)S(1)}, u32[]{:S(2)}) copy-start(f32[2048,256]{1,0:T(8,128)S(1)} %get-tuple-element.84.wide) | copy-start | bytes 6291460
  26.5 1.0 copy-start.9
  27.5 1.0 copy-start.11
  28.6 21.0 %collective-permute-start.4 = (f32[1,768]{1,0:T(1,128)S(1)}, f32[1,768]{1,0:T(1,128)S(1)}, u32[]{:S(2)}, u32[]{:S(2)}) collective-permute-start(f32[1,768]{1,0:T(1,128)S(1)} %psum.7.sums.m0), channel_id=1, source_target_pairs={{0,4},{4,0},{1,5},{5,1},{2,6},{6,2},{3,7},{7,3},{8,12},{12,8},{9,1... | collective-permute-start | bytes 9224 | tf_op jit(solution)/shard_map/ppermute | solution.py:407
  29.0 28.7 %collective-permute-start.6 = (bf16[2048,256]{1,0:T(8,128)(2,1)}, bf16[2048,256]{1,0:T(8,128)(2,1)S(1)}, u32[]{:S(2)}, u32[]{:S(2)}) collective-permute-start(bf16[2048,256]{1,0:T(8,128)(2,1)} %collective-permute-done.near), channel_id=1, source_target_pairs={{1,2},{2,1},{5,6},{6,5},{9,10},{10,9},{13,14},{14,13},{17,18},{18,... | collective-permute-start | bytes 3145736 | tf_op jit(solution)/shard_map/ppermute | solution.py:409
  29.8 30.3 %collective-permute-start.3 = (bf16[2048,256]{1,0:T(8,128)(2,1)}, bf16[2048,256]{1,0:T(8,128)(2,1)S(1)}, u32[]{:S(2)}, u32[]{:S(2)}) collective-permute-start(bf16[2048,256]{1,0:T(8,128)(2,1)} %collective-permute-done.1.mid1), channel_id=1, source_target_pairs={{1,0},{2,3},{5,4},{6,7},{9,8},{10,11},{13,12},{14,15},{17,16},{18,... | collective-permute-start | bytes 3145736 | tf_op jit(solution)/shard_map/ppermute | solution.py:408
  32.7 25.1 %collective-permute-start.8 = (f32[1,768]{1,0:T(1,128)S(1)}, f32[1,768]{1,0:T(1,128)S(1)}, u32[]{:S(2)}, u32[]{:S(2)}) collective-permute-start(f32[1,768]{1,0:T(1,128)S(1)} %psum.7.sums.m0), channel_id=1, source_target_pairs={{0,3},{1,2},{2,1},{3,0},{4,7},{5,6},{6,5},{7,4},{8,11},{9,10},{10,... | collective-permute-start | bytes 9224 | tf_op jit(solution)/shard_map/ppermute | solution.py:406
  49.6 25.1 %collective-permute-start.14 = (bf16[2048,256]{1,0:T(8,128)(2,1)}, bf16[2048,256]{1,0:T(8,128)(2,1)S(1)}, u32[]{:S(2)}, u32[]{:S(2)}) collective-permute-start(bf16[2048,256]{1,0:T(8,128)(2,1)} %copy-done.11), channel_id=1, source_target_pairs={{0,4},{4,0},{1,5},{5,1},{2,6},{6,2},{3,7},{7,3},{8,12},{12,8},{9,1... | collective-permute-start | bytes 3145736 | tf_op jit(solution)/shard_map/ppermute | solution.py:410
  51.4 2.8 %copy-start.3 = (bf16[2048,1024]{1,0:T(8,128)(2,1)S(1)}, bf16[2048,1024]{1,0:T(8,128)(2,1)}, u32[]{:S(2)}) copy-start(bf16[2048,1024]{1,0:T(8,128)(2,1)} %copy-done.2) | copy-start | bytes 12582916
  51.4 3.1 %copy-start.5 = (bf16[2048,256]{1,0:T(8,128)(2,1)S(1)}, bf16[2048,256]{1,0:T(8,128)(2,1)}, u32[]{:S(2)}) copy-start(bf16[2048,256]{1,0:T(8,128)(2,1)} %own_rows.3) | copy-start | bytes 3145732
  57.8 25.7 %collective-permute-start.13 = (bf16[2048,256]{1,0:T(8,128)(2,1)S(1)}, bf16[2048,256]{1,0:T(8,128)(2,1)S(1)}, u32[]{:S(2)}, u32[]{:S(2)}) collective-permute-start(bf16[2048,256]{1,0:T(8,128)(2,1)S(1)} %collective-permute-done.6.last1), channel_id=1, source_target_pairs={{1,0},{2,3},{5,4},{6,7},{9,8},{10,11},{13,12},{14,15},{17,16},{18,... | collective-permute-start | bytes 3145736 | tf_op jit(solution)/shard_map/ppermute | solution.py:427
  60.0 11.2 %copy-start.10 = (bf16[2048,256]{1,0:T(8,128)(2,1)S(1)}, bf16[2048,256]{1,0:T(8,128)(2,1)}, u32[]{:S(2)}) copy-start(bf16[2048,256]{1,0:T(8,128)(2,1)} %copy-done.9) | copy-start | bytes 3145732
  60.0 14.7 %copy-start.7 = (f32[2048,256]{1,0:T(8,128)S(1)}, f32[2048,256]{1,0:T(8,128)}, u32[]{:S(2)}) copy-start(f32[2048,256]{1,0:T(8,128)} %copy-done.6) | copy-start | bytes 6291460
  66.1 1.5 %collective-permute-start.10 = (bf16[1,256,384]{2,1,0:T(8,128)(2,1)S(1)}, bf16[1,256,384]{2,1,0:T(8,128)(2,1)S(1)}, u32[]{:S(2)}, u32[]{:S(2)}) collective-permute-start(bf16[1,256,384]{2,1,0:T(8,128)(2,1)S(1)} %get-tuple-element.79), channel_id=1, source_target_pairs={{0,8},{8,0},{16,24},{24,16},{1,9},{9,1},{17,25},{25,17},{2,10},{10... | collective-permute-start | bytes 589832 | tf_op jit(solution)/shard_map/ppermute | solution.py:448
  66.2 1.7 %collective-permute-start.11 = (bf16[1,256,384]{2,1,0:T(8,128)(2,1)S(1)}, bf16[1,256,384]{2,1,0:T(8,128)(2,1)S(1)}, u32[]{:S(2)}, u32[]{:S(2)}) collective-permute-start(bf16[1,256,384]{2,1,0:T(8,128)(2,1)S(1)} %get-tuple-element.80), channel_id=1, source_target_pairs={{0,8},{8,0},{16,24},{24,16},{1,9},{9,1},{17,25},{25,17},{2,10},{10... | collective-permute-start | bytes 589832 | tf_op jit(solution)/shard_map/ppermute | solution.py:448
  66.7 1.5 %collective-permute-start.12 = (bf16[1,256,384]{2,1,0:T(8,128)(2,1)S(1)}, bf16[1,256,384]{2,1,0:T(8,128)(2,1)S(1)}, u32[]{:S(2)}, u32[]{:S(2)}) collective-permute-start(bf16[1,256,384]{2,1,0:T(8,128)(2,1)S(1)} %get-tuple-element.81), channel_id=1, source_target_pairs={{0,8},{8,0},{16,24},{24,16},{1,9},{9,1},{17,25},{25,17},{2,10},{10... | collective-permute-start | bytes 589832 | tf_op jit(solution)/shard_map/ppermute | solution.py:448
  67.6 1.4 %collective-permute-start.9 = (bf16[1,256,384]{2,1,0:T(8,128)(2,1)S(1)}, bf16[1,256,384]{2,1,0:T(8,128)(2,1)S(1)}, u32[]{:S(2)}, u32[]{:S(2)}) collective-permute-start(bf16[1,256,384]{2,1,0:T(8,128)(2,1)S(1)} %get-tuple-element.78), channel_id=1, source_target_pairs={{0,8},{8,0},{16,24},{24,16},{1,9},{9,1},{17,25},{25,17},{2,10},{10... | collective-permute-start | bytes 589832 | tf_op jit(solution)/shard_map/ppermute | solution.py:448
  69.7 13.8 %collective-permute-start.15 = (bf16[256,768]{1,0:T(8,128)(2,1)S(1)}, bf16[256,768]{1,0:T(8,128)(2,1)S(1)}, u32[]{:S(2)}, u32[]{:S(2)}) collective-permute-start(bf16[256,768]{1,0:T(8,128)(2,1)S(1)} %shard_map.75), channel_id=1, source_target_pairs={{0,16},{8,24},{16,0},{24,8},{1,17},{9,25},{17,1},{25,9},{2,18},{10... | collective-permute-start | bytes 1179656 | tf_op jit(solution)/shard_map/ppermute | solution.py:453
  71.2 25.5 %collective-permute-start.24 = (bf16[2048,256]{1,0:T(8,128)(2,1)S(1)}, bf16[2048,256]{1,0:T(8,128)(2,1)S(1)}, u32[]{:S(2)}, u32[]{:S(2)}) collective-permute-start(bf16[2048,256]{1,0:T(8,128)(2,1)S(1)} %copy-done.10), channel_id=1, source_target_pairs={{0,4},{4,0},{1,5},{5,1},{2,6},{6,2},{3,7},{7,3},{8,12},{12,8},{9,1... | collective-permute-start | bytes 3145736 | tf_op jit(solution)/shard_map/ppermute | solution.py:428
  76.7 1.4 %collective-permute-start.16 = (bf16[1,256,256]{2,1,0:T(8,128)(2,1)S(1)}, bf16[1,256,256]{2,1,0:T(8,128)(2,1)S(1)}, u32[]{:S(2)}, u32[]{:S(2)}) collective-permute-start(bf16[1,256,256]{2,1,0:T(8,128)(2,1)S(1)} %get-tuple-element.89), channel_id=1, source_target_pairs={{0,8},{8,0},{16,24},{24,16},{1,9},{9,1},{17,25},{25,17},{2,10},{10... | collective-permute-start | bytes 393224 | tf_op jit(solution)/shard_map/ppermute | solution.py:448
  78.7 4.7 %collective-permute-start.17 = (bf16[256,128]{1,0:T(8,128)(2,1)S(1)}, bf16[256,128]{1,0:T(8,128)(2,1)S(1)}, u32[]{:S(2)}, u32[]{:S(2)}) collective-permute-start(bf16[256,128]{1,0:T(8,128)(2,1)S(1)} %shard_map.77), channel_id=1, source_target_pairs={{0,16},{8,24},{16,0},{24,8},{1,17},{9,25},{17,1},{25,9},{2,18},{10... | collective-permute-start | bytes 196616 | tf_op jit(solution)/shard_map/ppermute | solution.py:453
  86.8 2.5 %collective-permute-start.18 = (bf16[1,256,512]{2,1,0:T(8,128)(2,1)S(1)}, bf16[1,256,512]{2,1,0:T(8,128)(2,1)S(1)}, u32[]{:S(2)}, u32[]{:S(2)}) collective-permute-start(bf16[1,256,512]{2,1,0:T(8,128)(2,1)S(1)} %get-tuple-element.96), channel_id=1, source_target_pairs={{0,8},{8,0},{16,24},{24,16},{1,9},{9,1},{17,25},{25,17},{2,10},{10... | collective-permute-start | bytes 786440 | tf_op jit(solution)/shard_map/ppermute | solution.py:448
  86.9 2.5 %collective-permute-start.20 = (bf16[1,256,512]{2,1,0:T(8,128)(2,1)S(1)}, bf16[1,256,512]{2,1,0:T(8,128)(2,1)S(1)}, u32[]{:S(2)}, u32[]{:S(2)}) collective-permute-start(bf16[1,256,512]{2,1,0:T(8,128)(2,1)S(1)} %get-tuple-element.98), channel_id=1, source_target_pairs={{0,8},{8,0},{16,24},{24,16},{1,9},{9,1},{17,25},{25,17},{2,10},{10... | collective-permute-start | bytes 786440 | tf_op jit(solution)/shard_map/ppermute | solution.py:448
  87.4 1.7 %collective-permute-start.19 = (bf16[1,256,384]{2,1,0:T(8,128)(2,1)S(1)}, bf16[1,256,384]{2,1,0:T(8,128)(2,1)S(1)}, u32[]{:S(2)}, u32[]{:S(2)}) collective-permute-start(bf16[1,256,384]{2,1,0:T(8,128)(2,1)S(1)} %get-tuple-element.97), channel_id=1, source_target_pairs={{0,8},{8,0},{16,24},{24,16},{1,9},{9,1},{17,25},{25,17},{2,10},{10... | collective-permute-start | bytes 589832 | tf_op jit(solution)/shard_map/ppermute | solution.py:448
  87.4 1.9 %collective-permute-start.21 = (bf16[1,256,384]{2,1,0:T(8,128)(2,1)S(1)}, bf16[1,256,384]{2,1,0:T(8,128)(2,1)S(1)}, u32[]{:S(2)}, u32[]{:S(2)}) collective-permute-start(bf16[1,256,384]{2,1,0:T(8,128)(2,1)S(1)} %get-tuple-element.99), channel_id=1, source_target_pairs={{0,8},{8,0},{16,24},{24,16},{1,9},{9,1},{17,25},{25,17},{2,10},{10... | collective-permute-start | bytes 589832 | tf_op jit(solution)/shard_map/ppermute | solution.py:448
  90.0 12.8 %collective-permute-start.25 = (bf16[256,896]{1,0:T(8,128)(2,1)S(1)}, bf16[256,896]{1,0:T(8,128)(2,1)S(1)}, u32[]{:S(2)}, u32[]{:S(2)}) collective-permute-start(bf16[256,896]{1,0:T(8,128)(2,1)S(1)} %shard_map.79), channel_id=1, source_target_pairs={{0,16},{8,24},{16,0},{24,8},{1,17},{9,25},{17,1},{25,9},{2,18},{10... | collective-permute-start | bytes 1376264 | tf_op jit(solution)/shard_map/ppermute | solution.py:453
  92.5 4.5 %collective-permute-start.23 = (bf16[256,128]{1,0:T(8,128)(2,1)S(1)}, bf16[256,128]{1,0:T(8,128)(2,1)S(1)}, u32[]{:S(2)}, u32[]{:S(2)}) collective-permute-start(bf16[256,128]{1,0:T(8,128)(2,1)S(1)} %shard_map.81), channel_id=1, source_target_pairs={{0,8},{8,0},{16,24},{24,16},{1,9},{9,1},{17,25},{25,17},{2,10},{10... | collective-permute-start | bytes 196616 | tf_op jit(solution)/shard_map/ppermute | solution.py:465
  93.3 3.8 %collective-permute-start.22 = (bf16[256,768]{1,0:T(8,128)(2,1)S(1)}, bf16[256,768]{1,0:T(8,128)(2,1)S(1)}, u32[]{:S(2)}, u32[]{:S(2)}) collective-permute-start(bf16[256,768]{1,0:T(8,128)(2,1)S(1)} %shard_map.80), channel_id=1, source_target_pairs={{0,8},{8,0},{16,24},{24,16},{1,9},{9,1},{17,25},{25,17},{2,10},{10... | collective-permute-start | bytes 1179656 | tf_op jit(solution)/shard_map/ppermute | solution.py:465
  99.1 1.6 %collective-permute-start.26 = (bf16[2,256,256]{2,1,0:T(8,128)(2,1)S(1)}, bf16[2,256,256]{2,1,0:T(8,128)(2,1)S(1)}, u32[]{:S(2)}, u32[]{:S(2)}) collective-permute-start(bf16[2,256,256]{2,1,0:T(8,128)(2,1)S(1)} %get-tuple-element.112), channel_id=1, source_target_pairs={{0,8},{8,0},{16,24},{24,16},{1,9},{9,1},{17,25},{25,17},{2,10},{10... | collective-permute-start | bytes 786440 | tf_op jit(solution)/shard_map/ppermute | solution.py:433
  101.3 5.6 %collective-permute-start.31 = (bf16[256,256]{1,0:T(8,128)(2,1)S(1)}, bf16[256,256]{1,0:T(8,128)(2,1)S(1)}, u32[]{:S(2)}, u32[]{:S(2)}) collective-permute-start(bf16[256,256]{1,0:T(8,128)(2,1)S(1)} %shard_map.84), channel_id=1, source_target_pairs={{0,16},{8,24},{16,0},{24,8},{1,17},{9,25},{17,1},{25,9},{2,18},{10... | collective-permute-start | bytes 393224 | tf_op jit(solution)/shard_map/ppermute | solution.py:440
  103.5 1.4 %collective-permute-start.27 = (bf16[64,896]{1,0:T(8,128)(2,1)S(1)}, bf16[64,896]{1,0:T(8,128)(2,1)S(1)}, u32[]{:S(2)}, u32[]{:S(2)}) collective-permute-start(bf16[64,896]{1,0:T(8,128)(2,1)S(1)} %get-tuple-element.114), channel_id=1, source_target_pairs={{0,8},{8,0},{16,24},{24,16},{1,9},{9,1},{17,25},{25,17},{2,10},{10... | collective-permute-start | bytes 344072 | tf_op jit(solution)/shard_map/ppermute | solution.py:465
  103.6 1.5 %collective-permute-start.28 = (bf16[64,896]{1,0:T(8,128)(2,1)S(1)}, bf16[64,896]{1,0:T(8,128)(2,1)S(1)}, u32[]{:S(2)}, u32[]{:S(2)}) collective-permute-start(bf16[64,896]{1,0:T(8,128)(2,1)S(1)} %get-tuple-element.115), channel_id=1, source_target_pairs={{0,8},{8,0},{16,24},{24,16},{1,9},{9,1},{17,25},{25,17},{2,10},{10... | collective-permute-start | bytes 344072 | tf_op jit(solution)/shard_map/ppermute | solution.py:465
  104.1 1.3 %collective-permute-start.29 = (bf16[64,896]{1,0:T(8,128)(2,1)S(1)}, bf16[64,896]{1,0:T(8,128)(2,1)S(1)}, u32[]{:S(2)}, u32[]{:S(2)}) collective-permute-start(bf16[64,896]{1,0:T(8,128)(2,1)S(1)} %get-tuple-element.116), channel_id=1, source_target_pairs={{0,8},{8,0},{16,24},{24,16},{1,9},{9,1},{17,25},{25,17},{2,10},{10... | collective-permute-start | bytes 344072 | tf_op jit(solution)/shard_map/ppermute | solution.py:465
  104.2 1.4 %collective-permute-start.30 = (bf16[64,896]{1,0:T(8,128)(2,1)S(1)}, bf16[64,896]{1,0:T(8,128)(2,1)S(1)}, u32[]{:S(2)}, u32[]{:S(2)}) collective-permute-start(bf16[64,896]{1,0:T(8,128)(2,1)S(1)} %get-tuple-element.117), channel_id=1, source_target_pairs={{0,8},{8,0},{16,24},{24,16},{1,9},{9,1},{17,25},{25,17},{2,10},{10... | collective-permute-start | bytes 344072 | tf_op jit(solution)/shard_map/ppermute | solution.py:465

commit v5 on v4

--- a/solution.py
+++ b/solution.py
@@ -12,7 +12,7 @@
 VMEM = pl.BlockSpec(memory_space=pltpu.VMEM)
 SMEM = pl.BlockSpec(memory_space=pltpu.SMEM)
 MID, LOW, CORE, STRAIGHT, TABLE = 0, 1, 2, 3, 4
-MEAN_COST, FAR_COST, EARLY_COST, FIRST_COST, LAST_COST = 6, 3, 4, 0, 4
+MEAN_COST, FAR_COST, EARLY_COST, FIRST_COST, LAST_COST = 6, 3, 6, 0, 2
 WEIGH_COST, HOPS = 12, 4
 
 
@@ -204,19 +204,33 @@
         out[:, a : a + lanes] = weigh(wide[...], cols, grads[:, a : a + lanes])
 
 
-def chunk_kernel(per, slots, info, early, second, last, right_ref, send, keep):
+def flipped_kernel(start, far, wide, grads, out):
+    cols = far[:, start : start + grads.shape[1]]
+    out[...] = weigh(wide[...], cols, grads[...]).T
+
+
+def chunk_kernel(per, slots, kept, info, early, second, last, right, out):
     rw = last.shape[1]
-    right = right_ref[...]
-    result = dot(right, early[...]).astype(BF)
-    for j, block in enumerate((1, 2)):
-        by_block(info, block, 1, per, slots, (send,), keep, result[:, j * rw : (j + 1) * rw])
-    of_second = dot(right, second[...]).astype(BF)
-    of_last = dot(right, last[...]).astype(BF)
+    piece = rw // per
+
+    def block_of(tile, first, block):
+        for i in range(per):
+            walker = block * per + i
+
+            @pl.when((info[CORE] == walker % 2) == kept)
+            def _():
+                rows = tile[:, first + i * piece : first + (i + 1) * piece]
+                out[slots[walker]] = lax.dot_general(
+                    right[...], rows, (((1,), (0,)), ((), ())), preferred_element_type=F32
+                ).astype(BF)
+
+    block_of(early, 0, 1)
+    block_of(early, rw, 2)
 
     @functools.partial(low_or_high, info)
     def _(second_block, last_block):
-        by_block(info, second_block, 1, per, slots, (send,), keep, of_second)
-        by_block(info, last_block, 1, per, slots, (send,), keep, of_last)
+        block_of(second, 0, second_block)
+        block_of(last, 0, last_block)
 
 
 def pair(keep, gots, i):
@@ -473,7 +487,7 @@
 
     e_keep, early, *sends = call(
         functools.partial(early_kernel, count, per, place),
-        message_shapes(3 * cw) + [((samples, 2 * rw), BF)] + message_shapes(*[3 * cw // 4] * 4),
+        message_shapes(3 * cw) + [((samples, 2 * rw), BF)] + message_shapes(*[3 * cw // 2] * 2),
         info, o_rows, near, mid1, mid2, m0, m1, m2, m3, ow, far,
         cost=EARLY_COST,
     )
@@ -506,18 +520,22 @@
     bring_home(messages[1], 1, *sent)
     n = widths[1]
     (right,) = call(
-        functools.partial(weigh_kernel, cuts[1]),
-        [((samples, n), BF)],
+        functools.partial(flipped_kernel, cuts[1]),
+        [((n, samples), BF)],
         far, wide, far_grads[1],
         cost=WEIGH_COST,
     )
     messages[0][2], messages[1][2], right = lax.optimization_barrier(
         (messages[0][2], messages[1][2], right)
     )
-    send, keep = call(
-        functools.partial(chunk_kernel, per, place),
-        [((2 * per, n, piece), BF)] * 2,
-        info, early, second, last, after(right, *sent),
+    right = after(right, *sent)
+    send, keep = (
+        call(
+            functools.partial(chunk_kernel, per, place, kept),
+            [((2 * per, n, piece), BF)],
+            info, early, second, last, right,
+        )[0]
+        for kept in (False, True)
     )
     sent = reduce([send], keep, 0, 2 * per, [(None, (0, False, cuts[1]))])
     bring_home(messages[2], HOPS, *sent)

time: 110 us -> 110 us (level)
  waiting for transfers between devices: 32.1 us -> 29.8 us
  local copies, waits for them, and re-layouts: 11.9 us -> 14 us
    unnamed x26 -> x30, local copies, waits for them, and re-layouts: 10.7 us -> 12.9 us
    ppermute x9 -> x7, waiting for transfers between devices: 4.94 us -> 3.08 us  [reduce_rows(): gots = [lax.ppermute(send, 'walker', other_core) for send in sends]]
    ppermute x1, waiting for transfers between devices: 1.52 us -> 0.07 us  [reduce(): gots = [lax.ppermute(send, 'walker', other_core) for send in sends]]
    ppermute x3, waiting for transfers between devices: 2.41 us -> 3.74 us  [reduce_rows(): got_x = lax.ppermute(sent[0], 'walker', [(v, v ^ 2) for v in range(4)])]
    ppermute x1, waiting for transfers between devices: 1.96 us -> 3.11 us  [per_device(): far_grads = [lax.ppermute(grads[0], 'prow', flip)]]
    pallas_call x19 -> x20, Pallas kernels: 27.5 us -> 28.4 us  [call(): pl.pallas_call(kernel, out_shape=[jax.ShapeDtypeStruct(s, d) for s, d in...]
  transfers between devices with their start and end apart: 32 -> 30, of which waited for: 20 -> 18; matrix products, arithmetic and copies ran while one was open for 1% -> 1% of each run, Pallas kernels for 23% -> 24%
where the time goes in v5:
time: 110 us; the launch traced here: 109 us
  waiting for transfers between devices  29.8 us (27%)
  starting transfers between devices  29.3 us (27%)
  Pallas kernels  28.4 us (26%)
  local copies, waits for them, and re-layouts  14 us (13%)
  blocking collectives  6.55 us (6%)
    pallas_call x20, Pallas kernels, call(): pl.pallas_call(kernel, out_shape=[jax.ShapeDtypeStruct(s, d) for s, d in...  28.4 us
    ppermute x1, waiting for transfers between devices, per_device(): far_sums = lax.ppermute(m0, 'prow', flip)  14.1 us
    unnamed x30, local copies, waits for them, and re-layouts  12.9 us
    psum x1, blocking collectives, per_device(): m0 = lax.psum(sums, 'walker')  6.55 us
    ppermute x3, starting transfers between devices, reduce_rows(): got_x = lax.ppermute(sent[0], 'walker', [(v, v ^ 2) for v in range(4)])  5.13 us
    ppermute x3, waiting for transfers between devices, reduce_rows(): got_x = lax.ppermute(sent[0], 'walker', [(v, v ^ 2) for v in range(4)])  3.74 us
    ppermute x1, starting transfers between devices, per_device(): m1 = lax.ppermute(m0, 'pcol', outer)  3.2 us
    ppermute x1, waiting for transfers between devices, per_device(): far_grads = [lax.ppermute(grads[0], 'prow', flip)]  3.11 us
  transfers between devices with their start and end apart: 30, of which 18 were waited for; matrix products, arithmetic and copies ran while one was open for 1% of the time, Pallas kernels for 24%

profile of v5, /device:TPU:0, one launch (start us, length us, event | category | flops | bytes accessed | tf_op | source)
XLA Modules:
  0.0 109.1 jit_solution(1150440816848650022)
XLA Ops:
  0.6 3.0 %collective-permute-start.7 = (bf16[2048,512]{1,0:T(8,128)(2,1)}, bf16[2048,512]{1,0:T(8,128)(2,1)}, u32[]{:S(2)}, u32[]{:S(2)}) collective-permute-start(bf16[2048,512]{1,0:T(8,128)(2,1)} %cols.3), channel_id=1, source_target_pairs={{0,4},{4,0},{1,5},{5,1},{2,6},{6,2},{3,7},{7,3},{8,12},{12,8},{9,1... | collective-permute-start | bytes 6291464 | tf_op jit(solution)/shard_map/ppermute | solution.py:400
  3.7 1.6 %collective-permute-start = (bf16[2048,256]{1,0:T(8,128)(2,1)}, bf16[2048,256]{1,0:T(8,128)(2,1)}, u32[]{:S(2)}, u32[]{:S(2)}) collective-permute-start(bf16[2048,256]{1,0:T(8,128)(2,1)} %own_rows.3), channel_id=1, source_target_pairs={{0,1},{1,0},{2,3},{3,2},{4,5},{5,4},{6,7},{7,6},{8,9},{9,8},{10,11... | collective-permute-start | bytes 3145736 | tf_op jit(solution)/shard_map/ppermute | solution.py:401
  5.2 1.6 %collective-permute-start.1 = (bf16[2048,256]{1,0:T(8,128)(2,1)}, bf16[2048,256]{1,0:T(8,128)(2,1)}, u32[]{:S(2)}, u32[]{:S(2)}) collective-permute-start(bf16[2048,256]{1,0:T(8,128)(2,1)} %own_rows.3), channel_id=1, source_target_pairs={{1,2},{2,1},{5,6},{6,5},{9,10},{10,9},{13,14},{14,13},{17,18},{18,... | collective-permute-start | bytes 3145736 | tf_op jit(solution)/shard_map/ppermute | solution.py:402
  6.9 1.6 %copy-done.2 = bf16[2048,512]{1,0:T(8,128)(2,1)S(1)} copy-done((bf16[2048,512]{1,0:T(8,128)(2,1)S(1)}, bf16[2048,512]{1,0:T(8,128)(2,1)}, u32[]{:S(2)}) %copy-start.2) | copy-done | bytes 2097176
  8.5 1.2 %copy-done.4 = bf16[2048,256]{1,0:T(8,128)(2,1)S(1)} copy-done((bf16[2048,256]{1,0:T(8,128)(2,1)S(1)}, bf16[2048,256]{1,0:T(8,128)(2,1)}, u32[]{:S(2)}) %copy-start.4) | copy-done | bytes 1048600
  9.7 0.5 shard_map.68
  10.2 6.6 %psum.7.sums.m0 = f32[1,768]{1,0:T(1,128)S(1)} all-reduce(f32[1,768]{1,0:T(1,128)S(1)} %shard_map.68), channel_id=1, replica_groups=mesh['walker'=4,'prow'=2,'pcol'=4] {'walker'}, use_global_device_ids=true, to_apply=%region_0.1 | all-reduce | flops 768 | bytes 6144 | tf_op jit(solution)/shard_map/psum | solution.py:405
  16.8 3.2 %collective-permute-start.2 = (f32[1,768]{1,0:T(1,128)S(1)}, f32[1,768]{1,0:T(1,128)S(1)}, u32[]{:S(2)}, u32[]{:S(2)}) collective-permute-start(f32[1,768]{1,0:T(1,128)S(1)} %psum.7.sums.m0), channel_id=1, source_target_pairs={{0,1},{1,0},{2,3},{3,2},{4,5},{5,4},{6,7},{7,6},{8,9},{9,8},{10,11... | collective-permute-start | bytes 9224 | tf_op jit(solution)/shard_map/ppermute | solution.py:406
  20.0 0.4 copy.7.energy
  20.4 1.6 %copy-done.8 = bf16[2048,512]{1,0:T(8,128)(2,1)S(1)} copy-done((bf16[2048,512]{1,0:T(8,128)(2,1)S(1)}, bf16[2048,512]{1,0:T(8,128)(2,1)}, u32[]{:S(2)}) %copy-start.8) | copy-done | bytes 2097176
  22.0 1.2 %shard_map.69 = (bf16[2048,1024]{1,0:T(8,128)(2,1)S(1)}, f32[2048,256]{1,0:T(8,128)S(1)}, bf16[2048,256]{1,0:T(8,128)(2,1)S(1)}, bf16[2048,256]{1,0:T(8,128)(2,1)S(1)}) custom-call(bf16[2048,512]{1,0:T(8,128)(2,1)S(1)} %copy-done.3, bf16[2048,512]{1,0:T(8,128)(2,1)S(1)} %copy-done.8, f32[2048,1]{1,0:T(8,128)S(1)} %copy.7.energy, f32[1,768]{1,0:T(1,128)S(1)} %psum.7.sums.m0), custom_call_target="tpu_custom_call" | custom-call | tf_op jit(solution)/shard_map/pallas_call | solution.py:20
  23.2 1.9 %copy-done = bf16[2048,1024]{1,0:T(8,128)(2,1)} copy-done((bf16[2048,1024]{1,0:T(8,128)(2,1)}, bf16[2048,1024]{1,0:T(8,128)(2,1)S(1)}, u32[]{:S(2)}) %copy-start) | copy-done | bytes 4194328
  25.1 1.4 %copy-done.6 = f32[2048,256]{1,0:T(8,128)} copy-done((f32[2048,256]{1,0:T(8,128)}, f32[2048,256]{1,0:T(8,128)S(1)}, u32[]{:S(2)}) %copy-start.6) | copy-done | bytes 2097176
  26.5 1.0 copy-done.9
  27.4 1.0 copy-done.11
  28.6 0.4 collective-permute-start.4
  29.0 0.7 collective-permute-start.6
  29.7 1.3 %collective-permute-start.3 = (bf16[2048,256]{1,0:T(8,128)(2,1)}, bf16[2048,256]{1,0:T(8,128)(2,1)S(1)}, u32[]{:S(2)}, u32[]{:S(2)}) collective-permute-start(bf16[2048,256]{1,0:T(8,128)(2,1)} %collective-permute-done.1.mid1), channel_id=1, source_target_pairs={{1,0},{2,3},{5,4},{6,7},{9,8},{10,11},{13,12},{14,15},{17,16},{18,... | collective-permute-start | bytes 3145736 | tf_op jit(solution)/shard_map/ppermute | solution.py:422
  31.0 0.7 dynamic-slice_bitcast_fusion
  31.8 0.8 collective-permute-done.5.m2
  32.7 2.9 %collective-permute-start.8 = (f32[1,768]{1,0:T(1,128)S(1)}, f32[1,768]{1,0:T(1,128)S(1)}, u32[]{:S(2)}, u32[]{:S(2)}) collective-permute-start(f32[1,768]{1,0:T(1,128)S(1)} %psum.7.sums.m0), channel_id=1, source_target_pairs={{0,3},{1,2},{2,1},{3,0},{4,7},{5,6},{6,5},{7,4},{8,11},{9,10},{10,... | collective-permute-start | bytes 9224 | tf_op jit(solution)/shard_map/ppermute | solution.py:420
  35.6 14.1 %collective-permute-done.4.sums = f32[1,768]{1,0:T(1,128)S(1)} collective-permute-done((f32[1,768]{1,0:T(1,128)S(1)}, f32[1,768]{1,0:T(1,128)S(1)}, u32[]{:S(2)}, u32[]{:S(2)}) %collective-permute-start.4) | collective-permute-done | bytes 3104 | tf_op jit(solution)/shard_map/ppermute | solution.py:421
  49.6 1.7 %collective-permute-start.12 = (bf16[2048,256]{1,0:T(8,128)(2,1)}, bf16[2048,256]{1,0:T(8,128)(2,1)S(1)}, u32[]{:S(2)}, u32[]{:S(2)}) collective-permute-start(bf16[2048,256]{1,0:T(8,128)(2,1)} %copy-done.11), channel_id=1, source_target_pairs={{0,4},{4,0},{1,5},{5,1},{2,6},{6,2},{3,7},{7,3},{8,12},{12,8},{9,1... | collective-permute-start | bytes 3145736 | tf_op jit(solution)/shard_map/ppermute | solution.py:424
  51.4 2.1 %shard_map.71.far = bf16[2048,512]{1,0:T(8,128)(2,1)S(1)} custom-call(bf16[2048,512]{1,0:T(8,128)(2,1)} %collective-permute-done.7.raw, f32[1,512]{1,0:T(1,128)S(1)} %get-tuple-element.65.mean), custom_call_target="tpu_custom_call" | custom-call | flops 3449999872 | tf_op jit(solution)/shard_map/pallas_call | solution.py:20
  53.5 0.7 copy-done.1
  54.5 3.3 %shard_map.72 = (bf16[2048,256]{1,0:T(8,128)(2,1)S(1)}, bf16[256,1536]{1,0:T(8,128)(2,1)S(1)}) custom-call(s32[6]{0:T(128)S(1)} %concatenate.3.info, bf16[2048,256]{1,0:T(8,128)(2,1)S(1)} %copy-done.5, bf16[2048,256]{1,0:T(8,128)(2,1)} %collective-permute-done.near, f32[1,768]{1,0:T(1,128)S(1)} %psum.7.sums.m0, f32[1,256]{1,0:T(1,128)S(1)} %get-tuple-element.63.m1, ...), custom_call_target="tpu_custom_call" | custom-call | tf_op jit(solution)/shard_map/pallas_call | solution.py:20
  57.8 1.3 %collective-permute-start.11 = (bf16[2048,256]{1,0:T(8,128)(2,1)S(1)}, bf16[2048,256]{1,0:T(8,128)(2,1)S(1)}, u32[]{:S(2)}, u32[]{:S(2)}) collective-permute-start(bf16[2048,256]{1,0:T(8,128)(2,1)S(1)} %collective-permute-done.6.last1), channel_id=1, source_target_pairs={{1,0},{2,3},{5,4},{6,7},{9,8},{10,11},{13,12},{14,15},{17,16},{18,... | collective-permute-start | bytes 3145736 | tf_op jit(solution)/shard_map/ppermute | solution.py:441
  59.1 1.0 collective-permute-done.3.mid2
  60.0 1.0 copy-done.12
  61.0 1.2 %copy-done.13 = bf16[2048,256]{1,0:T(8,128)(2,1)S(1)} copy-done((bf16[2048,256]{1,0:T(8,128)(2,1)S(1)}, bf16[2048,256]{1,0:T(8,128)(2,1)}, u32[]{:S(2)}) %copy-start.13) | copy-done | bytes 1048600
  62.2 6.0 %shard_map.73 = (bf16[1,256,1536]{2,1,0:T(8,128)(2,1)S(1)}, bf16[2048,512]{1,0:T(8,128)(2,1)S(1)}, bf16[1,256,768]{2,1,0:T(8,128)(2,1)S(1)}, bf16[1,256,768]{2,1,0:T(8,128)(2,1)S(1)}) custom-call(s32[6]{0:T(128)S(1)} %concatenate.3.info, bf16[2048,256]{1,0:T(8,128)(2,1)S(1)} %copy-done.5, bf16[2048,256]{1,0:T(8,128)(2,1)} %collective-permute-done.near, ...), custom_call_target="tpu_custom_call" | custom-call | flops 6899999744 | tf_op jit(solution)/shard_map/pallas_call | solution.py:20
  68.3 0.5 collective-permute-start.9
  68.8 1.5 %collective-permute-start.22 = (bf16[2048,256]{1,0:T(8,128)(2,1)S(1)}, bf16[2048,256]{1,0:T(8,128)(2,1)S(1)}, u32[]{:S(2)}, u32[]{:S(2)}) collective-permute-start(bf16[2048,256]{1,0:T(8,128)(2,1)S(1)} %copy-done.10), channel_id=1, source_target_pairs={{0,4},{4,0},{1,5},{5,1},{2,6},{6,2},{3,7},{7,3},{8,12},{12,8},{9,1... | collective-permute-start | bytes 3145736 | tf_op jit(solution)/shard_map/ppermute | solution.py:442
  70.6 0.7 shard_map.75
  71.3 1.6 %collective-permute-start.13 = (bf16[256,768]{1,0:T(8,128)(2,1)S(1)}, bf16[256,768]{1,0:T(8,128)(2,1)S(1)}, u32[]{:S(2)}, u32[]{:S(2)}) collective-permute-start(bf16[256,768]{1,0:T(8,128)(2,1)S(1)} %shard_map.75), channel_id=1, source_target_pairs={{0,16},{8,24},{16,0},{24,8},{1,17},{9,25},{17,1},{25,9},{2,18},{10... | collective-permute-start | bytes 1179656 | tf_op jit(solution)/shard_map/ppermute | solution.py:467
  72.8 3.1 %collective-permute-done.12.grads = bf16[2048,256]{1,0:T(8,128)(2,1)S(1)} collective-permute-done((bf16[2048,256]{1,0:T(8,128)(2,1)}, bf16[2048,256]{1,0:T(8,128)(2,1)S(1)}, u32[]{:S(2)}, u32[]{:S(2)}) %collective-permute-start.12) | collective-permute-done | bytes 1048608 | tf_op jit(solution)/shard_map/ppermute | solution.py:424
  76.0 0.7 shard_map.74
  76.6 1.3 %shard_map.76 = (bf16[1,256,256]{2,1,0:T(8,128)(2,1)S(1)}, bf16[1,256,256]{2,1,0:T(8,128)(2,1)S(1)}) custom-call(s32[6]{0:T(128)S(1)} %concatenate.3.info, bf16[2048,512]{1,0:T(8,128)(2,1)S(1)} %get-tuple-element.81.early, bf16[2048,256]{1,0:T(8,128)(2,1)S(1)} %get-tuple-element.86.right.chunk), custom_call_target="tpu_custom_call" | custom-call | tf_op jit(solution)/shard_map/pallas_call | solution.py:20
  78.0 1.3 %collective-permute-done.14.refs_0_.refs_6_ = bf16[1,256,256]{2,1,0:T(8,128)(2,1)S(1)} collective-permute-done((bf16[1,256,256]{2,1,0:T(8,128)(2,1)S(1)}, bf16[1,256,256]{2,1,0:T(8,128)(2,1)S(1)}, u32[]{:S(2)}, u32[]{:S(2)}) %collective-permute-start.14) | collective-permute-done | bytes 131104 | tf_op jit(solution)/shard_map/ppermute | solution.py:462
  79.4 0.6 shard_map.77
  80.0 1.8 %collective-permute-start.15 = (bf16[256,128]{1,0:T(8,128)(2,1)S(1)}, bf16[256,128]{1,0:T(8,128)(2,1)S(1)}, u32[]{:S(2)}, u32[]{:S(2)}) collective-permute-start(bf16[256,128]{1,0:T(8,128)(2,1)S(1)} %shard_map.77), channel_id=1, source_target_pairs={{0,16},{8,24},{16,0},{24,8},{1,17},{9,25},{17,1},{25,9},{2,18},{10... | collective-permute-start | bytes 196616 | tf_op jit(solution)/shard_map/ppermute | solution.py:467
  81.7 2.5 %collective-permute-done.15.refs_1_.refs_7_ = bf16[256,128]{1,0:T(8,128)(2,1)S(1)} collective-permute-done((bf16[256,128]{1,0:T(8,128)(2,1)S(1)}, bf16[256,128]{1,0:T(8,128)(2,1)S(1)}, u32[]{:S(2)}, u32[]{:S(2)}) %collective-permute-start.15) | collective-permute-done | bytes 65568 | tf_op jit(solution)/shard_map/ppermute | solution.py:467
  84.3 3.3 %shard_map.78 = (bf16[1,256,1792]{2,1,0:T(8,128)(2,1)S(1)}, bf16[2048,256]{1,0:T(8,128)(2,1)S(1)}, bf16[1,256,512]{2,1,0:T(8,128)(2,1)S(1)}, bf16[1,256,384]{2,1...) custom-call(s32[6]{0:T(128)S(1)} %concatenate.3.info, ...), custom_call_target="tpu_custom_call" | custom-call | flops 2300000000 | tf_op jit(solution)/shard_map/pallas_call | solution.py:20
  87.7 0.5 collective-permute-start.18
  88.3 0.4 collective-permute-start.19
  88.7 1.2 %collective-permute-done.17.refs_1_.refs_11_ = bf16[1,256,384]{2,1,0:T(8,128)(2,1)S(1)} collective-permute-done((bf16[1,256,384]{2,1,0:T(8,128)(2,1)S(1)}, bf16[1,256,384]{2,1,0:T(8,128)(2,1)S(1)}, u32[]{:S(2)}, u32[]{:S(2)}) %collective-permute-start.17) | collective-permute-done | bytes 196640 | tf_op jit(solution)/shard_map/ppermute | solution.py:462
  90.2 0.7 shard_map.79
  90.9 1.8 %collective-permute-start.23 = (bf16[256,896]{1,0:T(8,128)(2,1)S(1)}, bf16[256,896]{1,0:T(8,128)(2,1)S(1)}, u32[]{:S(2)}, u32[]{:S(2)}) collective-permute-start(bf16[256,896]{1,0:T(8,128)(2,1)S(1)} %shard_map.79), channel_id=1, source_target_pairs={{0,16},{8,24},{16,0},{24,8},{1,17},{9,25},{17,1},{25,9},{2,18},{10... | collective-permute-start | bytes 1376264 | tf_op jit(solution)/shard_map/ppermute | solution.py:467
  92.6 0.6 shard_map.81
  93.3 0.7 shard_map.80
  94.0 0.6 collective-permute-start.20
  94.5 2.2 %collective-permute-done.22.grads = bf16[2048,256]{1,0:T(8,128)(2,1)S(1)} collective-permute-done((bf16[2048,256]{1,0:T(8,128)(2,1)S(1)}, bf16[2048,256]{1,0:T(8,128)(2,1)S(1)}, u32[]{:S(2)}, u32[]{:S(2)}) %collective-permute-start.22) | collective-permute-done | bytes 1048608 | tf_op jit(solution)/shard_map/ppermute | solution.py:442
  96.7 0.4 shard_map.82.right
  97.2 1.5 %shard_map.84 = bf16[2,256,256]{2,1,0:T(8,128)(2,1)S(1)} custom-call(s32[6]{0:T(128)S(1)} %concatenate.3.info, bf16[2048,512]{1,0:T(8,128)(2,1)S(1)} %get-tuple-element.81.early, bf16[2048,256]{1,0:T(8,128)(2,1)S(1)} %get-tuple-element.77.second, bf16[2048,256]{1,0:T(8,128)(2,1)S(1)} %get-tuple-element.102.last, bf16[256,2048]{1,0:T(8,128)(2,1)S(1)} %shard_map.82.right), custom_call_target="tpu_custom_call" | custom-call | tf_op jit(solution)/shard_map/pallas_call | solution.py:20
  98.7 1.4 %shard_map.83.keep.refs_19_ = bf16[2,256,256]{2,1,0:T(8,128)(2,1)S(1)} custom-call(s32[6]{0:T(128)S(1)} %concatenate.3.info, bf16[2048,512]{1,0:T(8,128)(2,1)S(1)} %get-tuple-element.81.early, bf16[2048,256]{1,0:T(8,128)(2,1)S(1)} %get-tuple-element.77.second, bf16[2048,256]{1,0:T(8,128)(2,1)S(1)} %get-tuple-element.102.last, ...), custom_call_target="tpu_custom_call" | custom-call | tf_op jit(solution)/shard_map/pallas_call | solution.py:20
  100.2 0.6 shard_map.85
  100.8 1.5 %collective-permute-start.29 = (bf16[256,256]{1,0:T(8,128)(2,1)S(1)}, bf16[256,256]{1,0:T(8,128)(2,1)S(1)}, u32[]{:S(2)}, u32[]{:S(2)}) collective-permute-start(bf16[256,256]{1,0:T(8,128)(2,1)S(1)} %shard_map.85), channel_id=1, source_target_pairs={{0,16},{8,24},{16,0},{24,8},{1,17},{9,25},{17,1},{25,9},{2,18},{10... | collective-permute-start | bytes 393224 | tf_op jit(solution)/shard_map/ppermute | solution.py:454
  102.3 1.2 %collective-permute-done.23.refs_4_.refs_14_ = bf16[256,896]{1,0:T(8,128)(2,1)S(1)} collective-permute-done((bf16[256,896]{1,0:T(8,128)(2,1)S(1)}, bf16[256,896]{1,0:T(8,128)(2,1)S(1)}, u32[]{:S(2)}, u32[]{:S(2)}) %collective-permute-start.23) | collective-permute-done | bytes 458784 | tf_op jit(solution)/shard_map/ppermute | solution.py:467
  103.5 0.7 shard_map.86
  104.3 0.5 collective-permute-start.26
  104.9 0.4 collective-permute-start.28
  105.8 0.3 collective-permute-done.27.refs_17_
  106.3 0.5 collective-permute-done.29.refs_21_
  106.8 2.2 %shard_map.87 = (f32[256,1024]{1,0:T(8,128)}, f32[256,1024]{1,0:T(8,128)}) custom-call(s32[6]{0:T(128)S(1)} %concatenate.3.info, bf16[1,256,1536]{2,1,0:T(8,128)(2,1)S(1)} %get-tuple-element.73.keep.refs_0_, bf16[1,256,768]{2,1,0:T(8,128)(2,1)S(1)} %collective-permute-done.9.refs_0_.refs_1_, ...), custom_call_target="tpu_custom_call" | custom-call | tf_op jit(solution)/shard_map/pallas_call | solution.py:20
  (50 shorter events, 2.5 us)
Async XLA Ops:
  0.6 50.8 %collective-permute-start.7 = (bf16[2048,512]{1,0:T(8,128)(2,1)}, bf16[2048,512]{1,0:T(8,128)(2,1)}, u32[]{:S(2)}, u32[]{:S(2)}) collective-permute-start(bf16[2048,512]{1,0:T(8,128)(2,1)} %cols.3), channel_id=1, source_target_pairs={{0,4},{4,0},{1,5},{5,1},{2,6},{6,2},{3,7},{7,3},{8,12},{12,8},{9,1... | collective-permute-start | bytes 6291464 | tf_op jit(solution)/shard_map/ppermute | solution.py:400
  3.7 25.0 %collective-permute-start = (bf16[2048,256]{1,0:T(8,128)(2,1)}, bf16[2048,256]{1,0:T(8,128)(2,1)}, u32[]{:S(2)}, u32[]{:S(2)}) collective-permute-start(bf16[2048,256]{1,0:T(8,128)(2,1)} %own_rows.3), channel_id=1, source_target_pairs={{0,1},{1,0},{2,3},{3,2},{4,5},{5,4},{6,7},{7,6},{8,9},{9,8},{10,11... | collective-permute-start | bytes 3145736 | tf_op jit(solution)/shard_map/ppermute | solution.py:401
  5.2 23.4 %collective-permute-start.1 = (bf16[2048,256]{1,0:T(8,128)(2,1)}, bf16[2048,256]{1,0:T(8,128)(2,1)}, u32[]{:S(2)}, u32[]{:S(2)}) collective-permute-start(bf16[2048,256]{1,0:T(8,128)(2,1)} %own_rows.3), channel_id=1, source_target_pairs={{1,2},{2,1},{5,6},{6,5},{9,10},{10,9},{13,14},{14,13},{17,18},{18,... | collective-permute-start | bytes 3145736 | tf_op jit(solution)/shard_map/ppermute | solution.py:402
  6.9 1.6 %copy-start.2 = (bf16[2048,512]{1,0:T(8,128)(2,1)S(1)}, bf16[2048,512]{1,0:T(8,128)(2,1)}, u32[]{:S(2)}) copy-start(bf16[2048,512]{1,0:T(8,128)(2,1)} %cols.3) | copy-start | bytes 6291460
  8.5 1.2 %copy-start.4 = (bf16[2048,256]{1,0:T(8,128)(2,1)S(1)}, bf16[2048,256]{1,0:T(8,128)(2,1)}, u32[]{:S(2)}) copy-start(bf16[2048,256]{1,0:T(8,128)(2,1)} %own_rows.3) | copy-start | bytes 3145732
  9.7 10.3 %copy-start.14 = (f32[2048]{0:T(1024)S(1)}, f32[2048]{0:T(1024)}, u32[]{:S(2)}) copy-start(f32[2048]{0:T(1024)} %param.8) | copy-start | bytes 24580
  9.7 10.7 %copy-start.3 = (bf16[2048,512]{1,0:T(8,128)(2,1)S(1)}, bf16[2048,512]{1,0:T(8,128)(2,1)}, u32[]{:S(2)}) copy-start(bf16[2048,512]{1,0:T(8,128)(2,1)} %cols.3) | copy-start | bytes 6291460
  16.8 11.8 %collective-permute-start.2 = (f32[1,768]{1,0:T(1,128)S(1)}, f32[1,768]{1,0:T(1,128)S(1)}, u32[]{:S(2)}, u32[]{:S(2)}) collective-permute-start(f32[1,768]{1,0:T(1,128)S(1)} %psum.7.sums.m0), channel_id=1, source_target_pairs={{0,1},{1,0},{2,3},{3,2},{4,5},{5,4},{6,7},{7,6},{8,9},{9,8},{10,11... | collective-permute-start | bytes 9224 | tf_op jit(solution)/shard_map/ppermute | solution.py:406
  20.0 12.7 %collective-permute-start.5 = (f32[1,768]{1,0:T(1,128)S(1)}, f32[1,768]{1,0:T(1,128)S(1)}, u32[]{:S(2)}, u32[]{:S(2)}) collective-permute-start(f32[1,768]{1,0:T(1,128)S(1)} %psum.7.sums.m0), channel_id=1, source_target_pairs={{0,2},{1,3},{2,0},{3,1},{4,6},{5,7},{6,4},{7,5},{8,10},{9,11},{10,... | collective-permute-start | bytes 9224 | tf_op jit(solution)/shard_map/ppermute | solution.py:407
  20.4 1.6 %copy-start.8 = (bf16[2048,512]{1,0:T(8,128)(2,1)S(1)}, bf16[2048,512]{1,0:T(8,128)(2,1)}, u32[]{:S(2)}) copy-start(bf16[2048,512]{1,0:T(8,128)(2,1)} %grads.1) | copy-start | bytes 6291460
  23.1 2.0 %copy-start = (bf16[2048,1024]{1,0:T(8,128)(2,1)}, bf16[2048,1024]{1,0:T(8,128)(2,1)S(1)}, u32[]{:S(2)}) copy-start(bf16[2048,1024]{1,0:T(8,128)(2,1)S(1)} %get-tuple-element.66.ow) | copy-start | bytes 12582916
  25.1 1.4 %copy-start.6 = (f32[2048,256]{1,0:T(8,128)}, f32[2048,256]{1,0:T(8,128)S(1)}, u32[]{:S(2)}) copy-start(f32[2048,256]{1,0:T(8,128)S(1)} %get-tuple-element.78.wide) | copy-start | bytes 6291460
  26.5 1.0 copy-start.9
  27.4 1.0 copy-start.11
  28.6 21.0 %collective-permute-start.4 = (f32[1,768]{1,0:T(1,128)S(1)}, f32[1,768]{1,0:T(1,128)S(1)}, u32[]{:S(2)}, u32[]{:S(2)}) collective-permute-start(f32[1,768]{1,0:T(1,128)S(1)} %psum.7.sums.m0), channel_id=1, source_target_pairs={{0,4},{4,0},{1,5},{5,1},{2,6},{6,2},{3,7},{7,3},{8,12},{12,8},{9,1... | collective-permute-start | bytes 9224 | tf_op jit(solution)/shard_map/ppermute | solution.py:421
  29.0 28.8 %collective-permute-start.6 = (bf16[2048,256]{1,0:T(8,128)(2,1)}, bf16[2048,256]{1,0:T(8,128)(2,1)S(1)}, u32[]{:S(2)}, u32[]{:S(2)}) collective-permute-start(bf16[2048,256]{1,0:T(8,128)(2,1)} %collective-permute-done.near), channel_id=1, source_target_pairs={{1,2},{2,1},{5,6},{6,5},{9,10},{10,9},{13,14},{14,13},{17,18},{18,... | collective-permute-start | bytes 3145736 | tf_op jit(solution)/shard_map/ppermute | solution.py:423
  29.7 30.3 %collective-permute-start.3 = (bf16[2048,256]{1,0:T(8,128)(2,1)}, bf16[2048,256]{1,0:T(8,128)(2,1)S(1)}, u32[]{:S(2)}, u32[]{:S(2)}) collective-permute-start(bf16[2048,256]{1,0:T(8,128)(2,1)} %collective-permute-done.1.mid1), channel_id=1, source_target_pairs={{1,0},{2,3},{5,4},{6,7},{9,8},{10,11},{13,12},{14,15},{17,16},{18,... | collective-permute-start | bytes 3145736 | tf_op jit(solution)/shard_map/ppermute | solution.py:422
  32.7 25.1 %collective-permute-start.8 = (f32[1,768]{1,0:T(1,128)S(1)}, f32[1,768]{1,0:T(1,128)S(1)}, u32[]{:S(2)}, u32[]{:S(2)}) collective-permute-start(f32[1,768]{1,0:T(1,128)S(1)} %psum.7.sums.m0), channel_id=1, source_target_pairs={{0,3},{1,2},{2,1},{3,0},{4,7},{5,6},{6,5},{7,4},{8,11},{9,10},{10,... | collective-permute-start | bytes 9224 | tf_op jit(solution)/shard_map/ppermute | solution.py:420
  49.6 26.3 %collective-permute-start.12 = (bf16[2048,256]{1,0:T(8,128)(2,1)}, bf16[2048,256]{1,0:T(8,128)(2,1)S(1)}, u32[]{:S(2)}, u32[]{:S(2)}) collective-permute-start(bf16[2048,256]{1,0:T(8,128)(2,1)} %copy-done.11), channel_id=1, source_target_pairs={{0,4},{4,0},{1,5},{5,1},{2,6},{6,2},{3,7},{7,3},{8,12},{12,8},{9,1... | collective-permute-start | bytes 3145736 | tf_op jit(solution)/shard_map/ppermute | solution.py:424
  51.4 2.8 %copy-start.1 = (bf16[2048,1024]{1,0:T(8,128)(2,1)S(1)}, bf16[2048,1024]{1,0:T(8,128)(2,1)}, u32[]{:S(2)}) copy-start(bf16[2048,1024]{1,0:T(8,128)(2,1)} %copy-done) | copy-start | bytes 12582916
  51.4 3.1 %copy-start.5 = (bf16[2048,256]{1,0:T(8,128)(2,1)S(1)}, bf16[2048,256]{1,0:T(8,128)(2,1)}, u32[]{:S(2)}) copy-start(bf16[2048,256]{1,0:T(8,128)(2,1)} %own_rows.3) | copy-start | bytes 3145732
  57.8 26.5 %collective-permute-start.11 = (bf16[2048,256]{1,0:T(8,128)(2,1)S(1)}, bf16[2048,256]{1,0:T(8,128)(2,1)S(1)}, u32[]{:S(2)}, u32[]{:S(2)}) collective-permute-start(bf16[2048,256]{1,0:T(8,128)(2,1)S(1)} %collective-permute-done.6.last1), channel_id=1, source_target_pairs={{1,0},{2,3},{5,4},{6,7},{9,8},{10,11},{13,12},{14,15},{17,16},{18,... | collective-permute-start | bytes 3145736 | tf_op jit(solution)/shard_map/ppermute | solution.py:441
  60.0 1.0 copy-start.12
  61.0 1.2 %copy-start.13 = (bf16[2048,256]{1,0:T(8,128)(2,1)S(1)}, bf16[2048,256]{1,0:T(8,128)(2,1)}, u32[]{:S(2)}) copy-start(bf16[2048,256]{1,0:T(8,128)(2,1)} %copy-done.12) | copy-start | bytes 3145732
  62.2 6.6 %copy-start.10 = (bf16[2048,256]{1,0:T(8,128)(2,1)S(1)}, bf16[2048,256]{1,0:T(8,128)(2,1)}, u32[]{:S(2)}) copy-start(bf16[2048,256]{1,0:T(8,128)(2,1)} %copy-done.9) | copy-start | bytes 3145732
  62.2 13.7 %copy-start.7 = (f32[2048,256]{1,0:T(8,128)S(1)}, f32[2048,256]{1,0:T(8,128)}, u32[]{:S(2)}) copy-start(f32[2048,256]{1,0:T(8,128)} %copy-done.6) | copy-start | bytes 6291460
  68.3 2.1 %collective-permute-start.10 = (bf16[1,256,768]{2,1,0:T(8,128)(2,1)S(1)}, bf16[1,256,768]{2,1,0:T(8,128)(2,1)S(1)}, u32[]{:S(2)}, u32[]{:S(2)}) collective-permute-start(bf16[1,256,768]{2,1,0:T(8,128)(2,1)S(1)} %get-tuple-element.75), channel_id=1, source_target_pairs={{0,8},{8,0},{16,24},{24,16},{1,9},{9,1},{17,25},{25,17},{2,10},{10... | collective-permute-start | bytes 1179656 | tf_op jit(solution)/shard_map/ppermute | solution.py:462
  68.3 2.3 %collective-permute-start.9 = (bf16[1,256,768]{2,1,0:T(8,128)(2,1)S(1)}, bf16[1,256,768]{2,1,0:T(8,128)(2,1)S(1)}, u32[]{:S(2)}, u32[]{:S(2)}) collective-permute-start(bf16[1,256,768]{2,1,0:T(8,128)(2,1)S(1)} %get-tuple-element.74), channel_id=1, source_target_pairs={{0,8},{8,0},{16,24},{24,16},{1,9},{9,1},{17,25},{25,17},{2,10},{10... | collective-permute-start | bytes 1179656 | tf_op jit(solution)/shard_map/ppermute | solution.py:462
  68.8 27.9 %collective-permute-start.22 = (bf16[2048,256]{1,0:T(8,128)(2,1)S(1)}, bf16[2048,256]{1,0:T(8,128)(2,1)S(1)}, u32[]{:S(2)}, u32[]{:S(2)}) collective-permute-start(bf16[2048,256]{1,0:T(8,128)(2,1)S(1)} %copy-done.10), channel_id=1, source_target_pairs={{0,4},{4,0},{1,5},{5,1},{2,6},{6,2},{3,7},{7,3},{8,12},{12,8},{9,1... | collective-permute-start | bytes 3145736 | tf_op jit(solution)/shard_map/ppermute | solution.py:442
  71.3 13.0 %collective-permute-start.13 = (bf16[256,768]{1,0:T(8,128)(2,1)S(1)}, bf16[256,768]{1,0:T(8,128)(2,1)S(1)}, u32[]{:S(2)}, u32[]{:S(2)}) collective-permute-start(bf16[256,768]{1,0:T(8,128)(2,1)S(1)} %shard_map.75), channel_id=1, source_target_pairs={{0,16},{8,24},{16,0},{24,8},{1,17},{9,25},{17,1},{25,9},{2,18},{10... | collective-permute-start | bytes 1179656 | tf_op jit(solution)/shard_map/ppermute | solution.py:467
  78.0 1.4 %collective-permute-start.14 = (bf16[1,256,256]{2,1,0:T(8,128)(2,1)S(1)}, bf16[1,256,256]{2,1,0:T(8,128)(2,1)S(1)}, u32[]{:S(2)}, u32[]{:S(2)}) collective-permute-start(bf16[1,256,256]{2,1,0:T(8,128)(2,1)S(1)} %get-tuple-element.83), channel_id=1, source_target_pairs={{0,8},{8,0},{16,24},{24,16},{1,9},{9,1},{17,25},{25,17},{2,10},{10... | collective-permute-start | bytes 393224 | tf_op jit(solution)/shard_map/ppermute | solution.py:462
  80.0 4.3 %collective-permute-start.15 = (bf16[256,128]{1,0:T(8,128)(2,1)S(1)}, bf16[256,128]{1,0:T(8,128)(2,1)S(1)}, u32[]{:S(2)}, u32[]{:S(2)}) collective-permute-start(bf16[256,128]{1,0:T(8,128)(2,1)S(1)} %shard_map.77), channel_id=1, source_target_pairs={{0,16},{8,24},{16,0},{24,8},{1,17},{9,25},{17,1},{25,9},{2,18},{10... | collective-permute-start | bytes 196616 | tf_op jit(solution)/shard_map/ppermute | solution.py:467
  87.6 2.5 %collective-permute-start.16 = (bf16[1,256,512]{2,1,0:T(8,128)(2,1)S(1)}, bf16[1,256,512]{2,1,0:T(8,128)(2,1)S(1)}, u32[]{:S(2)}, u32[]{:S(2)}) collective-permute-start(bf16[1,256,512]{2,1,0:T(8,128)(2,1)S(1)} %get-tuple-element.90), channel_id=1, source_target_pairs={{0,8},{8,0},{16,24},{24,16},{1,9},{9,1},{17,25},{25,17},{2,10},{10... | collective-permute-start | bytes 786440 | tf_op jit(solution)/shard_map/ppermute | solution.py:462
  87.7 2.5 %collective-permute-start.18 = (bf16[1,256,512]{2,1,0:T(8,128)(2,1)S(1)}, bf16[1,256,512]{2,1,0:T(8,128)(2,1)S(1)}, u32[]{:S(2)}, u32[]{:S(2)}) collective-permute-start(bf16[1,256,512]{2,1,0:T(8,128)(2,1)S(1)} %get-tuple-element.92), channel_id=1, source_target_pairs={{0,8},{8,0},{16,24},{24,16},{1,9},{9,1},{17,25},{25,17},{2,10},{10... | collective-permute-start | bytes 786440 | tf_op jit(solution)/shard_map/ppermute | solution.py:462
  88.2 1.7 %collective-permute-start.17 = (bf16[1,256,384]{2,1,0:T(8,128)(2,1)S(1)}, bf16[1,256,384]{2,1,0:T(8,128)(2,1)S(1)}, u32[]{:S(2)}, u32[]{:S(2)}) collective-permute-start(bf16[1,256,384]{2,1,0:T(8,128)(2,1)S(1)} %get-tuple-element.91), channel_id=1, source_target_pairs={{0,8},{8,0},{16,24},{24,16},{1,9},{9,1},{17,25},{25,17},{2,10},{10... | collective-permute-start | bytes 589832 | tf_op jit(solution)/shard_map/ppermute | solution.py:462
  88.3 1.9 %collective-permute-start.19 = (bf16[1,256,384]{2,1,0:T(8,128)(2,1)S(1)}, bf16[1,256,384]{2,1,0:T(8,128)(2,1)S(1)}, u32[]{:S(2)}, u32[]{:S(2)}) collective-permute-start(bf16[1,256,384]{2,1,0:T(8,128)(2,1)S(1)} %get-tuple-element.93), channel_id=1, source_target_pairs={{0,8},{8,0},{16,24},{24,16},{1,9},{9,1},{17,25},{25,17},{2,10},{10... | collective-permute-start | bytes 589832 | tf_op jit(solution)/shard_map/ppermute | solution.py:462
  90.9 12.6 %collective-permute-start.23 = (bf16[256,896]{1,0:T(8,128)(2,1)S(1)}, bf16[256,896]{1,0:T(8,128)(2,1)S(1)}, u32[]{:S(2)}, u32[]{:S(2)}) collective-permute-start(bf16[256,896]{1,0:T(8,128)(2,1)S(1)} %shard_map.79), channel_id=1, source_target_pairs={{0,16},{8,24},{16,0},{24,8},{1,17},{9,25},{17,1},{25,9},{2,18},{10... | collective-permute-start | bytes 1376264 | tf_op jit(solution)/shard_map/ppermute | solution.py:467
  93.2 3.9 %collective-permute-start.21 = (bf16[256,128]{1,0:T(8,128)(2,1)S(1)}, bf16[256,128]{1,0:T(8,128)(2,1)S(1)}, u32[]{:S(2)}, u32[]{:S(2)}) collective-permute-start(bf16[256,128]{1,0:T(8,128)(2,1)S(1)} %shard_map.81), channel_id=1, source_target_pairs={{0,8},{8,0},{16,24},{24,16},{1,9},{9,1},{17,25},{25,17},{2,10},{10... | collective-permute-start | bytes 196616 | tf_op jit(solution)/shard_map/ppermute | solution.py:479
  94.0 3.2 %collective-permute-start.20 = (bf16[256,768]{1,0:T(8,128)(2,1)S(1)}, bf16[256,768]{1,0:T(8,128)(2,1)S(1)}, u32[]{:S(2)}, u32[]{:S(2)}) collective-permute-start(bf16[256,768]{1,0:T(8,128)(2,1)S(1)} %shard_map.80), channel_id=1, source_target_pairs={{0,8},{8,0},{16,24},{24,16},{1,9},{9,1},{17,25},{25,17},{2,10},{10... | collective-permute-start | bytes 1179656 | tf_op jit(solution)/shard_map/ppermute | solution.py:479
  98.6 1.6 %collective-permute-start.24 = (bf16[2,256,256]{2,1,0:T(8,128)(2,1)S(1)}, bf16[2,256,256]{2,1,0:T(8,128)(2,1)S(1)}, u32[]{:S(2)}, u32[]{:S(2)}) collective-permute-start(bf16[2,256,256]{2,1,0:T(8,128)(2,1)S(1)} %shard_map.84), channel_id=1, source_target_pairs={{0,8},{8,0},{16,24},{24,16},{1,9},{9,1},{17,25},{25,17},{2,10},{10... | collective-permute-start | bytes 786440 | tf_op jit(solution)/shard_map/ppermute | solution.py:447
  100.8 5.9 %collective-permute-start.29 = (bf16[256,256]{1,0:T(8,128)(2,1)S(1)}, bf16[256,256]{1,0:T(8,128)(2,1)S(1)}, u32[]{:S(2)}, u32[]{:S(2)}) collective-permute-start(bf16[256,256]{1,0:T(8,128)(2,1)S(1)} %shard_map.85), channel_id=1, source_target_pairs={{0,16},{8,24},{16,0},{24,8},{1,17},{9,25},{17,1},{25,9},{2,18},{10... | collective-permute-start | bytes 393224 | tf_op jit(solution)/shard_map/ppermute | solution.py:454
  104.2 1.4 %collective-permute-start.25 = (bf16[64,896]{1,0:T(8,128)(2,1)S(1)}, bf16[64,896]{1,0:T(8,128)(2,1)S(1)}, u32[]{:S(2)}, u32[]{:S(2)}) collective-permute-start(bf16[64,896]{1,0:T(8,128)(2,1)S(1)} %get-tuple-element.106), channel_id=1, source_target_pairs={{0,8},{8,0},{16,24},{24,16},{1,9},{9,1},{17,25},{25,17},{2,10},{10... | collective-permute-start | bytes 344072 | tf_op jit(solution)/shard_map/ppermute | solution.py:479
  104.3 1.5 %collective-permute-start.26 = (bf16[64,896]{1,0:T(8,128)(2,1)S(1)}, bf16[64,896]{1,0:T(8,128)(2,1)S(1)}, u32[]{:S(2)}, u32[]{:S(2)}) collective-permute-start(bf16[64,896]{1,0:T(8,128)(2,1)S(1)} %get-tuple-element.107), channel_id=1, source_target_pairs={{0,8},{8,0},{16,24},{24,16},{1,9},{9,1},{17,25},{25,17},{2,10},{10... | collective-permute-start | bytes 344072 | tf_op jit(solution)/shard_map/ppermute | solution.py:479
  104.8 1.3 %collective-permute-start.27 = (bf16[64,896]{1,0:T(8,128)(2,1)S(1)}, bf16[64,896]{1,0:T(8,128)(2,1)S(1)}, u32[]{:S(2)}, u32[]{:S(2)}) collective-permute-start(bf16[64,896]{1,0:T(8,128)(2,1)S(1)} %get-tuple-element.108), channel_id=1, source_target_pairs={{0,8},{8,0},{16,24},{24,16},{1,9},{9,1},{17,25},{25,17},{2,10},{10... | collective-permute-start | bytes 344072 | tf_op jit(solution)/shard_map/ppermute | solution.py:479
  104.9 1.4 %collective-permute-start.28 = (bf16[64,896]{1,0:T(8,128)(2,1)S(1)}, bf16[64,896]{1,0:T(8,128)(2,1)S(1)}, u32[]{:S(2)}, u32[]{:S(2)}) collective-permute-start(bf16[64,896]{1,0:T(8,128)(2,1)S(1)} %get-tuple-element.109), channel_id=1, source_target_pairs={{0,8},{8,0},{16,24},{24,16},{1,9},{9,1},{17,25},{25,17},{2,10},{10... | collective-permute-start | bytes 344072 | tf_op jit(solution)/shard_map/ppermute | solution.py:479

commit v6 on v4

--- a/solution.py
+++ b/solution.py
@@ -12,8 +12,8 @@
 VMEM = pl.BlockSpec(memory_space=pltpu.VMEM)
 SMEM = pl.BlockSpec(memory_space=pltpu.SMEM)
 MID, LOW, CORE, STRAIGHT, TABLE = 0, 1, 2, 3, 4
-MEAN_COST, FAR_COST, EARLY_COST, FIRST_COST, LAST_COST = 6, 3, 4, 0, 4
-WEIGH_COST, HOPS = 12, 4
+MEAN_COST, FAR_COST, EARLY_COST, FIRST_COST, LAST_COST = 6, 3, 4, 0, 0
+WEIGH_COST, HOPS = 16, 4
 
 
 def call(kernel, outs, *args, scratch=(), limit=24, cost=0, out_spec=VMEM):
@@ -384,8 +384,8 @@
         ]
 
     far_raw = lax.ppermute(o_cols, "prow", flip)
+    mid1 = lax.ppermute(o_rows, "pcol", inner)
     near = lax.ppermute(o_rows, "pcol", outer)
-    mid1 = lax.ppermute(o_rows, "pcol", inner)
 
     (sums,) = call(sums_kernel, [((1, rw + cw), F32)], o_rows, o_cols)
     m0 = lax.psum(sums, "walker")
@@ -473,7 +473,7 @@
 
     e_keep, early, *sends = call(
         functools.partial(early_kernel, count, per, place),
-        message_shapes(3 * cw) + [((samples, 2 * rw), BF)] + message_shapes(*[3 * cw // 4] * 4),
+        message_shapes(3 * cw) + [((samples, 2 * rw), BF)] + message_shapes(*[3 * cw // 2] * 2),
         info, o_rows, near, mid1, mid2, m0, m1, m2, m3, ow, far,
         cost=EARLY_COST,
     )

time: 110 us -> 110 us (level)
  local copies, waits for them, and re-layouts: 11.9 us -> 14 us
  waiting for transfers between devices: 32.1 us -> 30.9 us
    unnamed x26 -> x30, local copies, waits for them, and re-layouts: 10.7 us -> 12.9 us
    ppermute x9 -> x7, waiting for transfers between devices: 4.94 us -> 3.08 us  [reduce_rows(): gots = [lax.ppermute(send, 'walker', other_core) for send in sends]]
    ppermute x1, waiting for transfers between devices: 1.96 us -> 3.12 us  [per_device(): far_grads = [lax.ppermute(grads[0], 'prow', flip)]]
  transfers between devices with their start and end apart: 32 -> 30, of which waited for: 20 -> 18; matrix products, arithmetic and copies ran while one was open for 1% -> 1% of each run, Pallas kernels for 23% -> 23%
where the time goes in v6:
time: 110 us; the launch traced here: 109 us
  waiting for transfers between devices  30.9 us (28%)
  starting transfers between devices  29.3 us (27%)
  Pallas kernels  27.5 us (25%)
  local copies, waits for them, and re-layouts  14 us (13%)
  blocking collectives  6.55 us (6%)
    pallas_call x19, Pallas kernels, call(): pl.pallas_call(kernel, out_shape=[jax.ShapeDtypeStruct(s, d) for s, d in...  27.5 us
    ppermute x1, waiting for transfers between devices, per_device(): far_sums = lax.ppermute(m0, 'prow', flip)  14.1 us
    unnamed x30, local copies, waits for them, and re-layouts  12.9 us
    psum x1, blocking collectives, per_device(): m0 = lax.psum(sums, 'walker')  6.55 us
    ppermute x3, starting transfers between devices, reduce_rows(): got_x = lax.ppermute(sent[0], 'walker', [(v, v ^ 2) for v in range(4)])  5.13 us
    ppermute x1, starting transfers between devices, per_device(): m1 = lax.ppermute(m0, 'pcol', outer)  3.21 us
    ppermute x3, waiting for transfers between devices, reduce_rows(): got_x = lax.ppermute(sent[0], 'walker', [(v, v ^ 2) for v in range(4)])  3.18 us
    ppermute x1, waiting for transfers between devices, per_device(): far_grads = [lax.ppermute(grads[0], 'prow', flip)]  3.12 us
  transfers between devices with their start and end apart: 30, of which 18 were waited for; matrix products, arithmetic and copies ran while one was open for 1% of the time, Pallas kernels for 23%

profile of v6, /device:TPU:0, one launch (start us, length us, event | category | flops | bytes accessed | tf_op | source)
XLA Modules:
  0.0 109.3 jit_solution(12528230673136282606)
XLA Ops:
  0.6 3.0 %collective-permute-start.7 = (bf16[2048,512]{1,0:T(8,128)(2,1)}, bf16[2048,512]{1,0:T(8,128)(2,1)}, u32[]{:S(2)}, u32[]{:S(2)}) collective-permute-start(bf16[2048,512]{1,0:T(8,128)(2,1)} %cols.3), channel_id=1, source_target_pairs={{0,4},{4,0},{1,5},{5,1},{2,6},{6,2},{3,7},{7,3},{8,12},{12,8},{9,1... | collective-permute-start | bytes 6291464 | tf_op jit(solution)/shard_map/ppermute | solution.py:386
  3.7 1.6 %collective-permute-start = (bf16[2048,256]{1,0:T(8,128)(2,1)}, bf16[2048,256]{1,0:T(8,128)(2,1)}, u32[]{:S(2)}, u32[]{:S(2)}) collective-permute-start(bf16[2048,256]{1,0:T(8,128)(2,1)} %own_rows.3), channel_id=1, source_target_pairs={{0,1},{1,0},{2,3},{3,2},{4,5},{5,4},{6,7},{7,6},{8,9},{9,8},{10,11... | collective-permute-start | bytes 3145736 | tf_op jit(solution)/shard_map/ppermute | solution.py:388
  5.2 1.6 %collective-permute-start.1 = (bf16[2048,256]{1,0:T(8,128)(2,1)}, bf16[2048,256]{1,0:T(8,128)(2,1)}, u32[]{:S(2)}, u32[]{:S(2)}) collective-permute-start(bf16[2048,256]{1,0:T(8,128)(2,1)} %own_rows.3), channel_id=1, source_target_pairs={{1,2},{2,1},{5,6},{6,5},{9,10},{10,9},{13,14},{14,13},{17,18},{18,... | collective-permute-start | bytes 3145736 | tf_op jit(solution)/shard_map/ppermute | solution.py:387
  6.9 1.6 %copy-done.2 = bf16[2048,512]{1,0:T(8,128)(2,1)S(1)} copy-done((bf16[2048,512]{1,0:T(8,128)(2,1)S(1)}, bf16[2048,512]{1,0:T(8,128)(2,1)}, u32[]{:S(2)}) %copy-start.2) | copy-done | bytes 2097176
  8.5 1.2 %copy-done.4 = bf16[2048,256]{1,0:T(8,128)(2,1)S(1)} copy-done((bf16[2048,256]{1,0:T(8,128)(2,1)S(1)}, bf16[2048,256]{1,0:T(8,128)(2,1)}, u32[]{:S(2)}) %copy-start.4) | copy-done | bytes 1048600
  9.7 0.5 shard_map.68
  10.2 6.6 %psum.7.sums.m0 = f32[1,768]{1,0:T(1,128)S(1)} all-reduce(f32[1,768]{1,0:T(1,128)S(1)} %shard_map.68), channel_id=1, replica_groups=mesh['walker'=4,'prow'=2,'pcol'=4] {'walker'}, use_global_device_ids=true, to_apply=%region_0.1 | all-reduce | flops 768 | bytes 6144 | tf_op jit(solution)/shard_map/psum | solution.py:391
  16.8 3.2 %collective-permute-start.2 = (f32[1,768]{1,0:T(1,128)S(1)}, f32[1,768]{1,0:T(1,128)S(1)}, u32[]{:S(2)}, u32[]{:S(2)}) collective-permute-start(f32[1,768]{1,0:T(1,128)S(1)} %psum.7.sums.m0), channel_id=1, source_target_pairs={{0,1},{1,0},{2,3},{3,2},{4,5},{5,4},{6,7},{7,6},{8,9},{9,8},{10,11... | collective-permute-start | bytes 9224 | tf_op jit(solution)/shard_map/ppermute | solution.py:392
  20.0 0.4 copy.7.energy
  20.4 1.6 %copy-done.8 = bf16[2048,512]{1,0:T(8,128)(2,1)S(1)} copy-done((bf16[2048,512]{1,0:T(8,128)(2,1)S(1)}, bf16[2048,512]{1,0:T(8,128)(2,1)}, u32[]{:S(2)}) %copy-start.8) | copy-done | bytes 2097176
  22.0 1.2 %shard_map.69 = (bf16[2048,1024]{1,0:T(8,128)(2,1)S(1)}, f32[2048,256]{1,0:T(8,128)S(1)}, bf16[2048,256]{1,0:T(8,128)(2,1)S(1)}, bf16[2048,256]{1,0:T(8,128)(2,1)S(1)}) custom-call(bf16[2048,512]{1,0:T(8,128)(2,1)S(1)} %copy-done.3, bf16[2048,512]{1,0:T(8,128)(2,1)S(1)} %copy-done.8, f32[2048,1]{1,0:T(8,128)S(1)} %copy.7.energy, f32[1,768]{1,0:T(1,128)S(1)} %psum.7.sums.m0), custom_call_target="tpu_custom_call" | custom-call | tf_op jit(solution)/shard_map/pallas_call | solution.py:20
  23.2 2.0 %copy-done = bf16[2048,1024]{1,0:T(8,128)(2,1)} copy-done((bf16[2048,1024]{1,0:T(8,128)(2,1)}, bf16[2048,1024]{1,0:T(8,128)(2,1)S(1)}, u32[]{:S(2)}) %copy-start) | copy-done | bytes 4194328
  25.1 1.4 %copy-done.6 = f32[2048,256]{1,0:T(8,128)} copy-done((f32[2048,256]{1,0:T(8,128)}, f32[2048,256]{1,0:T(8,128)S(1)}, u32[]{:S(2)}) %copy-start.6) | copy-done | bytes 2097176
  26.5 1.0 copy-done.9
  27.4 1.0 copy-done.11
  28.6 0.4 collective-permute-start.4
  29.0 0.7 collective-permute-start.6
  29.7 1.3 %collective-permute-start.3 = (bf16[2048,256]{1,0:T(8,128)(2,1)}, bf16[2048,256]{1,0:T(8,128)(2,1)S(1)}, u32[]{:S(2)}, u32[]{:S(2)}) collective-permute-start(bf16[2048,256]{1,0:T(8,128)(2,1)} %collective-permute-done.1.mid1), channel_id=1, source_target_pairs={{1,0},{2,3},{5,4},{6,7},{9,8},{10,11},{13,12},{14,15},{17,16},{18,... | collective-permute-start | bytes 3145736 | tf_op jit(solution)/shard_map/ppermute | solution.py:408
  31.0 0.7 dynamic-slice_bitcast_fusion
  31.8 0.8 collective-permute-done.5.m2
  32.7 2.9 %collective-permute-start.8 = (f32[1,768]{1,0:T(1,128)S(1)}, f32[1,768]{1,0:T(1,128)S(1)}, u32[]{:S(2)}, u32[]{:S(2)}) collective-permute-start(f32[1,768]{1,0:T(1,128)S(1)} %psum.7.sums.m0), channel_id=1, source_target_pairs={{0,3},{1,2},{2,1},{3,0},{4,7},{5,6},{6,5},{7,4},{8,11},{9,10},{10,... | collective-permute-start | bytes 9224 | tf_op jit(solution)/shard_map/ppermute | solution.py:406
  35.6 14.1 %collective-permute-done.4.sums = f32[1,768]{1,0:T(1,128)S(1)} collective-permute-done((f32[1,768]{1,0:T(1,128)S(1)}, f32[1,768]{1,0:T(1,128)S(1)}, u32[]{:S(2)}, u32[]{:S(2)}) %collective-permute-start.4) | collective-permute-done | bytes 3104 | tf_op jit(solution)/shard_map/ppermute | solution.py:407
  49.6 1.7 %collective-permute-start.12 = (bf16[2048,256]{1,0:T(8,128)(2,1)}, bf16[2048,256]{1,0:T(8,128)(2,1)S(1)}, u32[]{:S(2)}, u32[]{:S(2)}) collective-permute-start(bf16[2048,256]{1,0:T(8,128)(2,1)} %copy-done.11), channel_id=1, source_target_pairs={{0,4},{4,0},{1,5},{5,1},{2,6},{6,2},{3,7},{7,3},{8,12},{12,8},{9,1... | collective-permute-start | bytes 3145736 | tf_op jit(solution)/shard_map/ppermute | solution.py:410
  51.4 2.1 %shard_map.71.far = bf16[2048,512]{1,0:T(8,128)(2,1)S(1)} custom-call(bf16[2048,512]{1,0:T(8,128)(2,1)} %collective-permute-done.7.raw, f32[1,512]{1,0:T(1,128)S(1)} %get-tuple-element.67.mean), custom_call_target="tpu_custom_call" | custom-call | flops 3449999872 | tf_op jit(solution)/shard_map/pallas_call | solution.py:20
  53.5 0.7 copy-done.1
  54.5 3.3 %shard_map.72 = (bf16[2048,256]{1,0:T(8,128)(2,1)S(1)}, bf16[256,1536]{1,0:T(8,128)(2,1)S(1)}) custom-call(s32[6]{0:T(128)S(1)} %concatenate.3.info, bf16[2048,256]{1,0:T(8,128)(2,1)S(1)} %copy-done.5, bf16[2048,256]{1,0:T(8,128)(2,1)} %collective-permute-done.near, f32[1,768]{1,0:T(1,128)S(1)} %psum.7.sums.m0, f32[1,256]{1,0:T(1,128)S(1)} %get-tuple-element.65.m1, ...), custom_call_target="tpu_custom_call" | custom-call | tf_op jit(solution)/shard_map/pallas_call | solution.py:20
  57.8 1.3 %collective-permute-start.11 = (bf16[2048,256]{1,0:T(8,128)(2,1)S(1)}, bf16[2048,256]{1,0:T(8,128)(2,1)S(1)}, u32[]{:S(2)}, u32[]{:S(2)}) collective-permute-start(bf16[2048,256]{1,0:T(8,128)(2,1)S(1)} %collective-permute-done.6.last1), channel_id=1, source_target_pairs={{1,0},{2,3},{5,4},{6,7},{9,8},{10,11},{13,12},{14,15},{17,16},{18,... | collective-permute-start | bytes 3145736 | tf_op jit(solution)/shard_map/ppermute | solution.py:427
  59.1 1.0 collective-permute-done.3.mid2
  60.0 1.0 copy-done.12
  61.0 1.2 %copy-done.13 = bf16[2048,256]{1,0:T(8,128)(2,1)S(1)} copy-done((bf16[2048,256]{1,0:T(8,128)(2,1)S(1)}, bf16[2048,256]{1,0:T(8,128)(2,1)}, u32[]{:S(2)}) %copy-start.13) | copy-done | bytes 1048600
  62.2 6.0 %shard_map.73 = (bf16[1,256,1536]{2,1,0:T(8,128)(2,1)S(1)}, bf16[2048,512]{1,0:T(8,128)(2,1)S(1)}, bf16[1,256,768]{2,1,0:T(8,128)(2,1)S(1)}, bf16[1,256,768]{2,1,0:T(8,128)(2,1)S(1)}) custom-call(s32[6]{0:T(128)S(1)} %concatenate.3.info, bf16[2048,256]{1,0:T(8,128)(2,1)S(1)} %copy-done.5, bf16[2048,256]{1,0:T(8,128)(2,1)} %collective-permute-done.near, ...), custom_call_target="tpu_custom_call" | custom-call | flops 4600000000 | tf_op jit(solution)/shard_map/pallas_call | solution.py:20
  68.3 0.5 collective-permute-start.9
  68.8 1.5 %collective-permute-start.22 = (bf16[2048,256]{1,0:T(8,128)(2,1)S(1)}, bf16[2048,256]{1,0:T(8,128)(2,1)S(1)}, u32[]{:S(2)}, u32[]{:S(2)}) collective-permute-start(bf16[2048,256]{1,0:T(8,128)(2,1)S(1)} %copy-done.10), channel_id=1, source_target_pairs={{0,4},{4,0},{1,5},{5,1},{2,6},{6,2},{3,7},{7,3},{8,12},{12,8},{9,1... | collective-permute-start | bytes 3145736 | tf_op jit(solution)/shard_map/ppermute | solution.py:428
  70.6 0.7 shard_map.75
  71.3 1.6 %collective-permute-start.13 = (bf16[256,768]{1,0:T(8,128)(2,1)S(1)}, bf16[256,768]{1,0:T(8,128)(2,1)S(1)}, u32[]{:S(2)}, u32[]{:S(2)}) collective-permute-start(bf16[256,768]{1,0:T(8,128)(2,1)S(1)} %shard_map.75), channel_id=1, source_target_pairs={{0,16},{8,24},{16,0},{24,8},{1,17},{9,25},{17,1},{25,9},{2,18},{10... | collective-permute-start | bytes 1179656 | tf_op jit(solution)/shard_map/ppermute | solution.py:453
  72.8 3.1 %collective-permute-done.12.grads = bf16[2048,256]{1,0:T(8,128)(2,1)S(1)} collective-permute-done((bf16[2048,256]{1,0:T(8,128)(2,1)}, bf16[2048,256]{1,0:T(8,128)(2,1)S(1)}, u32[]{:S(2)}, u32[]{:S(2)}) %collective-permute-start.12) | collective-permute-done | bytes 1048608 | tf_op jit(solution)/shard_map/ppermute | solution.py:410
  76.0 0.7 shard_map.74
  76.6 1.3 %shard_map.76 = (bf16[1,256,256]{2,1,0:T(8,128)(2,1)S(1)}, bf16[1,256,256]{2,1,0:T(8,128)(2,1)S(1)}) custom-call(s32[6]{0:T(128)S(1)} %concatenate.3.info, bf16[2048,512]{1,0:T(8,128)(2,1)S(1)} %get-tuple-element.83.early, bf16[2048,256]{1,0:T(8,128)(2,1)S(1)} %get-tuple-element.88.right.chunk), custom_call_target="tpu_custom_call" | custom-call | tf_op jit(solution)/shard_map/pallas_call | solution.py:20
  78.0 1.3 %collective-permute-done.14.refs_0_.refs_6_ = bf16[1,256,256]{2,1,0:T(8,128)(2,1)S(1)} collective-permute-done((bf16[1,256,256]{2,1,0:T(8,128)(2,1)S(1)}, bf16[1,256,256]{2,1,0:T(8,128)(2,1)S(1)}, u32[]{:S(2)}, u32[]{:S(2)}) %collective-permute-start.14) | collective-permute-done | bytes 131104 | tf_op jit(solution)/shard_map/ppermute | solution.py:448
  79.4 0.6 shard_map.77
  80.0 1.8 %collective-permute-start.15 = (bf16[256,128]{1,0:T(8,128)(2,1)S(1)}, bf16[256,128]{1,0:T(8,128)(2,1)S(1)}, u32[]{:S(2)}, u32[]{:S(2)}) collective-permute-start(bf16[256,128]{1,0:T(8,128)(2,1)S(1)} %shard_map.77), channel_id=1, source_target_pairs={{0,16},{8,24},{16,0},{24,8},{1,17},{9,25},{17,1},{25,9},{2,18},{10... | collective-permute-start | bytes 196616 | tf_op jit(solution)/shard_map/ppermute | solution.py:453
  81.7 2.5 %collective-permute-done.15.refs_1_.refs_7_ = bf16[256,128]{1,0:T(8,128)(2,1)S(1)} collective-permute-done((bf16[256,128]{1,0:T(8,128)(2,1)S(1)}, bf16[256,128]{1,0:T(8,128)(2,1)S(1)}, u32[]{:S(2)}, u32[]{:S(2)}) %collective-permute-start.15) | collective-permute-done | bytes 65568 | tf_op jit(solution)/shard_map/ppermute | solution.py:453
  84.3 3.3 %shard_map.78 = (bf16[1,256,1792]{2,1,0:T(8,128)(2,1)S(1)}, bf16[2048,256]{1,0:T(8,128)(2,1)S(1)}, bf16[1,256,512]{2,1,0:T(8,128)(2,1)S(1)}, bf16[1,256,384]{2,1...) custom-call(s32[6]{0:T(128)S(1)} %concatenate.3.info, ...), custom_call_target="tpu_custom_call" | custom-call | tf_op jit(solution)/shard_map/pallas_call | solution.py:20
  87.7 0.5 collective-permute-start.18
  88.3 0.4 collective-permute-start.19
  88.7 1.2 %collective-permute-done.17.refs_1_.refs_11_ = bf16[1,256,384]{2,1,0:T(8,128)(2,1)S(1)} collective-permute-done((bf16[1,256,384]{2,1,0:T(8,128)(2,1)S(1)}, bf16[1,256,384]{2,1,0:T(8,128)(2,1)S(1)}, u32[]{:S(2)}, u32[]{:S(2)}) %collective-permute-start.17) | collective-permute-done | bytes 196640 | tf_op jit(solution)/shard_map/ppermute | solution.py:448
  90.2 0.7 shard_map.79
  90.8 1.8 %collective-permute-start.23 = (bf16[256,896]{1,0:T(8,128)(2,1)S(1)}, bf16[256,896]{1,0:T(8,128)(2,1)S(1)}, u32[]{:S(2)}, u32[]{:S(2)}) collective-permute-start(bf16[256,896]{1,0:T(8,128)(2,1)S(1)} %shard_map.79), channel_id=1, source_target_pairs={{0,16},{8,24},{16,0},{24,8},{1,17},{9,25},{17,1},{25,9},{2,18},{10... | collective-permute-start | bytes 1376264 | tf_op jit(solution)/shard_map/ppermute | solution.py:453
  92.6 0.6 shard_map.81
  93.3 0.7 shard_map.80
  94.0 0.6 collective-permute-start.20
  94.5 2.2 %collective-permute-done.22.grads = bf16[2048,256]{1,0:T(8,128)(2,1)S(1)} collective-permute-done((bf16[2048,256]{1,0:T(8,128)(2,1)S(1)}, bf16[2048,256]{1,0:T(8,128)(2,1)S(1)}, u32[]{:S(2)}, u32[]{:S(2)}) %collective-permute-start.22) | collective-permute-done | bytes 1048608 | tf_op jit(solution)/shard_map/ppermute | solution.py:428
  96.7 0.4 shard_map.82.right_ref
  97.1 2.1 %shard_map.83 = (bf16[2,256,256]{2,1,0:T(8,128)(2,1)S(1)}, bf16[2,256,256]{2,1,0:T(8,128)(2,1)S(1)}) custom-call(s32[6]{0:T(128)S(1)} %concatenate.3.info, bf16[2048,512]{1,0:T(8,128)(2,1)S(1)} %get-tuple-element.83.early, bf16[2048,256]{1,0:T(8,128)(2,1)S(1)} %get-tuple-element.79.second, bf16[2048,256]{1,0:T(8,128)(2,1)S(1)} %get-tuple-element.104.last, ...), custom_call_target="tpu_custom_call" | custom-call | tf_op jit(solution)/shard_map/pallas_call | solution.py:20
  99.3 1.5 %collective-permute-done.24.refs_0_.refs_20_ = bf16[2,256,256]{2,1,0:T(8,128)(2,1)S(1)} collective-permute-done((bf16[2,256,256]{2,1,0:T(8,128)(2,1)S(1)}, bf16[2,256,256]{2,1,0:T(8,128)(2,1)S(1)}, u32[]{:S(2)}, u32[]{:S(2)}) %collective-permute-start.24) | collective-permute-done | bytes 262176 | tf_op jit(solution)/shard_map/ppermute | solution.py:433
  100.8 0.6 shard_map.84
  101.4 1.5 %collective-permute-start.29 = (bf16[256,256]{1,0:T(8,128)(2,1)S(1)}, bf16[256,256]{1,0:T(8,128)(2,1)S(1)}, u32[]{:S(2)}, u32[]{:S(2)}) collective-permute-start(bf16[256,256]{1,0:T(8,128)(2,1)S(1)} %shard_map.84), channel_id=1, source_target_pairs={{0,16},{8,24},{16,0},{24,8},{1,17},{9,25},{17,1},{25,9},{2,18},{10... | collective-permute-start | bytes 393224 | tf_op jit(solution)/shard_map/ppermute | solution.py:440
  102.8 0.6 collective-permute-done.23.refs_4_.refs_14_
  103.5 0.7 shard_map.85
  104.3 0.5 collective-permute-start.26
  104.9 0.4 collective-permute-start.28
  105.8 0.3 collective-permute-done.27.refs_17_
  106.3 0.7 collective-permute-done.29.refs_21_
  107.0 2.2 %shard_map.86 = (f32[256,1024]{1,0:T(8,128)}, f32[256,1024]{1,0:T(8,128)}) custom-call(s32[6]{0:T(128)S(1)} %concatenate.3.info, bf16[1,256,1536]{2,1,0:T(8,128)(2,1)S(1)} %get-tuple-element.75.keep.refs_0_, bf16[1,256,768]{2,1,0:T(8,128)(2,1)S(1)} %collective-permute-done.9.refs_0_.refs_1_, ...), custom_call_target="tpu_custom_call" | custom-call | tf_op jit(solution)/shard_map/pallas_call | solution.py:20
  (49 shorter events, 2.5 us)
Async XLA Ops:
  0.6 50.8 %collective-permute-start.7 = (bf16[2048,512]{1,0:T(8,128)(2,1)}, bf16[2048,512]{1,0:T(8,128)(2,1)}, u32[]{:S(2)}, u32[]{:S(2)}) collective-permute-start(bf16[2048,512]{1,0:T(8,128)(2,1)} %cols.3), channel_id=1, source_target_pairs={{0,4},{4,0},{1,5},{5,1},{2,6},{6,2},{3,7},{7,3},{8,12},{12,8},{9,1... | collective-permute-start | bytes 6291464 | tf_op jit(solution)/shard_map/ppermute | solution.py:386
  3.7 25.0 %collective-permute-start = (bf16[2048,256]{1,0:T(8,128)(2,1)}, bf16[2048,256]{1,0:T(8,128)(2,1)}, u32[]{:S(2)}, u32[]{:S(2)}) collective-permute-start(bf16[2048,256]{1,0:T(8,128)(2,1)} %own_rows.3), channel_id=1, source_target_pairs={{0,1},{1,0},{2,3},{3,2},{4,5},{5,4},{6,7},{7,6},{8,9},{9,8},{10,11... | collective-permute-start | bytes 3145736 | tf_op jit(solution)/shard_map/ppermute | solution.py:388
  5.2 23.4 %collective-permute-start.1 = (bf16[2048,256]{1,0:T(8,128)(2,1)}, bf16[2048,256]{1,0:T(8,128)(2,1)}, u32[]{:S(2)}, u32[]{:S(2)}) collective-permute-start(bf16[2048,256]{1,0:T(8,128)(2,1)} %own_rows.3), channel_id=1, source_target_pairs={{1,2},{2,1},{5,6},{6,5},{9,10},{10,9},{13,14},{14,13},{17,18},{18,... | collective-permute-start | bytes 3145736 | tf_op jit(solution)/shard_map/ppermute | solution.py:387
  6.9 1.6 %copy-start.2 = (bf16[2048,512]{1,0:T(8,128)(2,1)S(1)}, bf16[2048,512]{1,0:T(8,128)(2,1)}, u32[]{:S(2)}) copy-start(bf16[2048,512]{1,0:T(8,128)(2,1)} %cols.3) | copy-start | bytes 6291460
  8.4 1.2 %copy-start.4 = (bf16[2048,256]{1,0:T(8,128)(2,1)S(1)}, bf16[2048,256]{1,0:T(8,128)(2,1)}, u32[]{:S(2)}) copy-start(bf16[2048,256]{1,0:T(8,128)(2,1)} %own_rows.3) | copy-start | bytes 3145732
  9.7 10.3 %copy-start.14 = (f32[2048]{0:T(1024)S(1)}, f32[2048]{0:T(1024)}, u32[]{:S(2)}) copy-start(f32[2048]{0:T(1024)} %param.8) | copy-start | bytes 24580
  9.7 10.7 %copy-start.3 = (bf16[2048,512]{1,0:T(8,128)(2,1)S(1)}, bf16[2048,512]{1,0:T(8,128)(2,1)}, u32[]{:S(2)}) copy-start(bf16[2048,512]{1,0:T(8,128)(2,1)} %cols.3) | copy-start | bytes 6291460
  16.8 11.9 %collective-permute-start.2 = (f32[1,768]{1,0:T(1,128)S(1)}, f32[1,768]{1,0:T(1,128)S(1)}, u32[]{:S(2)}, u32[]{:S(2)}) collective-permute-start(f32[1,768]{1,0:T(1,128)S(1)} %psum.7.sums.m0), channel_id=1, source_target_pairs={{0,1},{1,0},{2,3},{3,2},{4,5},{5,4},{6,7},{7,6},{8,9},{9,8},{10,11... | collective-permute-start | bytes 9224 | tf_op jit(solution)/shard_map/ppermute | solution.py:392
  20.0 12.7 %collective-permute-start.5 = (f32[1,768]{1,0:T(1,128)S(1)}, f32[1,768]{1,0:T(1,128)S(1)}, u32[]{:S(2)}, u32[]{:S(2)}) collective-permute-start(f32[1,768]{1,0:T(1,128)S(1)} %psum.7.sums.m0), channel_id=1, source_target_pairs={{0,2},{1,3},{2,0},{3,1},{4,6},{5,7},{6,4},{7,5},{8,10},{9,11},{10,... | collective-permute-start | bytes 9224 | tf_op jit(solution)/shard_map/ppermute | solution.py:393
  20.4 1.6 %copy-start.8 = (bf16[2048,512]{1,0:T(8,128)(2,1)S(1)}, bf16[2048,512]{1,0:T(8,128)(2,1)}, u32[]{:S(2)}) copy-start(bf16[2048,512]{1,0:T(8,128)(2,1)} %grads.1) | copy-start | bytes 6291460
  23.1 2.0 %copy-start = (bf16[2048,1024]{1,0:T(8,128)(2,1)}, bf16[2048,1024]{1,0:T(8,128)(2,1)S(1)}, u32[]{:S(2)}) copy-start(bf16[2048,1024]{1,0:T(8,128)(2,1)S(1)} %get-tuple-element.68.ow) | copy-start | bytes 12582916
  25.1 1.4 %copy-start.6 = (f32[2048,256]{1,0:T(8,128)}, f32[2048,256]{1,0:T(8,128)S(1)}, u32[]{:S(2)}) copy-start(f32[2048,256]{1,0:T(8,128)S(1)} %get-tuple-element.80.wide) | copy-start | bytes 6291460
  26.5 1.0 copy-start.9
  27.4 1.0 copy-start.11
  28.6 21.0 %collective-permute-start.4 = (f32[1,768]{1,0:T(1,128)S(1)}, f32[1,768]{1,0:T(1,128)S(1)}, u32[]{:S(2)}, u32[]{:S(2)}) collective-permute-start(f32[1,768]{1,0:T(1,128)S(1)} %psum.7.sums.m0), channel_id=1, source_target_pairs={{0,4},{4,0},{1,5},{5,1},{2,6},{6,2},{3,7},{7,3},{8,12},{12,8},{9,1... | collective-permute-start | bytes 9224 | tf_op jit(solution)/shard_map/ppermute | solution.py:407
  29.0 28.8 %collective-permute-start.6 = (bf16[2048,256]{1,0:T(8,128)(2,1)}, bf16[2048,256]{1,0:T(8,128)(2,1)S(1)}, u32[]{:S(2)}, u32[]{:S(2)}) collective-permute-start(bf16[2048,256]{1,0:T(8,128)(2,1)} %collective-permute-done.near), channel_id=1, source_target_pairs={{1,2},{2,1},{5,6},{6,5},{9,10},{10,9},{13,14},{14,13},{17,18},{18,... | collective-permute-start | bytes 3145736 | tf_op jit(solution)/shard_map/ppermute | solution.py:409
  29.7 30.3 %collective-permute-start.3 = (bf16[2048,256]{1,0:T(8,128)(2,1)}, bf16[2048,256]{1,0:T(8,128)(2,1)S(1)}, u32[]{:S(2)}, u32[]{:S(2)}) collective-permute-start(bf16[2048,256]{1,0:T(8,128)(2,1)} %collective-permute-done.1.mid1), channel_id=1, source_target_pairs={{1,0},{2,3},{5,4},{6,7},{9,8},{10,11},{13,12},{14,15},{17,16},{18,... | collective-permute-start | bytes 3145736 | tf_op jit(solution)/shard_map/ppermute | solution.py:408
  32.7 25.1 %collective-permute-start.8 = (f32[1,768]{1,0:T(1,128)S(1)}, f32[1,768]{1,0:T(1,128)S(1)}, u32[]{:S(2)}, u32[]{:S(2)}) collective-permute-start(f32[1,768]{1,0:T(1,128)S(1)} %psum.7.sums.m0), channel_id=1, source_target_pairs={{0,3},{1,2},{2,1},{3,0},{4,7},{5,6},{6,5},{7,4},{8,11},{9,10},{10,... | collective-permute-start | bytes 9224 | tf_op jit(solution)/shard_map/ppermute | solution.py:406
  49.6 26.3 %collective-permute-start.12 = (bf16[2048,256]{1,0:T(8,128)(2,1)}, bf16[2048,256]{1,0:T(8,128)(2,1)S(1)}, u32[]{:S(2)}, u32[]{:S(2)}) collective-permute-start(bf16[2048,256]{1,0:T(8,128)(2,1)} %copy-done.11), channel_id=1, source_target_pairs={{0,4},{4,0},{1,5},{5,1},{2,6},{6,2},{3,7},{7,3},{8,12},{12,8},{9,1... | collective-permute-start | bytes 3145736 | tf_op jit(solution)/shard_map/ppermute | solution.py:410
  51.4 2.8 %copy-start.1 = (bf16[2048,1024]{1,0:T(8,128)(2,1)S(1)}, bf16[2048,1024]{1,0:T(8,128)(2,1)}, u32[]{:S(2)}) copy-start(bf16[2048,1024]{1,0:T(8,128)(2,1)} %copy-done) | copy-start | bytes 12582916
  51.4 3.1 %copy-start.5 = (bf16[2048,256]{1,0:T(8,128)(2,1)S(1)}, bf16[2048,256]{1,0:T(8,128)(2,1)}, u32[]{:S(2)}) copy-start(bf16[2048,256]{1,0:T(8,128)(2,1)} %own_rows.3) | copy-start | bytes 3145732
  57.8 26.5 %collective-permute-start.11 = (bf16[2048,256]{1,0:T(8,128)(2,1)S(1)}, bf16[2048,256]{1,0:T(8,128)(2,1)S(1)}, u32[]{:S(2)}, u32[]{:S(2)}) collective-permute-start(bf16[2048,256]{1,0:T(8,128)(2,1)S(1)} %collective-permute-done.6.last1), channel_id=1, source_target_pairs={{1,0},{2,3},{5,4},{6,7},{9,8},{10,11},{13,12},{14,15},{17,16},{18,... | collective-permute-start | bytes 3145736 | tf_op jit(solution)/shard_map/ppermute | solution.py:427
  60.0 1.0 copy-start.12
  61.0 1.2 %copy-start.13 = (bf16[2048,256]{1,0:T(8,128)(2,1)S(1)}, bf16[2048,256]{1,0:T(8,128)(2,1)}, u32[]{:S(2)}) copy-start(bf16[2048,256]{1,0:T(8,128)(2,1)} %copy-done.12) | copy-start | bytes 3145732
  62.2 6.6 %copy-start.10 = (bf16[2048,256]{1,0:T(8,128)(2,1)S(1)}, bf16[2048,256]{1,0:T(8,128)(2,1)}, u32[]{:S(2)}) copy-start(bf16[2048,256]{1,0:T(8,128)(2,1)} %copy-done.9) | copy-start | bytes 3145732
  62.2 13.7 %copy-start.7 = (f32[2048,256]{1,0:T(8,128)S(1)}, f32[2048,256]{1,0:T(8,128)}, u32[]{:S(2)}) copy-start(f32[2048,256]{1,0:T(8,128)} %copy-done.6) | copy-start | bytes 6291460
  68.3 2.1 %collective-permute-start.10 = (bf16[1,256,768]{2,1,0:T(8,128)(2,1)S(1)}, bf16[1,256,768]{2,1,0:T(8,128)(2,1)S(1)}, u32[]{:S(2)}, u32[]{:S(2)}) collective-permute-start(bf16[1,256,768]{2,1,0:T(8,128)(2,1)S(1)} %get-tuple-element.77), channel_id=1, source_target_pairs={{0,8},{8,0},{16,24},{24,16},{1,9},{9,1},{17,25},{25,17},{2,10},{10... | collective-permute-start | bytes 1179656 | tf_op jit(solution)/shard_map/ppermute | solution.py:448
  68.3 2.3 %collective-permute-start.9 = (bf16[1,256,768]{2,1,0:T(8,128)(2,1)S(1)}, bf16[1,256,768]{2,1,0:T(8,128)(2,1)S(1)}, u32[]{:S(2)}, u32[]{:S(2)}) collective-permute-start(bf16[1,256,768]{2,1,0:T(8,128)(2,1)S(1)} %get-tuple-element.76), channel_id=1, source_target_pairs={{0,8},{8,0},{16,24},{24,16},{1,9},{9,1},{17,25},{25,17},{2,10},{10... | collective-permute-start | bytes 1179656 | tf_op jit(solution)/shard_map/ppermute | solution.py:448
  68.8 27.9 %collective-permute-start.22 = (bf16[2048,256]{1,0:T(8,128)(2,1)S(1)}, bf16[2048,256]{1,0:T(8,128)(2,1)S(1)}, u32[]{:S(2)}, u32[]{:S(2)}) collective-permute-start(bf16[2048,256]{1,0:T(8,128)(2,1)S(1)} %copy-done.10), channel_id=1, source_target_pairs={{0,4},{4,0},{1,5},{5,1},{2,6},{6,2},{3,7},{7,3},{8,12},{12,8},{9,1... | collective-permute-start | bytes 3145736 | tf_op jit(solution)/shard_map/ppermute | solution.py:428
  71.3 13.0 %collective-permute-start.13 = (bf16[256,768]{1,0:T(8,128)(2,1)S(1)}, bf16[256,768]{1,0:T(8,128)(2,1)S(1)}, u32[]{:S(2)}, u32[]{:S(2)}) collective-permute-start(bf16[256,768]{1,0:T(8,128)(2,1)S(1)} %shard_map.75), channel_id=1, source_target_pairs={{0,16},{8,24},{16,0},{24,8},{1,17},{9,25},{17,1},{25,9},{2,18},{10... | collective-permute-start | bytes 1179656 | tf_op jit(solution)/shard_map/ppermute | solution.py:453
  78.0 1.4 %collective-permute-start.14 = (bf16[1,256,256]{2,1,0:T(8,128)(2,1)S(1)}, bf16[1,256,256]{2,1,0:T(8,128)(2,1)S(1)}, u32[]{:S(2)}, u32[]{:S(2)}) collective-permute-start(bf16[1,256,256]{2,1,0:T(8,128)(2,1)S(1)} %get-tuple-element.85), channel_id=1, source_target_pairs={{0,8},{8,0},{16,24},{24,16},{1,9},{9,1},{17,25},{25,17},{2,10},{10... | collective-permute-start | bytes 393224 | tf_op jit(solution)/shard_map/ppermute | solution.py:448
  80.0 4.3 %collective-permute-start.15 = (bf16[256,128]{1,0:T(8,128)(2,1)S(1)}, bf16[256,128]{1,0:T(8,128)(2,1)S(1)}, u32[]{:S(2)}, u32[]{:S(2)}) collective-permute-start(bf16[256,128]{1,0:T(8,128)(2,1)S(1)} %shard_map.77), channel_id=1, source_target_pairs={{0,16},{8,24},{16,0},{24,8},{1,17},{9,25},{17,1},{25,9},{2,18},{10... | collective-permute-start | bytes 196616 | tf_op jit(solution)/shard_map/ppermute | solution.py:453
  87.6 2.5 %collective-permute-start.16 = (bf16[1,256,512]{2,1,0:T(8,128)(2,1)S(1)}, bf16[1,256,512]{2,1,0:T(8,128)(2,1)S(1)}, u32[]{:S(2)}, u32[]{:S(2)}) collective-permute-start(bf16[1,256,512]{2,1,0:T(8,128)(2,1)S(1)} %get-tuple-element.92), channel_id=1, source_target_pairs={{0,8},{8,0},{16,24},{24,16},{1,9},{9,1},{17,25},{25,17},{2,10},{10... | collective-permute-start | bytes 786440 | tf_op jit(solution)/shard_map/ppermute | solution.py:448
  87.7 2.5 %collective-permute-start.18 = (bf16[1,256,512]{2,1,0:T(8,128)(2,1)S(1)}, bf16[1,256,512]{2,1,0:T(8,128)(2,1)S(1)}, u32[]{:S(2)}, u32[]{:S(2)}) collective-permute-start(bf16[1,256,512]{2,1,0:T(8,128)(2,1)S(1)} %get-tuple-element.94), channel_id=1, source_target_pairs={{0,8},{8,0},{16,24},{24,16},{1,9},{9,1},{17,25},{25,17},{2,10},{10... | collective-permute-start | bytes 786440 | tf_op jit(solution)/shard_map/ppermute | solution.py:448
  88.2 1.7 %collective-permute-start.17 = (bf16[1,256,384]{2,1,0:T(8,128)(2,1)S(1)}, bf16[1,256,384]{2,1,0:T(8,128)(2,1)S(1)}, u32[]{:S(2)}, u32[]{:S(2)}) collective-permute-start(bf16[1,256,384]{2,1,0:T(8,128)(2,1)S(1)} %get-tuple-element.93), channel_id=1, source_target_pairs={{0,8},{8,0},{16,24},{24,16},{1,9},{9,1},{17,25},{25,17},{2,10},{10... | collective-permute-start | bytes 589832 | tf_op jit(solution)/shard_map/ppermute | solution.py:448
  88.3 1.9 %collective-permute-start.19 = (bf16[1,256,384]{2,1,0:T(8,128)(2,1)S(1)}, bf16[1,256,384]{2,1,0:T(8,128)(2,1)S(1)}, u32[]{:S(2)}, u32[]{:S(2)}) collective-permute-start(bf16[1,256,384]{2,1,0:T(8,128)(2,1)S(1)} %get-tuple-element.95), channel_id=1, source_target_pairs={{0,8},{8,0},{16,24},{24,16},{1,9},{9,1},{17,25},{25,17},{2,10},{10... | collective-permute-start | bytes 589832 | tf_op jit(solution)/shard_map/ppermute | solution.py:448
  90.8 12.6 %collective-permute-start.23 = (bf16[256,896]{1,0:T(8,128)(2,1)S(1)}, bf16[256,896]{1,0:T(8,128)(2,1)S(1)}, u32[]{:S(2)}, u32[]{:S(2)}) collective-permute-start(bf16[256,896]{1,0:T(8,128)(2,1)S(1)} %shard_map.79), channel_id=1, source_target_pairs={{0,16},{8,24},{16,0},{24,8},{1,17},{9,25},{17,1},{25,9},{2,18},{10... | collective-permute-start | bytes 1376264 | tf_op jit(solution)/shard_map/ppermute | solution.py:453
  93.2 3.9 %collective-permute-start.21 = (bf16[256,128]{1,0:T(8,128)(2,1)S(1)}, bf16[256,128]{1,0:T(8,128)(2,1)S(1)}, u32[]{:S(2)}, u32[]{:S(2)}) collective-permute-start(bf16[256,128]{1,0:T(8,128)(2,1)S(1)} %shard_map.81), channel_id=1, source_target_pairs={{0,8},{8,0},{16,24},{24,16},{1,9},{9,1},{17,25},{25,17},{2,10},{10... | collective-permute-start | bytes 196616 | tf_op jit(solution)/shard_map/ppermute | solution.py:465
  94.0 3.1 %collective-permute-start.20 = (bf16[256,768]{1,0:T(8,128)(2,1)S(1)}, bf16[256,768]{1,0:T(8,128)(2,1)S(1)}, u32[]{:S(2)}, u32[]{:S(2)}) collective-permute-start(bf16[256,768]{1,0:T(8,128)(2,1)S(1)} %shard_map.80), channel_id=1, source_target_pairs={{0,8},{8,0},{16,24},{24,16},{1,9},{9,1},{17,25},{25,17},{2,10},{10... | collective-permute-start | bytes 1179656 | tf_op jit(solution)/shard_map/ppermute | solution.py:465
  99.2 1.6 %collective-permute-start.24 = (bf16[2,256,256]{2,1,0:T(8,128)(2,1)S(1)}, bf16[2,256,256]{2,1,0:T(8,128)(2,1)S(1)}, u32[]{:S(2)}, u32[]{:S(2)}) collective-permute-start(bf16[2,256,256]{2,1,0:T(8,128)(2,1)S(1)} %get-tuple-element.108), channel_id=1, source_target_pairs={{0,8},{8,0},{16,24},{24,16},{1,9},{9,1},{17,25},{25,17},{2,10},{10... | collective-permute-start | bytes 786440 | tf_op jit(solution)/shard_map/ppermute | solution.py:433
  101.4 5.6 %collective-permute-start.29 = (bf16[256,256]{1,0:T(8,128)(2,1)S(1)}, bf16[256,256]{1,0:T(8,128)(2,1)S(1)}, u32[]{:S(2)}, u32[]{:S(2)}) collective-permute-start(bf16[256,256]{1,0:T(8,128)(2,1)S(1)} %shard_map.84), channel_id=1, source_target_pairs={{0,16},{8,24},{16,0},{24,8},{1,17},{9,25},{17,1},{25,9},{2,18},{10... | collective-permute-start | bytes 393224 | tf_op jit(solution)/shard_map/ppermute | solution.py:440
  104.2 1.4 %collective-permute-start.25 = (bf16[64,896]{1,0:T(8,128)(2,1)S(1)}, bf16[64,896]{1,0:T(8,128)(2,1)S(1)}, u32[]{:S(2)}, u32[]{:S(2)}) collective-permute-start(bf16[64,896]{1,0:T(8,128)(2,1)S(1)} %get-tuple-element.110), channel_id=1, source_target_pairs={{0,8},{8,0},{16,24},{24,16},{1,9},{9,1},{17,25},{25,17},{2,10},{10... | collective-permute-start | bytes 344072 | tf_op jit(solution)/shard_map/ppermute | solution.py:465
  104.3 1.5 %collective-permute-start.26 = (bf16[64,896]{1,0:T(8,128)(2,1)S(1)}, bf16[64,896]{1,0:T(8,128)(2,1)S(1)}, u32[]{:S(2)}, u32[]{:S(2)}) collective-permute-start(bf16[64,896]{1,0:T(8,128)(2,1)S(1)} %get-tuple-element.111), channel_id=1, source_target_pairs={{0,8},{8,0},{16,24},{24,16},{1,9},{9,1},{17,25},{25,17},{2,10},{10... | collective-permute-start | bytes 344072 | tf_op jit(solution)/shard_map/ppermute | solution.py:465
  104.8 1.3 %collective-permute-start.27 = (bf16[64,896]{1,0:T(8,128)(2,1)S(1)}, bf16[64,896]{1,0:T(8,128)(2,1)S(1)}, u32[]{:S(2)}, u32[]{:S(2)}) collective-permute-start(bf16[64,896]{1,0:T(8,128)(2,1)S(1)} %get-tuple-element.112), channel_id=1, source_target_pairs={{0,8},{8,0},{16,24},{24,16},{1,9},{9,1},{17,25},{25,17},{2,10},{10... | collective-permute-start | bytes 344072 | tf_op jit(solution)/shard_map/ppermute | solution.py:465
  104.9 1.4 %collective-permute-start.28 = (bf16[64,896]{1,0:T(8,128)(2,1)S(1)}, bf16[64,896]{1,0:T(8,128)(2,1)S(1)}, u32[]{:S(2)}, u32[]{:S(2)}) collective-permute-start(bf16[64,896]{1,0:T(8,128)(2,1)S(1)} %get-tuple-element.113), channel_id=1, source_target_pairs={{0,8},{8,0},{16,24},{24,16},{1,9},{9,1},{17,25},{25,17},{2,10},{10... | collective-permute-start | bytes 344072 | tf_op jit(solution)/shard_map/ppermute | solution.py:465
